TPU v7x, 512 devices: a whole 4x4x16 slice. The times are simulated.
512 devices in a mesh: chan: 128 (over x, y_lo, z), slab: 4 (over y_hi, core).
Axes of the slice: x: 4, y: 4 (y_hi: 2, y_lo: 2; y = y_hi * 2 + y_lo), z: 16, core: 2. Of those that a mesh axis runs over, the one named last changes fastest.
Arguments:
- volume_now: float32 [1024, 4, 16, 512], P('chan', 'slab'), may hold values from 0.05 to 22
- extrapolated: float32 [1024, 4, 16, 512], P('chan', 'slab'), may hold values from -5 to 24
- dual_grad: float32 [3, 1024, 4, 16, 512], P(None, 'chan', 'slab'), may hold values from -3 to 3
- dual_data: float32 [1024, 4, 4096], P('chan', 'slab'), may hold values from -6 to 6
- measured: float32 [1024, 4, 4096], P('chan', 'slab'), may hold values from -6 to 18
- projector: bfloat16 [64, 128, 128], replicated, may hold values from -0.375 to 0.375
- tile_rows: int32 [64], replicated, may hold values from 0 to 31
- tile_cols: int32 [64], replicated, may hold values from 0 to 63
- dual_step: float32 [1], replicated, may hold values from 0.3 to 0.6
- primal_step: float32 [1], replicated, may hold values from 0.2 to 0.5
- reg_weight: float32 [1], replicated, may hold values from 1.2 to 2.4
Outputs:
- updated: float32 [1024, 4, 16, 512], P('chan', 'slab')
- dual_grad_new: float32 [3, 1024, 4, 16, 512], P(None, 'chan', 'slab')
- dual_data_new: float32 [1024, 4, 4096], P('chan', 'slab')
- totals: float32 [2], replicated
Inputs may be any that keep to these rules, and one draw needn't show every extreme that they name: `tile_rows`: ray block of each tile; several tiles may share a block. `tile_cols`: pixel block of each tile, blocks counted along the row-by-row pixel order.
All inputs are finite; a program needn't handle non-finite values.
Results may differ from a plain program's by a relative error of at most 0.002.
Values sent between devices are 32-bit elements; how exact they have to be, the bound alone decides.
No kernel may reach another device: no remote copies, remote signals or barrier semaphores. Data moves between devices by JAX's collectives and lax.ppermute only.
A program may use at most 64 MiB of HBM per device.

v0:
```python
import math

import jax
import jax.numpy as jnp
from jax import lax
from jax.sharding import Mesh
from jax.sharding import PartitionSpec as P

SWEEPS = 6
CHAN = ("chan_0", "chan_1", "chan_2")


index_pairs = ((0, 0), (1, 1), (2, 2), (0, 1), (0, 2), (1, 2))
sweep_order = ((0, 1), (0, 2), (1, 2))


def from_behind(block, axis, distance):
    devices = range(lax.axis_size(axis))
    route = [(i - distance, i) for i in devices if i - distance in devices]
    return lax.ppermute(block, axis, route)


def in_blocks(value, dim, peers):
    dims = value.shape
    blocks = value.reshape(*dims[:dim], peers, dims[dim] // peers, *dims[dim + 1 :])
    return jnp.moveaxis(blocks, dim, 0)


def summed_on_arrival(value, axis, dim):
    peers = lax.axis_size(axis)
    blocks = lax.all_to_all(in_blocks(value, dim, peers), axis, 0, 0, tiled=True)
    return jnp.sum(blocks, axis=0)


def sum_by_axis(value, axes, dim):
    far, near = axes
    own = summed_on_arrival(in_blocks(value, dim, lax.axis_size(far)), near, dim + 1)
    return jnp.sum(lax.all_to_all(own, far, 0, 0, tiled=True), axis=0)


def copy_for_each(value, axis):
    copies = jnp.broadcast_to(value, (lax.axis_size(axis), *value.shape))
    return lax.all_to_all(copies, axis, split_axis=0, concat_axis=0, tiled=True)


def laid_out(blocks, dim):
    blocks = jnp.moveaxis(blocks, 0, dim)
    dims = blocks.shape
    return blocks.reshape(*dims[:dim], dims[dim] * dims[dim + 1], *dims[dim + 2 :])


def gathered_by_axis(value, axes, dim):
    far, near = axes
    blocks = copy_for_each(copy_for_each(value, far), near)
    return laid_out(blocks.swapaxes(0, 1).reshape(-1, *value.shape), dim)


def taken_together(value, axis):
    everything = copy_for_each(value, axis)
    return jnp.sum(everything, axis=0)


def rotate_columns(matrix, first_idx, second_idx, cosine, sine_value):
    result = [list(row) for row in matrix]
    for row_idx in range(3):
        left_val = matrix[row_idx][first_idx]
        right_val = matrix[row_idx][second_idx]
        result[row_idx][first_idx] = cosine * left_val - sine_value * right_val
        result[row_idx][second_idx] = sine_value * left_val + cosine * right_val
    return result


def rotate_rows(matrix, first_idx, second_idx, cosine, sine_value):
    result = [list(row) for row in matrix]
    for col_idx in range(3):
        upper_val = matrix[first_idx][col_idx]
        lower_val = matrix[second_idx][col_idx]
        result[first_idx][col_idx] = cosine * upper_val - sine_value * lower_val
        result[second_idx][col_idx] = sine_value * upper_val + cosine * lower_val
    return result


def unpack(entry_list):
    return [
        [entry_list[0], entry_list[3], entry_list[4]],
        [entry_list[3], entry_list[1], entry_list[5]],
        [entry_list[4], entry_list[5], entry_list[2]],
    ]


def pack_entries(matrix):
    return jnp.stack([matrix[first_idx][second_idx] for first_idx, second_idx in index_pairs])


def spectral_factor(matrix, radius):
    vectors = [[1.0 if row_idx == col_idx else 0.0 for col_idx in range(3)] for row_idx in range(3)]
    for sweep_idx in range(SWEEPS):
        for first_idx, second_idx in sweep_order:
            angle_half = 0.5 * jnp.arctan2(
                2.0 * matrix[first_idx][second_idx],
                matrix[second_idx][second_idx] - matrix[first_idx][first_idx],
            )
            cosine = jnp.cos(angle_half)
            sine_value = jnp.sin(angle_half)
            matrix = rotate_rows(
                rotate_columns(matrix, first_idx, second_idx, cosine, sine_value),
                first_idx,
                second_idx,
                cosine,
                sine_value,
            )
            vectors = rotate_columns(vectors, first_idx, second_idx, cosine, sine_value)
    root_values = [jnp.sqrt(jnp.maximum(matrix[diag_idx][diag_idx], 0.0)) for diag_idx in range(3)]
    scales = [radius / jnp.maximum(root_values[diag_idx], radius) for diag_idx in range(3)]
    factor = [
        [
            vectors[row_idx][0] * scales[0] * vectors[col_idx][0]
            + vectors[row_idx][1] * scales[1] * vectors[col_idx][1]
            + vectors[row_idx][2] * scales[2] * vectors[col_idx][2]
            for col_idx in range(3)
        ]
        for row_idx in range(3)
    ]
    excess = (
        jnp.maximum(root_values[0] - radius, 0.0)
        + jnp.maximum(root_values[1] - radius, 0.0)
        + jnp.maximum(root_values[2] - radius, 0.0)
    ) / radius
    return (factor, excess)


def apply_factor(candidate, matrix):
    return jnp.stack(
        [
            candidate[0] * matrix[0][col_idx]
            + candidate[1] * matrix[1][col_idx]
            + candidate[2] * matrix[2][col_idx]
            for col_idx in range(3)
        ]
    )


def forward_difference(volume, along_axis):
    length = volume.shape[along_axis]
    later = lax.slice_in_dim(volume, 1, length, axis=along_axis)
    kept_part = lax.slice_in_dim(volume, 0, length - 1, axis=along_axis)
    zero_layer = jnp.zeros_like(lax.slice_in_dim(volume, 0, 1, axis=along_axis))
    return jnp.concatenate([later - kept_part, zero_layer], axis=along_axis)


def backward_difference(component, along_axis):
    length = component.shape[along_axis]
    kept_part = lax.slice_in_dim(component, 0, length - 1, axis=along_axis)
    zero_layer = jnp.zeros_like(lax.slice_in_dim(component, 0, 1, axis=along_axis))
    masked = jnp.concatenate([kept_part, zero_layer], axis=along_axis)
    earlier = jnp.concatenate([zero_layer, kept_part], axis=along_axis)
    return masked - earlier


def project_forward(rounded, projector, tile_rows, tile_cols, rays):
    channels, slices, pixels = rounded.shape
    tile_edge = projector.shape[1]
    row_blocks = rays // tile_edge
    blocks = rounded.reshape(channels * slices, pixels // tile_edge, tile_edge)
    picked = jnp.take(blocks, tile_cols, axis=1)
    products = jnp.einsum("tij,btj->bti", projector, picked, preferred_element_type=jnp.float32)
    selector = (tile_rows[:, None] == jnp.arange(row_blocks, dtype=jnp.int32)[None, :]).astype(
        jnp.float32
    )
    sinogram = jnp.einsum("tr,bti->bri", selector, products, precision=lax.Precision.HIGHEST)
    return sinogram.reshape(channels, slices, rays)


def project_back(data_low, projector, tile_rows, tile_cols, pixels):
    channels, slices, rays = data_low.shape
    tile_edge = projector.shape[1]
    col_blocks = pixels // tile_edge
    blocks = data_low.reshape(channels * slices, rays // tile_edge, tile_edge)
    picked = jnp.take(blocks, tile_rows, axis=1)
    products = jnp.einsum("tij,bti->btj", projector, picked, preferred_element_type=jnp.float32)
    selector = (tile_cols[:, None] == jnp.arange(col_blocks, dtype=jnp.int32)[None, :]).astype(
        jnp.float32
    )
    volume = jnp.einsum("tc,btj->bcj", selector, products, precision=lax.Precision.HIGHEST)
    return volume.reshape(channels, slices, pixels)


def on_device(
    volume_now,
    extrapolated,
    dual_grad,
    dual_data,
    measured,
    projector,
    tile_rows,
    tile_cols,
    dual_step,
    primal_step,
    reg_weight,
):
    dual_rate = dual_step[0]
    primal_rate = primal_step[0]
    channels, slices, row_count, col_count = volume_now.shape
    pixels = row_count * col_count
    rays = dual_data.shape[2]
    chan_count = lax.axis_size(CHAN)
    slab_count = lax.axis_size("slab")
    total_channels = channels * chan_count
    last_slice = lax.axis_index("slab") == slab_count - 1
    following = from_behind(extrapolated, "slab", -1)
    rounded = extrapolated.reshape(channels, slices, pixels).astype(jnp.bfloat16)
    projected = project_forward(rounded, projector, tile_rows, tile_cols, rays)
    residual = projected - measured
    data_new = (dual_data + dual_rate * residual) / (1.0 + dual_rate)
    misfit_part = jnp.sum(residual * residual)
    across = jnp.where(last_slice, 0.0, following - extrapolated)
    gradient = jnp.stack(
        [forward_difference(extrapolated, 2), forward_difference(extrapolated, 3), across]
    )
    candidate = dual_grad + dual_rate * gradient
    partial_gram = jnp.stack(
        [
            jnp.sum(candidate[first_idx] * candidate[second_idx], axis=0)
            for first_idx, second_idx in index_pairs
        ]
    ).reshape(6, slices * pixels)
    radius = reg_weight[0] * math.sqrt(total_channels)
    gram_rows = sum_by_axis(partial_gram, ("chan_0", ("chan_1", "chan_2")), 1)
    factor, excess = spectral_factor(
        unpack([gram_rows[entry_idx] for entry_idx in range(6)]), radius
    )
    packed = pack_entries(factor)
    partials = jnp.stack([misfit_part, jnp.sum(excess)]).reshape(2, 1)
    factor_rows, gathered = (
        gathered_by_axis(packed, ("chan_0", ("chan_1", "chan_2")), 1),
        gathered_by_axis(partials, ("chan_0", ("chan_1", "chan_2")), 1),
    )
    combined = taken_together(jnp.sum(gathered, axis=1), "slab")
    matrix = unpack(
        [factor_rows[entry_idx].reshape(slices, row_count, col_count) for entry_idx in range(6)]
    )
    grad_new = apply_factor(candidate, matrix)
    prior_layer = from_behind(grad_new[2], "slab", 1)
    masked = jnp.where(last_slice, 0.0, grad_new[2])
    divergence = (
        backward_difference(grad_new[0], 2)
        + backward_difference(grad_new[1], 3)
        + masked
        - prior_layer
    )
    data_low = data_new.astype(jnp.bfloat16)
    back_proj = project_back(data_low, projector, tile_rows, tile_cols, pixels).reshape(
        volume_now.shape
    )
    updated = jnp.maximum(volume_now - primal_rate * (back_proj - divergence), 0.0)
    totals = jnp.stack(
        [
            combined[0] / (total_channels * slab_count * slices * rays),
            combined[1] / (slab_count * slices * pixels),
        ]
    )
    return (updated, grad_new, data_new, totals)


def solution(mesh):
    torus = Mesh(
        mesh.devices.reshape(4, 2, 16, mesh.shape["slab"]), ("chan_0", "chan_1", "chan_2", "slab")
    )
    placed = (
        P(CHAN, "slab", None, None),
        P(CHAN, "slab", None, None),
        P(None, CHAN, "slab", None, None),
        P(CHAN, "slab", None),
        P(CHAN, "slab", None),
        P(),
        P(),
        P(),
        P(),
        P(),
        P(),
    )
    return jax.shard_map(
        on_device,
        mesh=torus,
        in_specs=placed,
        out_specs=(
            P(CHAN, "slab", None, None),
            P(None, CHAN, "slab", None, None),
            P(CHAN, "slab", None),
            P(),
        ),
        check_vma=False,
    )
```

profile of v0, /device:TPU:1, one launch (start us, length us, event | category | flops | bytes accessed | tf_op | source)
XLA Modules:
  0.0 157.4 jit_solution(2410706900562791472)
XLA Ops:
  0.7 8.9 %collective-permute-start = (f32[8,1,16,512]{3,2,0,1:T(8,128)}, f32[8,1,16,512]{3,2,0,1:T(8,128)S(1)}, u32[]{:S(2)}, u32[]{:S(2)}) collective-permute-start(f32[8,1,16,512]{3,2,0,1:T(8,128)} %bitcast.224), channel_id=1, source_target_pairs={{1,0},{2,1},{3,2},{5,4},{6,5},{7,6},{9,8},{10,9},{11,10},{13,12},{... | collective-permute-start | bytes 786440 | tf_op jit(solution)/shard_map/ppermute | solution.py:20
  9.6 1.2 slice_subtract_fusion
  10.8 1.1 slice_subtract_fusion.1
  11.9 0.7 compare_select_fusion.1
  12.6 0.7 pad_bitcast_fusion
  14.6 1.4 fusion.1
  16.3 0.7 copy-done.3
  17.0 1.2 reshape.432
  18.2 1.0 copy.197
  19.2 2.0 %reshape.455 = f32[32,1,1536]{2,1,0:T(1,128)} reshape(f32[32,6,4,64]{3,2,1,0:T(4,128)} %bitcast.231) | data formatting | bytes 393216
  21.2 13.0 %all-to-all-start = ((f32[32,1,1536]{2,1,0:T(1,128)}), f32[32,1,1536]{2,1,0:T(1,128)}, u32[]{:S(2)}, u32[]{:S(2)}) async-start(f32[32,1,1536]{2,1,0:T(1,128)} %reshape.455), calls=%async_computation | async-start | bytes 393216 | tf_op jit(solution)/shard_map/all_to_all | solution.py:31
  34.2 0.7 pad_clamp_fusion
  35.1 0.6 gather_fusion
  35.7 1.2 convolution_bitcast_fusion.2
  37.2 15.2 %all-to-all-done = f32[32,1,1536]{2,1,0:T(1,128)} async-done(((f32[32,1,1536]{2,1,0:T(1,128)}), f32[32,1,1536]{2,1,0:T(1,128)}, u32[]{:S(2)}, u32[]{:S(2)}) %all-to-all-start) | async-done | bytes 196640 | tf_op jit(solution)/shard_map/all_to_all | solution.py:31
  52.9 2.7 %reduce.13 = f32[32,1536]{1,0:T(8,128)} reduce(f32[32,1,1536]{2,1,0:T(1,128)} %all-to-all-done, f32[]{:T(128)} %broadcast.672), dimensions={1}, to_apply=%all_to_all.24.reduce_sub_computation | reduce | bytes 393220 | tf_op jit(solution)/shard_map/all_to_all | solution.py:31
  55.6 1.1 reshape.456
  56.8 0.7 reshape.457
  57.5 4.0 %all-to-all-start.1 = ((f32[4,1,384]{2,1,0:T(1,128)}), f32[4,1,384]{2,1,0:T(1,128)S(1)}, u32[]{:S(2)}, u32[]{:S(2)}) async-start(f32[4,1,384]{2,1,0:T(1,128)} %reshape.457), calls=%async_computation.1 | async-start | bytes 12288 | tf_op jit(solution)/shard_map/all_to_all | solution.py:38
  61.5 0.9 multiply_reduce_fusion
  63.1 2.6 %all-to-all-done.1 = f32[4,1,384]{2,1,0:T(1,128)S(1)} async-done(((f32[4,1,384]{2,1,0:T(1,128)}), f32[4,1,384]{2,1,0:T(1,128)S(1)}, u32[]{:S(2)}, u32[]{:S(2)}) %all-to-all-start.1) | async-done | bytes 6176 | tf_op jit(solution)/shard_map/all_to_all | solution.py:38
  65.7 0.7 reduce.14
  69.3 2.1 %divide_reduce_fusion = f32[]{:T(128)} fusion(f32[]{:T(128)} %bitcast.30, f32[6,64]{1,0:T(8,128)S(1)} %reduce_sum.115), kind=kLoop, calls=%fused_computation.113 | loop fusion | flops 43071 | bytes 1544 | tf_op jit(solution)/shard_map/reduce_sum | solution.py:233
  71.4 1.4 pad_maximum_fusion.1
  73.4 3.2 %all-to-all-start.4 = ((f32[4,2,1]{1,2,0:T(1,128)}), f32[4,2,1]{1,2,0:T(1,128)S(1)}, u32[]{:S(2)}, u32[]{:S(2)}) async-start(f32[4,2,1]{1,2,0:T(1,128)} %broadcast_in_dim.54), calls=%async_computation.4 | async-start | bytes 4096 | tf_op jit(solution)/shard_map/all_to_all | solution.py:43
  76.8 3.8 %all-to-all-done.4 = f32[4,2,1]{1,2,0:T(1,128)S(1)} async-done(((f32[4,2,1]{1,2,0:T(1,128)}), f32[4,2,1]{1,2,0:T(1,128)S(1)}, u32[]{:S(2)}, u32[]{:S(2)}) %all-to-all-start.4) | async-done | bytes 64 | tf_op jit(solution)/shard_map/all_to_all | solution.py:43
  81.3 3.9 %all-to-all-start.5 = ((f32[32,4,2,1]{1,2,3,0:T(2,128)}), f32[32,4,2,1]{1,2,3,0:T(2,128)S(1)}, u32[]{:S(2)}, u32[]{:S(2)}) async-start(f32[32,4,2,1]{1,2,3,0:T(2,128)} %broadcast_in_dim.55), calls=%async_computation.5 | async-start | bytes 65536 | tf_op jit(solution)/shard_map/all_to_all | solution.py:43
  85.2 0.7 reshape.459
  85.9 11.8 %all-to-all-done.5 = f32[32,4,2,1]{1,2,3,0:T(2,128)S(1)} async-done(((f32[32,4,2,1]{1,2,3,0:T(2,128)}), f32[32,4,2,1]{1,2,3,0:T(2,128)S(1)}, u32[]{:S(2)}, u32[]{:S(2)}) %all-to-all-start.5) | async-done | bytes 1056 | tf_op jit(solution)/shard_map/all_to_all | solution.py:43
  97.8 3.2 %all-to-all-start.2 = ((f32[4,1,384]{2,1,0:T(1,128)}), f32[4,1,384]{2,1,0:T(1,128)S(1)}, u32[]{:S(2)}, u32[]{:S(2)}) async-start(f32[4,1,384]{2,1,0:T(1,128)} %reshape.459), calls=%async_computation.2 | async-start | bytes 12288 | tf_op jit(solution)/shard_map/all_to_all | solution.py:43
  101.0 1.9 %convert_reduce_fusion = (bf16[8,4096]{1,0:T(8,128)(2,1)S(1)}, f32[8,1,4096]{2,1,0:T(1,128)}) fusion(f32[]{:T(128)S(6)} %add.1660, f32[8,1,4096]{2,1,0:T(1,128)} %param.14, f32[8,1,4096]{2,1,0:T(1,128)S(1)} %bitcast.233, f32[8,1,4096]{2,1,0:T(1,128)} %param.15, f32[]{:T(128)} %bitcast.220), kind=kLoop, calls=%fused_computation.55 | loop fusion | flops 163840 | bytes 589832 | tf_op jit(solution)/shard_map/convert_element_type | solution.py:251
  103.1 2.0 %all-to-all-done.2 = f32[4,1,384]{2,1,0:T(1,128)S(1)} async-done(((f32[4,1,384]{2,1,0:T(1,128)}), f32[4,1,384]{2,1,0:T(1,128)S(1)}, u32[]{:S(2)}, u32[]{:S(2)}) %all-to-all-start.2) | async-done | bytes 6176 | tf_op jit(solution)/shard_map/all_to_all | solution.py:43
  105.7 9.5 %all-to-all-start.6 = ((f32[4,1,2]{2,1,0:T(1,128)}), f32[4,1,2]{2,1,0:T(1,128)S(1)}, u32[]{:S(2)}, u32[]{:S(2)}) async-start(f32[4,1,2]{2,1,0:T(1,128)} %broadcast_in_dim.56), calls=%async_computation.6 | async-start | bytes 4096 | tf_op jit(solution)/shard_map/all_to_all | solution.py:43
  115.2 0.7 reduce.15
  116.0 1.1 reshape.461
  117.0 2.6 %all-to-all-done.6 = f32[4,1,2]{2,1,0:T(1,128)S(1)} async-done(((f32[4,1,2]{2,1,0:T(1,128)}), f32[4,1,2]{2,1,0:T(1,128)S(1)}, u32[]{:S(2)}, u32[]{:S(2)}) %all-to-all-start.6) | async-done | bytes 64 | tf_op jit(solution)/shard_map/all_to_all | solution.py:43
  119.7 4.8 %all-to-all-start.3 = ((f32[32,1,1536]{2,1,0:T(1,128)}), f32[32,1,1536]{2,1,0:T(1,128)}, u32[]{:S(2)}, u32[]{:S(2)}) async-start(f32[32,1,1536]{2,1,0:T(1,128)} %reshape.461), calls=%async_computation.3 | async-start | bytes 393216 | tf_op jit(solution)/shard_map/all_to_all | solution.py:43
  124.5 0.6 gather_fusion.1
  125.1 0.7 convolution_bitcast_fusion.1
  129.3 12.8 %all-to-all-done.3 = f32[32,1,1536]{2,1,0:T(1,128)} async-done(((f32[32,1,1536]{2,1,0:T(1,128)}), f32[32,1,1536]{2,1,0:T(1,128)}, u32[]{:S(2)}, u32[]{:S(2)}) %all-to-all-start.3) | async-done | bytes 196640 | tf_op jit(solution)/shard_map/all_to_all | solution.py:43
  142.1 2.7 %reduce.16 = f32[32,1536]{1,0:T(8,128)} reduce(f32[32,1,1536]{2,1,0:T(1,128)} %all-to-all-done.3, f32[]{:T(128)} %broadcast.672), dimensions={1}, to_apply=%all_to_all.27.reduce_sub_computation | reduce | bytes 393220 | tf_op jit(solution)/shard_map/all_to_all | solution.py:43
  144.8 1.1 reshape.462
  146.0 0.7 fusion.67
  146.7 0.9 mul.7190
  148.2 5.0 %collective-permute-start.1 = (f32[8,1,16,512]{3,2,0,1:T(8,128)S(1)}, f32[8,1,16,512]{3,2,0,1:T(8,128)S(1)}, u32[]{:S(2)}, u32[]{:S(2)}) collective-permute-start(f32[8,1,16,512]{3,2,0,1:T(8,128)S(1)} %get-tuple-element.305), channel_id=1, source_target_pairs={{0,1},{1,2},{2,3},{4,5},{5,6},{6,7},{8,9},{9,10},{10,11},{12,13},{... | collective-permute-start | bytes 786440 | tf_op jit(solution)/shard_map/ppermute | solution.py:20
  153.4 1.0 pad_maximum_fusion
  154.3 2.2 %collective-permute-done.1 = f32[8,1,16,512]{3,2,0,1:T(8,128)S(1)} collective-permute-done((f32[8,1,16,512]{3,2,0,1:T(8,128)S(1)}, f32[8,1,16,512]{3,2,0,1:T(8,128)S(1)}, u32[]{:S(2)}, u32[]{:S(2)}) %collective-permute-start.1) | collective-permute-done | bytes 262176 | tf_op jit(solution)/shard_map/ppermute | solution.py:20
  156.5 0.9 fusion.15
  (121 shorter events, 9.4 us)
Async XLA Ops:
  0.6 35.1 %copy-start = (bf16[64,128,128]{2,1,0:T(8,128)(2,1)S(1)}, bf16[64,128,128]{2,1,0:T(8,128)(2,1)}, u32[]{:S(2)}) copy-start(bf16[64,128,128]{2,1,0:T(8,128)(2,1)} %param.16) | copy-start | bytes 6291460
  0.6 13.9 %copy-start.1 = (f32[8,1,16,512]{3,2,1,0:T(8,128)S(1)}, f32[8,1,16,512]{3,2,1,0:T(8,128)}, u32[]{:S(2)}) copy-start(f32[8,1,16,512]{3,2,1,0:T(8,128)} %param.12) | copy-start | bytes 786436
  0.7 13.3 %copy-start.6 = (s32[64]{0:T(128)S(1)}, s32[64]{0:T(128)}, u32[]{:S(2)}) copy-start(s32[64]{0:T(128)} %param.18) | copy-start | bytes 772
  0.7 13.8 %collective-permute-start = (f32[8,1,16,512]{3,2,0,1:T(8,128)}, f32[8,1,16,512]{3,2,0,1:T(8,128)S(1)}, u32[]{:S(2)}, u32[]{:S(2)}) collective-permute-start(f32[8,1,16,512]{3,2,0,1:T(8,128)} %bitcast.224), channel_id=1, source_target_pairs={{1,0},{2,1},{3,2},{5,4},{6,5},{7,6},{9,8},{10,9},{11,10},{13,12},{... | collective-permute-start | bytes 786440 | tf_op jit(solution)/shard_map/ppermute | solution.py:20
  16.3 0.7 copy-start.3
  21.2 15.7 %copy-start.5 = (s32[64]{0:T(128)S(1)}, s32[64]{0:T(128)}, u32[]{:S(2)}) copy-start(s32[64]{0:T(128)} %param.17) | copy-start | bytes 772
  21.2 31.2 %all-to-all-start = ((f32[32,1,1536]{2,1,0:T(1,128)}), f32[32,1,1536]{2,1,0:T(1,128)}, u32[]{:S(2)}, u32[]{:S(2)}) async-start(f32[32,1,1536]{2,1,0:T(1,128)} %reshape.455), calls=%async_computation | async-start | bytes 393216 | tf_op jit(solution)/shard_map/all_to_all | solution.py:31
  35.7 25.8 %copy-start.2 = (f32[8,1,4096]{2,1,0:T(1,128)S(1)}, f32[8,1,4096]{2,1,0:T(1,128)}, u32[]{:S(2)}) copy-start(f32[8,1,4096]{2,1,0:T(1,128)} %param.15) | copy-start | bytes 393220
  57.5 8.2 %all-to-all-start.1 = ((f32[4,1,384]{2,1,0:T(1,128)}), f32[4,1,384]{2,1,0:T(1,128)S(1)}, u32[]{:S(2)}, u32[]{:S(2)}) async-start(f32[4,1,384]{2,1,0:T(1,128)} %reshape.457), calls=%async_computation.1 | async-start | bytes 12288 | tf_op jit(solution)/shard_map/all_to_all | solution.py:38
  73.4 7.2 %all-to-all-start.4 = ((f32[4,2,1]{1,2,0:T(1,128)}), f32[4,2,1]{1,2,0:T(1,128)S(1)}, u32[]{:S(2)}, u32[]{:S(2)}) async-start(f32[4,2,1]{1,2,0:T(1,128)} %broadcast_in_dim.54), calls=%async_computation.4 | async-start | bytes 4096 | tf_op jit(solution)/shard_map/all_to_all | solution.py:43
  81.3 16.4 %all-to-all-start.5 = ((f32[32,4,2,1]{1,2,3,0:T(2,128)}), f32[32,4,2,1]{1,2,3,0:T(2,128)S(1)}, u32[]{:S(2)}, u32[]{:S(2)}) async-start(f32[32,4,2,1]{1,2,3,0:T(2,128)} %broadcast_in_dim.55), calls=%async_computation.5 | async-start | bytes 65536 | tf_op jit(solution)/shard_map/all_to_all | solution.py:43
  97.8 7.4 %all-to-all-start.2 = ((f32[4,1,384]{2,1,0:T(1,128)}), f32[4,1,384]{2,1,0:T(1,128)S(1)}, u32[]{:S(2)}, u32[]{:S(2)}) async-start(f32[4,1,384]{2,1,0:T(1,128)} %reshape.459), calls=%async_computation.2 | async-start | bytes 12288 | tf_op jit(solution)/shard_map/all_to_all | solution.py:43
  105.7 14.0 %all-to-all-start.6 = ((f32[4,1,2]{2,1,0:T(1,128)}), f32[4,1,2]{2,1,0:T(1,128)S(1)}, u32[]{:S(2)}, u32[]{:S(2)}) async-start(f32[4,1,2]{2,1,0:T(1,128)} %broadcast_in_dim.56), calls=%async_computation.6 | async-start | bytes 4096 | tf_op jit(solution)/shard_map/all_to_all | solution.py:43
  119.7 22.4 %all-to-all-start.3 = ((f32[32,1,1536]{2,1,0:T(1,128)}), f32[32,1,1536]{2,1,0:T(1,128)}, u32[]{:S(2)}, u32[]{:S(2)}) async-start(f32[32,1,1536]{2,1,0:T(1,128)} %reshape.461), calls=%async_computation.3 | async-start | bytes 393216 | tf_op jit(solution)/shard_map/all_to_all | solution.py:43
  148.2 8.3 %copy-start.4 = (f32[8,1,16,512]{3,2,1,0:T(8,128)S(1)}, f32[8,1,16,512]{3,2,1,0:T(8,128)}, u32[]{:S(2)}) copy-start(f32[8,1,16,512]{3,2,1,0:T(8,128)} %param.11) | copy-start | bytes 786436
  148.2 8.3 %copy-start.7 = (pred[16]{0:T(512)(128)(4,1)S(1)}, pred[16]{0:T(512)(128)(4,1)}, u32[]{:S(2)}) copy-start(pred[16]{0:T(512)(128)(4,1)} %constant.53.clone.1) | copy-start | bytes 52
  148.2 8.3 %copy-start.8 = (pred[512]{0:T(512)(128)(4,1)S(1)}, pred[512]{0:T(512)(128)(4,1)}, u32[]{:S(2)}) copy-start(pred[512]{0:T(512)(128)(4,1)} %constant.60.clone.1) | copy-start | bytes 1540
  148.2 8.3 %collective-permute-start.1 = (f32[8,1,16,512]{3,2,0,1:T(8,128)S(1)}, f32[8,1,16,512]{3,2,0,1:T(8,128)S(1)}, u32[]{:S(2)}, u32[]{:S(2)}) collective-permute-start(f32[8,1,16,512]{3,2,0,1:T(8,128)S(1)} %get-tuple-element.305), channel_id=1, source_target_pairs={{0,1},{1,2},{2,3},{4,5},{5,6},{6,7},{8,9},{9,10},{10,11},{12,13},{... | collective-permute-start | bytes 786440 | tf_op jit(solution)/shard_map/ppermute | solution.py:20
where the time goes:
time: 158 us; the launch traced here: 157 us
  starting transfers between devices  55.5 us (35%)
  waiting for transfers between devices  53.1 us (34%)
  other arithmetic  23.8 us (15%)
  local copies, waits for them, and re-layouts  18.1 us (11%)
  between operations  4.51 us (3%)
  matrix products  2.47 us (2%)
    all_to_all x5, waiting for transfers between devices, copy_for_each(): return lax.all_to_all(copies, axis, split_axis=0, concat_axis=0, tiled=True)  33.1 us
    all_to_all x5, starting transfers between devices, copy_for_each(): return lax.all_to_all(copies, axis, split_axis=0, concat_axis=0, tiled=True)  24.6 us
    all_to_all x1, waiting for transfers between devices, summed_on_arrival(): lax.all_to_all(in_blocks(value, dim, peers), axis, 0, 0, tiled=True)  15.2 us
    ppermute x2, starting transfers between devices, from_behind(): return lax.ppermute(block, axis, route)  13.9 us
    all_to_all x1, starting transfers between devices, summed_on_arrival(): lax.all_to_all(in_blocks(value, dim, peers), axis, 0, 0, tiled=True)  13 us
    unnamed x32, local copies, waits for them, and re-layouts  7.69 us
    all_to_all x1, starting transfers between devices, sum_by_axis(): return jnp.sum(lax.all_to_all(own, far, 0, 0, tiled=True), axis=0)  4.01 us
    all_to_all x2, other arithmetic, copy_for_each(): return lax.all_to_all(copies, axis, split_axis=0, concat_axis=0, tiled=True)  3.36 us
  transfers between devices with their start and end apart: 9, of which 8 were waited for; matrix products, arithmetic and copies ran while one was open for 11% of the time, Pallas kernels for 0%

commit v1 on v0

v1 whole, which is shorter than its diff:
```python
import math

import jax
import jax.numpy as jnp
from jax import lax
from jax.experimental import pallas as pl
from jax.experimental.pallas import tpu as pltpu
from jax.sharding import Mesh
from jax.sharding import PartitionSpec as P

SWEEPS = 6
CHAN = ("x", "y", "zfar", "znear")
SHARE = ("x", "y", "znear")
FAR = "zfar"
LANES = 128

index_pairs = ((0, 0), (1, 1), (2, 2), (0, 1), (0, 2), (1, 2))
entry_of = {pair: k for k, pair in enumerate(index_pairs)}
sweep_order = ((0, 1), (0, 2), (1, 2))

VMEM = pl.BlockSpec(memory_space=pltpu.VMEM)
SMEM = pl.BlockSpec(memory_space=pltpu.SMEM)


def from_behind(block, axis, distance):
    devices = range(lax.axis_size(axis))
    route = [(i - distance, i) for i in devices if i - distance in devices]
    return lax.ppermute(block, axis, route)


def gram_kernel(rate_ref, keep_ref, x_ref, next_ref, dual_ref, cand_ref, out_ref):
    channels, rows, cols = x_ref.shape
    tiles = cols // LANES
    per_row = len(index_pairs) * tiles
    rate = rate_ref[0]
    keep = keep_ref[0]
    row_id = lax.broadcasted_iota(jnp.int32, (rows, LANES), 0)
    lane_id = lax.broadcasted_iota(jnp.int32, (rows, LANES), 1)
    inner_row = row_id < rows - 1
    edge_lane = lane_id == LANES - 1
    for j in range(tiles):
        here = pl.ds(j * LANES, LANES)
        sums = [jnp.zeros((rows, LANES), jnp.float32) for _ in index_pairs]
        for c in range(channels):
            x = x_ref[c, :, here]
            below = pltpu.roll(x, rows - 1, 0)
            right = pltpu.roll(x, LANES - 1, 1)
            if j + 1 < tiles:
                after = pltpu.roll(x_ref[c, :, pl.ds((j + 1) * LANES, LANES)], LANES - 1, 1)
            else:
                after = x
            steps = (
                jnp.where(inner_row, below - x, 0.0),
                jnp.where(edge_lane, after, right) - x,
                (next_ref[c, :, here] - x) * keep,
            )
            cand = [dual_ref[a, c, :, here] + rate * steps[a] for a in range(3)]
            for a in range(3):
                cand_ref[a, c, :, here] = cand[a]
            sums = [s + cand[a] * cand[b] for s, (a, b) in zip(sums, index_pairs)]
        for k, s in enumerate(sums):
            out_ref[pl.ds(k * tiles + j, rows, stride=per_row), :] = s


def pass_on_kernel(parts_ref, misfit_ref, out_ref):
    peers, per_row, _ = parts_ref.shape
    total = parts_ref[0]
    for p in range(1, peers):
        total = total + parts_ref[p]
    misfit = misfit_ref[...]
    for p in range(out_ref.shape[0]):
        out_ref[p, :per_row, :] = total
        out_ref[p, per_row:, :] = misfit


def rotate(entry, vectors, p, q):
    k = 3 - p - q
    pq, kp, kq = (entry_of[tuple(sorted(s))] for s in ((p, q), (k, p), (k, q)))
    across, twice = entry[q] - entry[p], 2.0 * entry[pq]
    square = across * across + twice * twice
    still = square == 0.0
    inverse = lax.rsqrt(jnp.where(still, 1.0, square))
    length = square * inverse
    half = jnp.where(still, 1.0, 0.5 + 0.5 * jnp.abs(across) * inverse)
    root = lax.rsqrt(half)
    large, small = half * root, 0.5 * jnp.abs(twice) * inverse * root
    ahead = across >= 0.0
    cosine = jnp.where(ahead, large, small)
    sine = jnp.where(ahead, small, large)
    sine = jnp.where(twice < 0.0, -sine, sine)
    middle = entry[p] + entry[q]
    entry, vectors = list(entry), [list(row) for row in vectors]
    entry[p], entry[q] = 0.5 * (middle - length), 0.5 * (middle + length)
    entry[pq] = jnp.where(still, entry[pq], 0.0)
    entry[kp], entry[kq] = (
        cosine * entry[kp] - sine * entry[kq],
        sine * entry[kp] + cosine * entry[kq],
    )
    for row in vectors:
        row[p], row[q] = cosine * row[p] - sine * row[q], sine * row[p] + cosine * row[q]
    return entry, vectors


def factor_kernel(radius_ref, parts_ref, out_ref):
    peers, held, _ = parts_ref.shape
    tiles = out_ref.shape[1] // 8
    entries = len(index_pairs)

    def summed(start, size):
        total = parts_ref[0, pl.ds(start, size), :]
        for p in range(1, peers):
            total = total + parts_ref[p, pl.ds(start, size), :]
        return total

    radius = radius_ref[0]
    entry = [summed(k * tiles, tiles) for k in range(entries)]
    one, zero = jnp.ones_like(entry[0]), jnp.zeros_like(entry[0])
    vectors = [[one if r == c else zero for c in range(3)] for r in range(3)]
    for _ in range(SWEEPS):
        for p, q in sweep_order:
            entry, vectors = rotate(entry, vectors, p, q)
    roots = [jnp.sqrt(jnp.maximum(entry[d], 0.0)) for d in range(3)]
    scales = [radius / jnp.maximum(root, radius) for root in roots]
    excess = sum(jnp.maximum(root - radius, 0.0) for root in roots) / radius
    misfit = sum(summed(k, tiles) for k in range(entries * tiles, held, tiles))
    rows = [
        sum(vectors[a][d] * scales[d] * vectors[b][d] for d in range(3)) for a, b in index_pairs
    ] + [excess, misfit]
    for p in range(out_ref.shape[0]):
        for k, row in enumerate(rows):
            out_ref[p, pl.ds(k * tiles, tiles), :] = row


def apply_kernel(factor_ref, cand_ref, new_ref, send_ref, sums_ref):
    _, channels, rows, cols = cand_ref.shape
    tiles = cols // LANES
    entries = len(index_pairs)
    per_row = factor_ref.shape[0] // rows

    def image(k, j):
        return factor_ref[pl.ds(k * tiles + j, rows, stride=per_row), :]

    for k in range(2):
        sums_ref[k] = sum(image(entries + k, j) for j in range(tiles))
    for j in range(tiles):
        here = pl.ds(j * LANES, LANES)
        factor = [image(k, j) for k in range(entries)]
        for c in range(channels):
            cand = [cand_ref[a, c, :, here] for a in range(3)]
            for a in (2, 1, 0):
                new = sum(cand[b] * factor[entry_of[tuple(sorted((b, a)))]] for b in range(3))
                new_ref[a, c, :, here] = new
                if a == 2:
                    send_ref[c, :, here] = new


def backward_difference(component, along_axis):
    length = component.shape[along_axis]
    kept_part = lax.slice_in_dim(component, 0, length - 1, axis=along_axis)
    zero_layer = jnp.zeros_like(lax.slice_in_dim(component, 0, 1, axis=along_axis))
    masked = jnp.concatenate([kept_part, zero_layer], axis=along_axis)
    earlier = jnp.concatenate([zero_layer, kept_part], axis=along_axis)
    return masked - earlier


def picked_blocks(blocks, where, count):
    chosen = (where[:, None] == jnp.arange(count, dtype=jnp.int32)[None, :]).astype(jnp.bfloat16)
    return jnp.einsum("tc,bcj->tbj", chosen, blocks, preferred_element_type=jnp.float32).astype(
        jnp.bfloat16
    )


def gathered_products(products, where, count):
    chosen = (where[:, None] == jnp.arange(count, dtype=jnp.int32)[None, :]).astype(jnp.float32)
    return jnp.einsum("tc,tbj->bcj", chosen, products, precision=lax.Precision.HIGHEST)


def on_device(
    volume_now,
    extrapolated,
    dual_grad,
    dual_data,
    measured,
    projector,
    tile_rows,
    tile_cols,
    dual_step,
    primal_step,
    reg_weight,
):
    f32 = jnp.float32
    dual_rate = dual_step[0]
    primal_rate = primal_step[0]
    channels, slices, row_count, col_count = volume_now.shape
    pixels = row_count * col_count
    rays = dual_data.shape[2]
    edge = projector.shape[1]
    share_count, far_count = lax.axis_size(SHARE), lax.axis_size(FAR)
    slab_count = lax.axis_size("slab")
    total_channels = channels * share_count * far_count
    tiles = col_count // LANES
    held = len(index_pairs) * tiles
    last_slice = lax.axis_index("slab") == slab_count - 1
    images = (channels, row_count, col_count)

    following = from_behind(extrapolated, "slab", -1)
    keep = jnp.where(last_slice, 0.0, 1.0).reshape(1)
    candidate, partial_gram = pl.pallas_call(
        gram_kernel,
        out_shape=(
            jax.ShapeDtypeStruct((3, *images), f32),
            jax.ShapeDtypeStruct((row_count * held, LANES), f32),
        ),
        in_specs=[SMEM, SMEM, VMEM, VMEM, VMEM],
        out_specs=(VMEM, VMEM),
        name="gram",
    )(
        dual_step,
        keep,
        extrapolated.reshape(images),
        following.reshape(images),
        dual_grad.reshape(3, *images),
    )
    gram_parts = lax.all_to_all(
        partial_gram.reshape(share_count, held, LANES), SHARE, 0, 0, tiled=True
    )

    rounded = extrapolated.reshape(channels, pixels // edge, edge).astype(jnp.bfloat16)
    picked = picked_blocks(rounded, tile_cols, pixels // edge)
    products = jnp.einsum("tij,tbj->tbi", projector, picked, preferred_element_type=f32)
    projected = gathered_products(products, tile_rows, rays // edge)
    residual = projected - measured.reshape(projected.shape)
    data_new = (dual_data.reshape(projected.shape) + dual_rate * residual) / (1.0 + dual_rate)
    misfit_part = jnp.sum((residual * residual).reshape(-1, 8, LANES), axis=0)

    to_far = pl.pallas_call(
        pass_on_kernel,
        out_shape=jax.ShapeDtypeStruct((far_count, held + 8, LANES), f32),
        in_specs=[VMEM, VMEM],
        out_specs=VMEM,
        name="pass_on",
    )(gram_parts, misfit_part)
    far_parts = lax.all_to_all(to_far, FAR, 0, 0, tiled=True)

    data_low = data_new.astype(jnp.bfloat16)
    picked_back = picked_blocks(data_low, tile_rows, rays // edge)
    products_back = jnp.einsum("tij,tbi->tbj", projector, picked_back, preferred_element_type=f32)
    back_proj = gathered_products(products_back, tile_cols, pixels // edge).reshape(
        volume_now.shape
    )

    radius = reg_weight * math.sqrt(total_channels)
    to_share = pl.pallas_call(
        factor_kernel,
        out_shape=jax.ShapeDtypeStruct((share_count, 8 * tiles, LANES), f32),
        in_specs=[SMEM, VMEM],
        out_specs=VMEM,
        name="factor",
    )(radius, far_parts)
    factor_rows = lax.all_to_all(to_share, SHARE, 0, 0, tiled=True)

    grad_new, to_next, sums = pl.pallas_call(
        apply_kernel,
        out_shape=(
            jax.ShapeDtypeStruct((3, *images), f32),
            jax.ShapeDtypeStruct(images, f32),
            jax.ShapeDtypeStruct((2, row_count, LANES), f32),
        ),
        in_specs=[VMEM, VMEM],
        out_specs=(VMEM, VMEM, VMEM),
        name="apply",
    )(factor_rows.reshape(share_count * 8 * tiles, LANES), candidate)
    prior_layer = from_behind(to_next, "slab", 1)

    sums = jnp.broadcast_to(sums.sum(axis=(1, 2))[None, :, None], (slab_count, 2, LANES))
    combined = lax.all_to_all(sums, "slab", 0, 0, tiled=True)[:, :, 0].sum(axis=0)

    masked = jnp.where(last_slice, 0.0, to_next)
    ready = volume_now.reshape(images) - primal_rate * (
        back_proj.reshape(images)
        - (backward_difference(grad_new[0], 1) + backward_difference(grad_new[1], 2) + masked)
    )
    updated = jnp.maximum(ready - primal_rate * prior_layer, 0.0)
    totals = jnp.stack(
        [
            combined[1] / (total_channels * slab_count * slices * rays),
            combined[0] / (slab_count * slices * pixels),
        ]
    )
    return (
        updated.reshape(volume_now.shape),
        grad_new.reshape(dual_grad.shape),
        data_new.reshape(dual_data.shape),
        totals,
    )


def solution(mesh):
    torus = Mesh(
        mesh.devices.reshape(4, 2, 8, 2, mesh.shape["slab"]), ("x", "y", "zfar", "znear", "slab")
    )
    placed = (
        P(CHAN, "slab", None, None),
        P(CHAN, "slab", None, None),
        P(None, CHAN, "slab", None, None),
        P(CHAN, "slab", None),
        P(CHAN, "slab", None),
        P(),
        P(),
        P(),
        P(),
        P(),
        P(),
    )
    return jax.shard_map(
        on_device,
        mesh=torus,
        in_specs=placed,
        out_specs=(
            P(CHAN, "slab", None, None),
            P(None, CHAN, "slab", None, None),
            P(CHAN, "slab", None),
            P(),
        ),
        check_vma=False,
    )
```

time: 158 us -> 92 us (0.58)
  waiting for transfers between devices: 53.1 us -> 22.7 us
  other arithmetic: 23.8 us -> 5.19 us
  starting transfers between devices: 55.5 us -> 42.6 us
  local copies, waits for them, and re-layouts: 18.1 us -> 5.23 us
  Pallas kernels: 0 us -> 8.64 us
    all_to_all x7 -> x4, waiting for transfers between devices: 50.9 us -> 22.7 us  [the longest x1 12 us: on_device(): far_parts = lax.all_to_all(to_far, FAR, 0, 0, tiled=True)]
    all_to_all x7 -> x4, starting transfers between devices: 41.6 us -> 26.9 us  [the longest x1 13.9 us: on_device(): far_parts = lax.all_to_all(to_far, FAR, 0, 0, tiled=True)]
    pallas_call x0 -> x4, Pallas kernels: none -> 8.64 us  [the longest x1 2.51 us: on_device(): pl.pallas_call(gram_kernel, out_shape=(jax.ShapeDtypeStruct((3, *images),...]
    all_to_all x4 -> x0, other arithmetic: 6.71 us -> none  [the longest x2 3.36 us: copy_for_each(): return lax.all_to_all(copies, axis, split_axis=0, concat_axis=0, tiled=True)]
    unnamed x32 -> x26, local copies, waits for them, and re-layouts: 7.69 us -> 2.78 us
    sub x12 -> x0, other arithmetic: 2.56 us -> none  [the longest x2 2.31 us: forward_difference(): return jnp.concatenate([later - kept_part, zero_layer], axis=along_axis)]
    another operation x4 -> x1, other arithmetic: 2.94 us -> 0.59 us  [on_device(): jnp.stack([combined[1] / (total_channels * slab_count * slices * rays), c...]
    add x14 -> x0, other arithmetic: 2.23 us -> none  [the longest x1 1.39 us: on_device(): candidate = dual_grad + dual_rate * gradient]
  transfers between devices with their start and end apart: 9 -> 6, of which waited for: 8 -> 4; matrix products, arithmetic and copies ran while one was open for 11% -> 9% of each run, Pallas kernels for 0% -> 0%
where the time goes in v1:
time: 92 us; the launch traced here: 91.3 us
  starting transfers between devices  42.6 us (46%)
  waiting for transfers between devices  22.7 us (25%)
  Pallas kernels  8.64 us (9%)
  local copies, waits for them, and re-layouts  5.23 us (6%)
  other arithmetic  5.19 us (6%)
  between operations  4.09 us (4%)
  matrix products  2.83 us (3%)
    ppermute x2, starting transfers between devices, from_behind(): return lax.ppermute(block, axis, route)  15.7 us
    all_to_all x1, starting transfers between devices, on_device(): far_parts = lax.all_to_all(to_far, FAR, 0, 0, tiled=True)  13.9 us
    all_to_all x1, waiting for transfers between devices, on_device(): far_parts = lax.all_to_all(to_far, FAR, 0, 0, tiled=True)  12 us
    all_to_all x1, starting transfers between devices, on_device(): lax.all_to_all(partial_gram.reshape(share_count, held, LANES), SHARE, 0,...  6.19 us
    all_to_all x1, waiting for transfers between devices, on_device(): factor_rows = lax.all_to_all(to_share, SHARE, 0, 0, tiled=True)  4.78 us
    all_to_all x1, waiting for transfers between devices, on_device(): lax.all_to_all(partial_gram.reshape(share_count, held, LANES), SHARE, 0,...  3.84 us
    all_to_all x1, starting transfers between devices, on_device(): factor_rows = lax.all_to_all(to_share, SHARE, 0, 0, tiled=True)  3.53 us
    all_to_all x1, starting transfers between devices, on_device(): lax.all_to_all(sums, 'slab', 0, 0, tiled=True)[:, :, 0].sum(axis=0)  3.24 us
  transfers between devices with their start and end apart: 6, of which 4 were waited for; matrix products, arithmetic and copies ran while one was open for 9% of the time, Pallas kernels for 0%

profile of v1, /device:TPU:1, one launch (start us, length us, event | category | flops | bytes accessed | tf_op | source)
XLA Modules:
  0.0 91.3 jit_solution(3033787188239059009)
XLA Ops:
  0.6 0.0 copy-start
  0.6 0.0 copy-start.9
  0.7 8.9 %collective-permute-start = (f32[8,1,16,512]{3,2,0,1:T(8,128)}, f32[8,1,16,512]{3,2,0,1:T(8,128)S(1)}, u32[]{:S(2)}, u32[]{:S(2)}) collective-permute-start(f32[8,1,16,512]{3,2,0,1:T(8,128)} %bitcast.64), channel_id=1, source_target_pairs={{1,0},{2,1},{3,2},{5,4},{6,5},{7,6},{9,8},{10,9},{11,10},{13,12},{... | collective-permute-start | bytes 786440 | tf_op jit(solution)/shard_map/ppermute | solution.py:28
  9.6 1.0 %convert_element_type.19 = bf16[8,1,16,512]{3,2,1,0:T(8,128)(2,1)S(1)} convert(f32[8,1,16,512]{3,2,1,0:T(8,128)} %param.12) | non-fusion elementwise | flops 65536 | bytes 393216 | tf_op jit(solution)/shard_map/convert_element_type | solution.py:228
  11.2 0.1 convert_element_type.20
  11.3 0.0 collective-permute-done
  11.3 0.0 copy-start.5
  11.3 0.7 copy-done.5
  12.0 2.5 %gram.1 = (f32[3,8,16,512]{3,2,1,0:T(8,128)}, f32[384,128]{1,0:T(8,128)}) custom-call(f32[1]{0:T(128)} %copy.48.rate_ref, f32[1]{0:T(128)} %bitcast.10.keep_ref, f32[8,16,512]{2,1,0:T(8,128)} %bitcast.65, f32[8,16,512]{2,1,0:T(8,128)} %bitcast.72, f32[3,8,16,512]{3,2,1,0:T(8,128)} %bitcast.69), custom_call_target="tpu_custom_call" | custom-call | tf_op jit(solution)/shard_map/gram/pallas_call | solution.py:208
  14.6 6.2 %all-to-all-start = ((f32[16,24,128]{2,1,0:T(8,128)}), f32[16,24,128]{2,1,0:T(8,128)S(1)}, u32[]{:S(2)}, u32[]{:S(2)}) async-start(f32[16,24,128]{2,1,0:T(8,128)} %bitcast.73), calls=%async_computation | async-start | bytes 393216 | tf_op jit(solution)/shard_map/all_to_all | solution.py:224
  20.7 0.0 copy-done.9
  20.8 0.2 convolution_convert_fusion
  21.0 0.0 copy-done
  21.0 1.2 %fusion.8 = f32[64,8,128]{2,1,0:T(8,128)S(1)} fusion(bf16[64,128,128]{2,1,0:T(8,128)(2,1)S(1)} %copy-done, bf16[64,8,128]{2,0,1:T(8,128)(2,1)S(1)} %convolution_convert_fusion), kind=kOutput, calls=%fused_computation.15 | convolution fusion | flops 16777216 | bytes 2490368 | tf_op jit(solution)/shard_map/tij,tbj->tbi/dot_general | solution.py:230
  22.2 0.0 copy-done.7
  22.2 0.0 copy-done.8
  22.2 0.0 copy-done.10
  22.2 0.3 add_divide_fusion
  22.5 0.0 copy-start.4
  22.5 0.6 reduce_sum.27.misfit_ref
  23.1 3.8 %all-to-all-done.parts_ref = f32[16,24,128]{2,1,0:T(8,128)S(1)} async-done(((f32[16,24,128]{2,1,0:T(8,128)}), f32[16,24,128]{2,1,0:T(8,128)S(1)}, u32[]{:S(2)}, u32[]{:S(2)}) %all-to-all-start) | async-done | bytes 196640 | tf_op jit(solution)/shard_map/all_to_all | solution.py:224
  27.0 0.7 copy-done.2
  27.6 1.6 %pass_on.1 = f32[8,32,128]{2,1,0:T(8,128)} custom-call(f32[16,24,128]{2,1,0:T(8,128)} %copy-done.2, f32[8,128]{1,0:T(8,128)} %reduce_sum.27.misfit_ref), custom_call_target="tpu_custom_call" | custom-call | tf_op jit(solution)/shard_map/pass_on/pallas_call | solution.py:236
  29.3 13.9 %all-to-all-start.1 = ((f32[8,32,128]{2,1,0:T(8,128)}), f32[8,32,128]{2,1,0:T(8,128)S(1)}, u32[]{:S(2)}, u32[]{:S(2)}) async-start(f32[8,32,128]{2,1,0:T(8,128)} %pass_on.1), calls=%async_computation.1 | async-start | bytes 262144 | tf_op jit(solution)/shard_map/all_to_all | solution.py:243
  43.8 12.0 %all-to-all-done.1.parts_ref = f32[8,32,128]{2,1,0:T(8,128)S(1)} async-done(((f32[8,32,128]{2,1,0:T(8,128)}), f32[8,32,128]{2,1,0:T(8,128)S(1)}, u32[]{:S(2)}, u32[]{:S(2)}) %all-to-all-start.1) | async-done | bytes 131104 | tf_op jit(solution)/shard_map/all_to_all | solution.py:243
  55.9 0.7 copy-done.3
  56.5 2.1 %factor.1 = f32[16,32,128]{2,1,0:T(8,128)} custom-call(f32[1]{0:T(128)S(6)} %mul.25.radius_ref, f32[8,32,128]{2,1,0:T(8,128)} %copy-done.3), custom_call_target="tpu_custom_call" | custom-call | tf_op jit(solution)/shard_map/factor/pallas_call | solution.py:253
  58.6 3.5 %all-to-all-start.2 = ((f32[16,32,128]{2,1,0:T(8,128)}), f32[16,32,128]{2,1,0:T(8,128)S(1)}, u32[]{:S(2)}, u32[]{:S(2)}) async-start(f32[16,32,128]{2,1,0:T(8,128)} %factor.1), calls=%async_computation.2 | async-start | bytes 524288 | tf_op jit(solution)/shard_map/all_to_all | solution.py:260
  62.1 0.2 convolution_convert_fusion.1
  62.4 0.6 fusion.6
  63.0 0.0 copy-done.4
  63.0 0.0 copy-start.12
  63.0 0.3 convolution_bitcast_fusion
  64.0 4.8 %all-to-all-done.2 = f32[16,32,128]{2,1,0:T(8,128)S(1)} async-done(((f32[16,32,128]{2,1,0:T(8,128)}), f32[16,32,128]{2,1,0:T(8,128)S(1)}, u32[]{:S(2)}, u32[]{:S(2)}) %all-to-all-start.2) | async-done | bytes 262176 | tf_op jit(solution)/shard_map/all_to_all | solution.py:260
  68.8 0.7 copy-done.1
  69.5 2.4 %apply.1 = (f32[3,8,16,512]{3,2,1,0:T(8,128)}, f32[8,16,512]{2,1,0:T(8,128)}, f32[2,16,128]{2,1,0:T(8,128)}) custom-call(f32[512,128]{1,0:T(8,128)} %bitcast.66, f32[3,8,16,512]{3,2,1,0:T(8,128)} %get-tuple-element.10.cand_ref), custom_call_target="tpu_custom_call" | custom-call | tf_op jit(solution)/shard_map/apply/pallas_call | solution.py:262
  72.0 6.8 %collective-permute-start.1 = (f32[8,16,512]{2,1,0:T(8,128)}, f32[8,16,512]{2,1,0:T(8,128)S(1)}, u32[]{:S(2)}, u32[]{:S(2)}) collective-permute-start(f32[8,16,512]{2,1,0:T(8,128)} %get-tuple-element.12), channel_id=1, source_target_pairs={{0,1},{1,2},{2,3},{4,5},{5,6},{6,7},{8,9},{9,10},{10,11},{12,13},{... | collective-permute-start | bytes 786440 | tf_op jit(solution)/shard_map/ppermute | solution.py:28
  78.8 0.8 reduce_sum.28
  79.6 0.7 broadcast_in_dim.3
  80.2 3.2 %all-to-all-start.3 = ((f32[4,2,128]{2,1,0:T(2,128)}), f32[4,2,128]{2,1,0:T(2,128)S(1)}, u32[]{:S(2)}, u32[]{:S(2)}) async-start(f32[4,2,128]{2,1,0:T(2,128)} %broadcast_in_dim.3), calls=%async_computation.3 | async-start | bytes 8192 | tf_op jit(solution)/shard_map/all_to_all | solution.py:276
  83.5 1.1 %slice_bitcast_fusion.1 = (f32[8,16,512]{2,1,0:T(8,128)S(1)}, f32[8,16,512]{2,1,0:T(8,128)S(1)}) fusion(f32[3,8,16,512]{3,2,1,0:T(8,128)} %get-tuple-element.11), kind=kLoop, calls=%fused_computation.12 | loop fusion | bytes 1048576 | tf_op jit(solution)/shard_map/squeeze | solution.py:281
  84.6 2.1 %all-to-all-done.3 = f32[4,2,128]{2,1,0:T(2,128)S(1)} async-done(((f32[4,2,128]{2,1,0:T(2,128)}), f32[4,2,128]{2,1,0:T(2,128)S(1)}, u32[]{:S(2)}, u32[]{:S(2)}) %all-to-all-start.3) | async-done | bytes 4128 | tf_op jit(solution)/shard_map/all_to_all | solution.py:276
  86.6 0.1 slice_reduce_fusion
  86.7 0.6 fusion.21
  88.6 0.6 pad_maximum_fusion
  89.2 0.0 collective-permute-done.1
  89.2 0.0 copy-done.6
  89.2 2.1 %fusion.3 = f32[8,1,16,512]{3,2,1,0:T(8,128)} fusion(f32[8,1,16,512]{3,2,1,0:T(8,128)S(1)} %copy-done.6, f32[8,16,512]{2,1,0:T(8,128)S(1)} %collective-permute-done.1, f32[8,16,512]{2,1,0:T(8,128)S(1)} %reshape_reshape.3, f32[8,16,512]{2,1,0:T(8,128)} %get-tuple-element.12, f32[8,16,511]{2,1,0:T(8,128)S(1)} %bitcast.68, f32[8,15,512]{2,1,0:T(8,128)S(1)} %bitcast.67, ...), kind=kLoop, calls=%fused_computation.8 | loop fusion | flops 851968 | bytes 2342933
  (11 shorter events, 0.1 us)
Async XLA Ops:
  0.6 20.4 %copy-start = (bf16[64,128,128]{2,1,0:T(8,128)(2,1)S(1)}, bf16[64,128,128]{2,1,0:T(8,128)(2,1)}, u32[]{:S(2)}) copy-start(bf16[64,128,128]{2,1,0:T(8,128)(2,1)} %param.16) | copy-start | bytes 6291460
  0.6 20.1 %copy-start.9 = (s32[64]{0:T(128)S(1)}, s32[64]{0:T(128)}, u32[]{:S(2)}) copy-start(s32[64]{0:T(128)} %param.18) | copy-start | bytes 772
  0.7 10.7 %collective-permute-start = (f32[8,1,16,512]{3,2,0,1:T(8,128)}, f32[8,1,16,512]{3,2,0,1:T(8,128)S(1)}, u32[]{:S(2)}, u32[]{:S(2)}) collective-permute-start(f32[8,1,16,512]{3,2,0,1:T(8,128)} %bitcast.64), channel_id=1, source_target_pairs={{1,0},{2,1},{3,2},{5,4},{6,5},{7,6},{9,8},{10,9},{11,10},{13,12},{... | collective-permute-start | bytes 786440 | tf_op jit(solution)/shard_map/ppermute | solution.py:28
  11.3 0.7 copy-start.5
  12.0 10.2 %copy-start.7 = (f32[8,1,4096]{2,1,0:T(1,128)S(1)}, f32[8,1,4096]{2,1,0:T(1,128)}, u32[]{:S(2)}) copy-start(f32[8,1,4096]{2,1,0:T(1,128)} %param.14) | copy-start | bytes 393220
  12.0 10.2 %copy-start.8 = (f32[8,1,4096]{2,1,0:T(1,128)S(1)}, f32[8,1,4096]{2,1,0:T(1,128)}, u32[]{:S(2)}) copy-start(f32[8,1,4096]{2,1,0:T(1,128)} %param.15) | copy-start | bytes 393220
  12.0 10.2 %copy-start.10 = (s32[64]{0:T(128)S(1)}, s32[64]{0:T(128)}, u32[]{:S(2)}) copy-start(s32[64]{0:T(128)} %param.17) | copy-start | bytes 772
  14.6 12.4 %all-to-all-start = ((f32[16,24,128]{2,1,0:T(8,128)}), f32[16,24,128]{2,1,0:T(8,128)S(1)}, u32[]{:S(2)}, u32[]{:S(2)}) async-start(f32[16,24,128]{2,1,0:T(8,128)} %bitcast.73), calls=%async_computation | async-start | bytes 393216 | tf_op jit(solution)/shard_map/all_to_all | solution.py:224
  22.5 40.6 %copy-start.4 = (f32[8,32,128]{2,1,0:T(8,128)}, f32[8,32,128]{2,1,0:T(8,128)S(1)}, u32[]{:S(2)}) copy-start(f32[8,32,128]{2,1,0:T(8,128)S(1)} %get-tuple-element.28) | copy-start | bytes 393220
  27.0 0.7 copy-start.2
  29.3 26.6 %all-to-all-start.1 = ((f32[8,32,128]{2,1,0:T(8,128)}), f32[8,32,128]{2,1,0:T(8,128)S(1)}, u32[]{:S(2)}, u32[]{:S(2)}) async-start(f32[8,32,128]{2,1,0:T(8,128)} %pass_on.1), calls=%async_computation.1 | async-start | bytes 262144 | tf_op jit(solution)/shard_map/all_to_all | solution.py:243
  55.9 0.7 copy-start.3
  58.6 10.2 %all-to-all-start.2 = ((f32[16,32,128]{2,1,0:T(8,128)}), f32[16,32,128]{2,1,0:T(8,128)S(1)}, u32[]{:S(2)}, u32[]{:S(2)}) async-start(f32[16,32,128]{2,1,0:T(8,128)} %factor.1), calls=%async_computation.2 | async-start | bytes 524288 | tf_op jit(solution)/shard_map/all_to_all | solution.py:260
  63.0 26.2 %copy-start.6 = (f32[8,1,16,512]{3,2,1,0:T(8,128)S(1)}, f32[8,1,16,512]{3,2,1,0:T(8,128)}, u32[]{:S(2)}) copy-start(f32[8,1,16,512]{3,2,1,0:T(8,128)} %param.11) | copy-start | bytes 786436
  63.0 26.2 %copy-start.11 = (pred[16]{0:T(512)(128)(4,1)S(1)}, pred[16]{0:T(512)(128)(4,1)}, u32[]{:S(2)}) copy-start(pred[16]{0:T(512)(128)(4,1)} %constant.10.clone.1) | copy-start | bytes 52
  63.0 26.2 %copy-start.12 = (pred[512]{0:T(512)(128)(4,1)S(1)}, pred[512]{0:T(512)(128)(4,1)}, u32[]{:S(2)}) copy-start(pred[512]{0:T(512)(128)(4,1)} %constant.24.clone.1) | copy-start | bytes 1540
  68.8 0.7 copy-start.1
  72.0 17.3 %collective-permute-start.1 = (f32[8,16,512]{2,1,0:T(8,128)}, f32[8,16,512]{2,1,0:T(8,128)S(1)}, u32[]{:S(2)}, u32[]{:S(2)}) collective-permute-start(f32[8,16,512]{2,1,0:T(8,128)} %get-tuple-element.12), channel_id=1, source_target_pairs={{0,1},{1,2},{2,3},{4,5},{5,6},{6,7},{8,9},{9,10},{10,11},{12,13},{... | collective-permute-start | bytes 786440 | tf_op jit(solution)/shard_map/ppermute | solution.py:28
  80.2 6.4 %all-to-all-start.3 = ((f32[4,2,128]{2,1,0:T(2,128)}), f32[4,2,128]{2,1,0:T(2,128)S(1)}, u32[]{:S(2)}, u32[]{:S(2)}) async-start(f32[4,2,128]{2,1,0:T(2,128)} %broadcast_in_dim.3), calls=%async_computation.3 | async-start | bytes 8192 | tf_op jit(solution)/shard_map/all_to_all | solution.py:276

commit v2 on v1

--- a/solution.py
+++ b/solution.py
@@ -1,3 +1,4 @@
+import functools
 import math
 
 import jax
@@ -17,9 +18,18 @@
 index_pairs = ((0, 0), (1, 1), (2, 2), (0, 1), (0, 2), (1, 2))
 entry_of = {pair: k for k, pair in enumerate(index_pairs)}
 sweep_order = ((0, 1), (0, 2), (1, 2))
+own_pairs = ((0, 0), (1, 1), (0, 1))
 
 VMEM = pl.BlockSpec(memory_space=pltpu.VMEM)
 SMEM = pl.BlockSpec(memory_space=pltpu.SMEM)
+
+
+def near(array):
+    return pltpu.with_memory_space_constraint(array, pltpu.VMEM)
+
+
+def kept_near(shape):
+    return pltpu.VMEM(shape, jnp.float32)
 
 
 def from_behind(block, axis, distance):
@@ -28,19 +38,15 @@
     return lax.ppermute(block, axis, route)
 
 
-def gram_kernel(rate_ref, keep_ref, x_ref, next_ref, dual_ref, cand_ref, out_ref):
+def own_kernel(rate_ref, x_ref, dual_ref, cand_ref, sums_ref):
     channels, rows, cols = x_ref.shape
     tiles = cols // LANES
-    per_row = len(index_pairs) * tiles
     rate = rate_ref[0]
-    keep = keep_ref[0]
-    row_id = lax.broadcasted_iota(jnp.int32, (rows, LANES), 0)
-    lane_id = lax.broadcasted_iota(jnp.int32, (rows, LANES), 1)
-    inner_row = row_id < rows - 1
-    edge_lane = lane_id == LANES - 1
+    inner_row = lax.broadcasted_iota(jnp.int32, (rows, LANES), 0) < rows - 1
+    edge_lane = lax.broadcasted_iota(jnp.int32, (rows, LANES), 1) == LANES - 1
     for j in range(tiles):
         here = pl.ds(j * LANES, LANES)
-        sums = [jnp.zeros((rows, LANES), jnp.float32) for _ in index_pairs]
+        sums = [jnp.zeros((rows, LANES), jnp.float32) for _ in own_pairs]
         for c in range(channels):
             x = x_ref[c, :, here]
             below = pltpu.roll(x, rows - 1, 0)
@@ -49,17 +55,35 @@
                 after = pltpu.roll(x_ref[c, :, pl.ds((j + 1) * LANES, LANES)], LANES - 1, 1)
             else:
                 after = x
-            steps = (
-                jnp.where(inner_row, below - x, 0.0),
-                jnp.where(edge_lane, after, right) - x,
-                (next_ref[c, :, here] - x) * keep,
-            )
-            cand = [dual_ref[a, c, :, here] + rate * steps[a] for a in range(3)]
-            for a in range(3):
+            steps = (jnp.where(inner_row, below - x, 0.0), jnp.where(edge_lane, after, right) - x)
+            cand = [dual_ref[a, c, :, here] + rate * steps[a] for a in range(2)]
+            for a in range(2):
                 cand_ref[a, c, :, here] = cand[a]
-            sums = [s + cand[a] * cand[b] for s, (a, b) in zip(sums, index_pairs)]
+            sums = [s + cand[a] * cand[b] for s, (a, b) in zip(sums, own_pairs)]
         for k, s in enumerate(sums):
-            out_ref[pl.ds(k * tiles + j, rows, stride=per_row), :] = s
+            sums_ref[k, :, here] = s
+
+
+def gram_kernel(rate_ref, keep_ref, x_ref, next_ref, dual_ref, own_ref, sums_ref, cand_ref, out_ref):
+    channels, rows, cols = x_ref.shape
+    tiles = cols // LANES
+    per_row = len(index_pairs) * tiles
+    rate = rate_ref[0]
+    keep = keep_ref[0]
+    for j in range(tiles):
+        here = pl.ds(j * LANES, LANES)
+        sums = {pair: sums_ref[k, :, here] for k, pair in enumerate(own_pairs)}
+        for b in range(3):
+            sums[b, 2] = jnp.zeros((rows, LANES), jnp.float32)
+        for c in range(channels):
+            step = (next_ref[c, :, here] - x_ref[c, :, here]) * keep
+            cand = dual_ref[2, c, :, here] + rate * step
+            cand_ref[c, :, here] = cand
+            for b in range(2):
+                sums[b, 2] = sums[b, 2] + own_ref[b, c, :, here] * cand
+            sums[2, 2] = sums[2, 2] + cand * cand
+        for k, pair in enumerate(index_pairs):
+            out_ref[pl.ds(k * tiles + j, rows, stride=per_row), :] = sums[pair]
 
 
 def pass_on_kernel(parts_ref, misfit_ref, out_ref):
@@ -101,10 +125,10 @@
     return entry, vectors
 
 
-def factor_kernel(radius_ref, parts_ref, out_ref):
+def factor_kernel(radius_ref, parts_ref, out_ref, sums_ref):
     peers, held, _ = parts_ref.shape
-    tiles = out_ref.shape[1] // 8
     entries = len(index_pairs)
+    tiles = out_ref.shape[1] // entries
 
     def summed(start, size):
         total = parts_ref[0, pl.ds(start, size), :]
@@ -122,45 +146,84 @@
     roots = [jnp.sqrt(jnp.maximum(entry[d], 0.0)) for d in range(3)]
     scales = [radius / jnp.maximum(root, radius) for root in roots]
     excess = sum(jnp.maximum(root - radius, 0.0) for root in roots) / radius
-    misfit = sum(summed(k, tiles) for k in range(entries * tiles, held, tiles))
     rows = [
         sum(vectors[a][d] * scales[d] * vectors[b][d] for d in range(3)) for a, b in index_pairs
-    ] + [excess, misfit]
+    ]
     for p in range(out_ref.shape[0]):
         for k, row in enumerate(rows):
             out_ref[p, pl.ds(k * tiles, tiles), :] = row
-
-
-def apply_kernel(factor_ref, cand_ref, new_ref, send_ref, sums_ref):
-    _, channels, rows, cols = cand_ref.shape
+    misfit = jnp.sum(summed(entries * tiles, held - entries * tiles), axis=0, keepdims=True)
+    excess = jnp.sum(excess, axis=0, keepdims=True)
+    for p in range(sums_ref.shape[0]):
+        sums_ref[p, pl.ds(0, 1), :] = misfit
+        sums_ref[p, pl.ds(1, 1), :] = excess
+
+
+def factor_image(factor_ref, rows, tiles):
+    per_row = factor_ref.shape[0] // rows
+
+    def image(a, b, j):
+        k = entry_of[tuple(sorted((a, b)))]
+        return factor_ref[pl.ds(k * tiles + j, rows, stride=per_row), :]
+
+    return image
+
+
+def slice_kernel(factor_ref, own_ref, cand_ref, new_ref):
+    channels, rows, cols = cand_ref.shape
     tiles = cols // LANES
-    entries = len(index_pairs)
-    per_row = factor_ref.shape[0] // rows
-
-    def image(k, j):
-        return factor_ref[pl.ds(k * tiles + j, rows, stride=per_row), :]
-
-    for k in range(2):
-        sums_ref[k] = sum(image(entries + k, j) for j in range(tiles))
+    image = factor_image(factor_ref, rows, tiles)
     for j in range(tiles):
         here = pl.ds(j * LANES, LANES)
-        factor = [image(k, j) for k in range(entries)]
+        factor = [image(b, 2, j) for b in range(3)]
         for c in range(channels):
-            cand = [cand_ref[a, c, :, here] for a in range(3)]
-            for a in (2, 1, 0):
-                new = sum(cand[b] * factor[entry_of[tuple(sorted((b, a)))]] for b in range(3))
-                new_ref[a, c, :, here] = new
-                if a == 2:
-                    send_ref[c, :, here] = new
-
-
-def backward_difference(component, along_axis):
-    length = component.shape[along_axis]
-    kept_part = lax.slice_in_dim(component, 0, length - 1, axis=along_axis)
-    zero_layer = jnp.zeros_like(lax.slice_in_dim(component, 0, 1, axis=along_axis))
-    masked = jnp.concatenate([kept_part, zero_layer], axis=along_axis)
-    earlier = jnp.concatenate([zero_layer, kept_part], axis=along_axis)
-    return masked - earlier
+            new_ref[c, :, here] = (
+                own_ref[0, c, :, here] * factor[0]
+                + own_ref[1, c, :, here] * factor[1]
+                + cand_ref[c, :, here] * factor[2]
+            )
+
+
+def rest_kernel(
+    rate_ref, keep_ref, factor_ref, own_ref, cand_ref, slice_ref, volume_ref, back_ref, new_ref, ready_ref
+):
+    channels, rows, cols = cand_ref.shape
+    tiles = cols // LANES
+    rate = rate_ref[0]
+    keep = keep_ref[0]
+    image = factor_image(factor_ref, rows, tiles)
+    row_id = lax.broadcasted_iota(jnp.int32, (rows, LANES), 0)
+    lane_id = lax.broadcasted_iota(jnp.int32, (rows, LANES), 1)
+    before = [None] * channels
+    for j in range(tiles):
+        here = pl.ds(j * LANES, LANES)
+        factor = [[image(b, a, j) for b in range(3)] for a in range(2)]
+        for c in range(channels):
+            cand = [own_ref[0, c, :, here], own_ref[1, c, :, here], cand_ref[c, :, here]]
+            new = [sum(cand[b] * factor[a][b] for b in range(3)) for a in range(2)]
+            along = slice_ref[c, :, here]
+            for a in range(2):
+                new_ref[a, c, :, here] = new[a]
+            new_ref[2, c, :, here] = along
+            kept = jnp.where(row_id < rows - 1, new[0], 0.0)
+            spread = kept - jnp.where(row_id > 0, pltpu.roll(new[0], 1, 0), 0.0)
+            left = pltpu.roll(new[1], 1, 1)
+            earlier = jnp.where(lane_id > 0, left, 0.0 if j == 0 else before[c])
+            before[c] = left
+            kept = new[1] if j + 1 < tiles else jnp.where(lane_id < LANES - 1, new[1], 0.0)
+            spread = spread + (kept - earlier) + keep * along
+            ready_ref[c, :, here] = volume_ref[c, :, here] - rate * (back_ref[c, :, here] - spread)
+
+
+def finish_kernel(counts, rate_ref, ready_ref, prior_ref, sums_ref, updated_ref, totals_ref):
+    rate = rate_ref[0]
+    for c in range(ready_ref.shape[0]):
+        updated_ref[c] = jnp.maximum(ready_ref[c] - rate * prior_ref[c], 0.0)
+    total = sums_ref[0]
+    for p in range(1, sums_ref.shape[0]):
+        total = total + sums_ref[p]
+    for k, count in enumerate(counts):
+        totals_ref[k] = jnp.sum(total[k : k + 1]) / count
 
 
 def picked_blocks(blocks, where, count):
@@ -190,7 +253,6 @@
 ):
     f32 = jnp.float32
     dual_rate = dual_step[0]
-    primal_rate = primal_step[0]
     channels, slices, row_count, col_count = volume_now.shape
     pixels = row_count * col_count
     rays = dual_data.shape[2]
@@ -203,23 +265,32 @@
     last_slice = lax.axis_index("slab") == slab_count - 1
     images = (channels, row_count, col_count)
 
+    keep = jnp.where(last_slice, 0.0, 1.0).reshape(1)
+    image_form = jax.ShapeDtypeStruct(images, f32)
+    x_near, dual_near = near(extrapolated.reshape(images)), near(dual_grad.reshape(3, *images))
+
     following = from_behind(extrapolated, "slab", -1)
-    keep = jnp.where(last_slice, 0.0, 1.0).reshape(1)
-    candidate, partial_gram = pl.pallas_call(
+    own, own_sums = pl.pallas_call(
+        own_kernel,
+        out_shape=(kept_near((2, *images)), kept_near((len(own_pairs), row_count, col_count))),
+        in_specs=[SMEM, VMEM, VMEM],
+        out_specs=(VMEM, VMEM),
+        name="own",
+    )(dual_step, x_near, dual_near)
+    cand, partial_gram = pl.pallas_call(
         gram_kernel,
-        out_shape=(
-            jax.ShapeDtypeStruct((3, *images), f32),
-            jax.ShapeDtypeStruct((row_count * held, LANES), f32),
-        ),
-        in_specs=[SMEM, SMEM, VMEM, VMEM, VMEM],
+        out_shape=(kept_near(images), jax.ShapeDtypeStruct((row_count * held, LANES), f32)),
+        in_specs=[SMEM, SMEM, VMEM, VMEM, VMEM, VMEM, VMEM],
         out_specs=(VMEM, VMEM),
         name="gram",
     )(
         dual_step,
         keep,
-        extrapolated.reshape(images),
-        following.reshape(images),
-        dual_grad.reshape(3, *images),
+        x_near,
+        near(following.reshape(images)),
+        dual_near,
+        near(own),
+        near(own_sums),
     )
     gram_parts = lax.all_to_all(
         partial_gram.reshape(share_count, held, LANES), SHARE, 0, 0, tiled=True
@@ -239,7 +310,7 @@
         in_specs=[VMEM, VMEM],
         out_specs=VMEM,
         name="pass_on",
-    )(gram_parts, misfit_part)
+    )(near(gram_parts), near(misfit_part))
     far_parts = lax.all_to_all(to_far, FAR, 0, 0, tiled=True)
 
     data_low = data_new.astype(jnp.bfloat16)
@@ -250,43 +321,52 @@
     )
 
     radius = reg_weight * math.sqrt(total_channels)
-    to_share = pl.pallas_call(
+    to_share, sums = pl.pallas_call(
         factor_kernel,
-        out_shape=jax.ShapeDtypeStruct((share_count, 8 * tiles, LANES), f32),
+        out_shape=(
+            jax.ShapeDtypeStruct((share_count, held, LANES), f32),
+            jax.ShapeDtypeStruct((share_count * slab_count, 2, LANES), f32),
+        ),
         in_specs=[SMEM, VMEM],
+        out_specs=(VMEM, VMEM),
+        name="factor",
+    )(radius, near(far_parts))
+    factor_rows = lax.all_to_all(to_share, SHARE, 0, 0, tiled=True)
+    all_sums = lax.all_to_all(sums, (*SHARE, "slab"), 0, 0, tiled=True)
+    factor_near = near(factor_rows.reshape(share_count * held, LANES))
+
+    new_slice = pl.pallas_call(
+        slice_kernel,
+        out_shape=kept_near(images),
+        in_specs=[VMEM, VMEM, VMEM],
         out_specs=VMEM,
-        name="factor",
-    )(radius, far_parts)
-    factor_rows = lax.all_to_all(to_share, SHARE, 0, 0, tiled=True)
-
-    grad_new, to_next, sums = pl.pallas_call(
-        apply_kernel,
-        out_shape=(
-            jax.ShapeDtypeStruct((3, *images), f32),
-            jax.ShapeDtypeStruct(images, f32),
-            jax.ShapeDtypeStruct((2, row_count, LANES), f32),
-        ),
-        in_specs=[VMEM, VMEM],
-        out_specs=(VMEM, VMEM, VMEM),
-        name="apply",
-    )(factor_rows.reshape(share_count * 8 * tiles, LANES), candidate)
-    prior_layer = from_behind(to_next, "slab", 1)
-
-    sums = jnp.broadcast_to(sums.sum(axis=(1, 2))[None, :, None], (slab_count, 2, LANES))
-    combined = lax.all_to_all(sums, "slab", 0, 0, tiled=True)[:, :, 0].sum(axis=0)
-
-    masked = jnp.where(last_slice, 0.0, to_next)
-    ready = volume_now.reshape(images) - primal_rate * (
-        back_proj.reshape(images)
-        - (backward_difference(grad_new[0], 1) + backward_difference(grad_new[1], 2) + masked)
-    )
-    updated = jnp.maximum(ready - primal_rate * prior_layer, 0.0)
-    totals = jnp.stack(
-        [
-            combined[1] / (total_channels * slab_count * slices * rays),
-            combined[0] / (slab_count * slices * pixels),
-        ]
-    )
+        name="slice",
+    )(factor_near, near(own), near(cand))
+    prior_layer = from_behind(new_slice, "slab", 1)
+    grad_new, ready = pl.pallas_call(
+        rest_kernel,
+        out_shape=(jax.ShapeDtypeStruct((3, *images), f32), kept_near(images)),
+        in_specs=[SMEM, SMEM] + [VMEM] * 6,
+        out_specs=(VMEM, VMEM),
+        name="rest",
+    )(
+        primal_step,
+        keep,
+        factor_near,
+        near(own),
+        near(cand),
+        near(new_slice),
+        near(volume_now.reshape(images)),
+        near(back_proj.reshape(images)),
+    )
+    counts = (total_channels * slab_count * slices * rays, slab_count * slices * pixels)
+    updated, totals = pl.pallas_call(
+        functools.partial(finish_kernel, counts),
+        out_shape=(image_form, jax.ShapeDtypeStruct((2,), f32)),
+        in_specs=[SMEM, VMEM, VMEM, VMEM],
+        out_specs=(VMEM, SMEM),
+        name="finish",
+    )(primal_step, near(ready), near(prior_layer), near(all_sums))
     return (
         updated.reshape(volume_now.shape),
         grad_new.reshape(dual_grad.shape),

time: 92 us -> 81.9 us (0.89)
  other arithmetic: 5.19 us -> 1.01 us
  Pallas kernels: 8.64 us -> 4.84 us
  matrix products: 2.83 us -> 5.99 us
  local copies, waits for them, and re-layouts: 5.23 us -> 2.24 us
  starting transfers between devices: 42.6 us -> 40.5 us
  between operations: 4.09 us -> 2.82 us
  waiting for transfers between devices: 22.7 us -> 23.8 us
    pallas_call x3 -> x6, Pallas kernels: 7.04 us -> 4.17 us  [the longest x1 1.17 us: on_device(): pl.pallas_call(factor_kernel, out_shape=(jax.ShapeDtypeStruct((share_coun...]
    all_to_all x1, starting transfers between devices: 3.24 us -> 5.64 us  [on_device(): all_sums = lax.all_to_all(sums, (*SHARE, 'slab'), 0, 0, tiled=True)]
    all_to_all x1, waiting for transfers between devices: 12 us -> 14.4 us  [on_device(): far_parts = lax.all_to_all(to_far, FAR, 0, 0, tiled=True)]
    all_to_all x1, starting transfers between devices: 6.19 us -> 3.87 us  [on_device(): lax.all_to_all(partial_gram.reshape(share_count, held, LANES), SHARE, 0,...]
    unnamed x1 -> x0, other arithmetic: 2.07 us -> none
    all_to_all x1, waiting for transfers between devices: 2.05 us -> 0.01 us  [on_device(): all_sums = lax.all_to_all(sums, (*SHARE, 'slab'), 0, 0, tiled=True)]
    ppermute x2, starting transfers between devices: 15.7 us -> 13.8 us  [from_behind(): return lax.ppermute(block, axis, route)]
    dot_general x1, matrix products: 0.65 us -> 2.23 us  [on_device(): jnp.einsum('tij,tbi->tbj', projector, picked_back, preferred_element_type...]
  transfers between devices with their start and end apart: 6 -> 6, of which waited for: 4 -> 3; matrix products, arithmetic and copies ran while one was open for 9% -> 9% of each run, Pallas kernels for 0% -> 2%
where the time goes in v2:
time: 81.9 us; the launch traced here: 81.2 us
  starting transfers between devices  40.5 us (49%)
  waiting for transfers between devices  23.8 us (29%)
  matrix products  5.99 us (7%)
  Pallas kernels  4.84 us (6%)
  between operations  2.82 us (3%)
  local copies, waits for them, and re-layouts  2.24 us (3%)
  other arithmetic  1.01 us (1%)
    all_to_all x1, waiting for transfers between devices, on_device(): far_parts = lax.all_to_all(to_far, FAR, 0, 0, tiled=True)  14.4 us
    ppermute x2, starting transfers between devices, from_behind(): return lax.ppermute(block, axis, route)  13.8 us
    all_to_all x1, starting transfers between devices, on_device(): far_parts = lax.all_to_all(to_far, FAR, 0, 0, tiled=True)  13.6 us
    all_to_all x1, waiting for transfers between devices, on_device(): factor_rows = lax.all_to_all(to_share, SHARE, 0, 0, tiled=True)  6.26 us
    all_to_all x1, starting transfers between devices, on_device(): all_sums = lax.all_to_all(sums, (*SHARE, 'slab'), 0, 0, tiled=True)  5.64 us
    all_to_all x1, starting transfers between devices, on_device(): lax.all_to_all(partial_gram.reshape(share_count, held, LANES), SHARE, 0,...  3.87 us
    all_to_all x1, starting transfers between devices, on_device(): factor_rows = lax.all_to_all(to_share, SHARE, 0, 0, tiled=True)  3.52 us
    all_to_all x1, waiting for transfers between devices, on_device(): lax.all_to_all(partial_gram.reshape(share_count, held, LANES), SHARE, 0,...  3.2 us
  transfers between devices with their start and end apart: 6, of which 3 were waited for; matrix products, arithmetic and copies ran while one was open for 9% of the time, Pallas kernels for 2%

profile of v2, /device:TPU:1, one launch (start us, length us, event | category | flops | bytes accessed | tf_op | source)
XLA Modules:
  0.0 81.2 jit_solution(12971433388796551384)
XLA Ops:
  0.6 0.0 copy-start.6
  0.6 8.8 %collective-permute-start = (f32[8,1,16,512]{3,2,0,1:T(8,128)}, f32[8,1,16,512]{3,2,0,1:T(8,128)S(1)}, u32[]{:S(2)}, u32[]{:S(2)}) collective-permute-start(f32[8,1,16,512]{3,2,0,1:T(8,128)} %bitcast.44), channel_id=1, source_target_pairs={{1,0},{2,1},{3,2},{5,4},{6,5},{7,6},{9,8},{10,9},{11,10},{13,12},{... | collective-permute-start | bytes 786440 | tf_op jit(solution)/shard_map/ppermute | solution.py:38
  9.4 1.0 %convert_element_type.19 = bf16[8,1,16,512]{3,2,1,0:T(8,128)(2,1)S(1)} convert(f32[8,1,16,512]{3,2,1,0:T(8,128)} %param.12) | non-fusion elementwise | flops 65536 | bytes 393216 | tf_op jit(solution)/shard_map/convert_element_type | solution.py:299
  11.1 0.1 convert_element_type.20
  11.2 0.0 copy-start
  11.2 1.1 %copy-done = f32[3,8,1,16,512]{4,3,2,1,0:T(8,128)S(1)} copy-done((f32[3,8,1,16,512]{4,3,2,1,0:T(8,128)S(1)}, f32[3,8,1,16,512]{4,3,2,1,0:T(8,128)}, u32[]{:S(2)}) %copy-start) | copy-done | bytes 786456
  12.3 0.0 copy-start.1
  12.3 0.9 %copy-done.1 = f32[8,1,16,512]{3,2,1,0:T(8,128)S(1)} copy-done((f32[8,1,16,512]{3,2,1,0:T(8,128)S(1)}, f32[8,1,16,512]{3,2,1,0:T(8,128)}, u32[]{:S(2)}) %copy-start.1) | copy-done | bytes 262168
  13.3 0.2 own.1
  13.4 0.0 collective-permute-done
  13.5 0.0 copy-start.4
  13.5 0.0 copy-start.5
  13.5 0.0 copy-start.7
  13.5 0.8 %gram.1 = (f32[8,16,512]{2,1,0:T(8,128)S(1)}, f32[384,128]{1,0:T(8,128)}) custom-call(f32[1]{0:T(128)} %copy.33.rate_ref, f32[1]{0:T(128)} %bitcast.keep_ref, f32[8,16,512]{2,1,0:T(8,128)S(1)} %bitcast.46, f32[8,16,512]{2,1,0:T(8,128)S(1)} %bitcast.49, f32[3,8,16,512]{3,2,1,0:T(8,128)S(1)} %bitcast.43, f32[2,8,16,512]{3,2,1,0:T(8,128)S(1)} %get-tuple-element.14.own_ref, ...), custom_call_target="tpu_custom_call" | custom-call | tf_op jit(solution)/shard_map/gram/pallas_call | solution.py:280
  14.3 3.9 %all-to-all-start = ((f32[16,24,128]{2,1,0:T(8,128)}), f32[16,24,128]{2,1,0:T(8,128)S(1)}, u32[]{:S(2)}, u32[]{:S(2)}) async-start(f32[16,24,128]{2,1,0:T(8,128)} %bitcast.53), calls=%async_computation | async-start | bytes 393216 | tf_op jit(solution)/shard_map/all_to_all | solution.py:295
  18.2 0.0 copy-done.6
  18.2 0.2 fusion.9
  18.5 2.8 %fusion.3 = f32[64,8,128]{2,1,0:T(8,128)S(1)} fusion(bf16[64,128,128]{2,1,0:T(8,128)(2,1)} %param.16, bf16[64,8,128]{2,0,1:T(8,128)(2,1)S(1)} %fusion.9), kind=kOutput, calls=%fused_computation.7 | convolution fusion | flops 16777216 | bytes 2490368 | tf_op jit(solution)/shard_map/tij,tbj->tbi/dot_general | solution.py:301
  21.2 0.0 copy-done.4
  21.2 0.0 copy-done.5
  21.2 0.0 copy-done.7
  21.3 0.3 add_divide_fusion
  21.5 0.0 copy-start.3
  21.6 3.2 %all-to-all-done.parts_ref = f32[16,24,128]{2,1,0:T(8,128)S(1)} async-done(((f32[16,24,128]{2,1,0:T(8,128)}), f32[16,24,128]{2,1,0:T(8,128)S(1)}, u32[]{:S(2)}, u32[]{:S(2)}) %all-to-all-start) | async-done | bytes 196640 | tf_op jit(solution)/shard_map/all_to_all | solution.py:295
  24.8 0.7 pass_on.1
  25.5 13.6 %all-to-all-start.1 = ((f32[8,32,128]{2,1,0:T(8,128)}), f32[8,32,128]{2,1,0:T(8,128)S(1)}, u32[]{:S(2)}, u32[]{:S(2)}) async-start(f32[8,32,128]{2,1,0:T(8,128)} %pass_on.1), calls=%async_computation.1 | async-start | bytes 262144 | tf_op jit(solution)/shard_map/all_to_all | solution.py:314
  39.7 14.4 %all-to-all-done.1.parts_ref = f32[8,32,128]{2,1,0:T(8,128)S(1)} async-done(((f32[8,32,128]{2,1,0:T(8,128)}), f32[8,32,128]{2,1,0:T(8,128)S(1)}, u32[]{:S(2)}, u32[]{:S(2)}) %all-to-all-start.1) | async-done | bytes 131104 | tf_op jit(solution)/shard_map/all_to_all | solution.py:314
  54.1 1.2 %factor.1 = (f32[16,24,128]{2,1,0:T(8,128)}, f32[64,2,128]{2,1,0:T(2,128)}) custom-call(f32[1]{0:T(128)S(6)} %mul.12.radius_ref, f32[8,32,128]{2,1,0:T(8,128)S(1)} %all-to-all-done.1.parts_ref), custom_call_target="tpu_custom_call" | custom-call | tf_op jit(solution)/shard_map/factor/pallas_call | solution.py:324
  55.2 3.5 %all-to-all-start.2 = ((f32[16,24,128]{2,1,0:T(8,128)}), f32[16,24,128]{2,1,0:T(8,128)S(1)}, u32[]{:S(2)}, u32[]{:S(2)}) async-start(f32[16,24,128]{2,1,0:T(8,128)} %get-tuple-element.17), calls=%async_computation.2 | async-start | bytes 393216 | tf_op jit(solution)/shard_map/all_to_all | solution.py:334
  58.8 0.2 fusion.5
  59.0 6.3 %all-to-all-done.2 = f32[16,24,128]{2,1,0:T(8,128)S(1)} async-done(((f32[16,24,128]{2,1,0:T(8,128)}), f32[16,24,128]{2,1,0:T(8,128)S(1)}, u32[]{:S(2)}, u32[]{:S(2)}) %all-to-all-start.2) | async-done | bytes 196640 | tf_op jit(solution)/shard_map/all_to_all | solution.py:334
  65.3 5.6 %all-to-all-start.3 = ((f32[64,2,128]{2,1,0:T(2,128)}), f32[64,2,128]{2,1,0:T(2,128)S(1)}, u32[]{:S(2)}, u32[]{:S(2)}) async-start(f32[64,2,128]{2,1,0:T(2,128)} %get-tuple-element.20), calls=%async_computation.3 | async-start | bytes 131072 | tf_op jit(solution)/shard_map/all_to_all | solution.py:335
  70.9 0.0 copy-start.2
  70.9 0.1 slice.1.slice_ref
  71.0 5.0 %collective-permute-start.1 = (f32[8,16,512]{2,1,0:T(8,128)S(1)}, f32[8,16,512]{2,1,0:T(8,128)S(1)}, u32[]{:S(2)}, u32[]{:S(2)}) collective-permute-start(f32[8,16,512]{2,1,0:T(8,128)S(1)} %slice.1.slice_ref), channel_id=1, source_target_pairs={{0,1},{1,2},{2,3},{4,5},{5,6},{6,7},{8,9},{9,10},{10,11},{12,13},{... | collective-permute-start | bytes 786440 | tf_op jit(solution)/shard_map/ppermute | solution.py:38
  76.1 2.2 %fusion.4 = f32[64,8,128]{2,1,0:T(8,128)S(1)} fusion(bf16[64,128,128]{2,1,0:T(8,128)(2,1)} %param.16, bf16[64,8,128]{2,0,1:T(8,128)(2,1)S(1)} %fusion.5), kind=kOutput, calls=%fused_computation.8 | convolution fusion | flops 16777216 | bytes 2490368 | tf_op jit(solution)/shard_map/tij,tbi->tbj/dot_general | solution.py:318
  78.3 0.0 copy-done.3
  79.0 0.3 convolution_bitcast_fusion
  79.3 0.0 copy-done.2
  79.3 1.1 %rest.1 = (f32[3,8,16,512]{3,2,1,0:T(8,128)}, f32[8,16,512]{2,1,0:T(8,128)S(1)}) custom-call(f32[1]{0:T(128)S(6)} %copy.34.rate_ref, f32[1]{0:T(128)} %bitcast.keep_ref, f32[384,128]{1,0:T(8,128)S(1)} %bitcast.48, f32[2,8,16,512]{3,2,1,0:T(8,128)S(1)} %get-tuple-element.14.own_ref, f32[8,16,512]{2,1,0:T(8,128)S(1)} %get-tuple-element.18.cand_ref, ...), custom_call_target="tpu_custom_call" | custom-call | tf_op jit(solution)/shard_map/rest/pallas_call | solution.py:346
  80.4 0.0 all-to-all-done.3.sums_ref
  80.4 0.0 collective-permute-done.1.prior_ref
  80.4 0.8 finish.1
  (2 shorter events, 0.1 us)
Async XLA Ops:
  0.6 17.6 %copy-start.6 = (s32[64]{0:T(128)S(1)}, s32[64]{0:T(128)}, u32[]{:S(2)}) copy-start(s32[64]{0:T(128)} %param.18) | copy-start | bytes 772
  0.6 12.8 %collective-permute-start = (f32[8,1,16,512]{3,2,0,1:T(8,128)}, f32[8,1,16,512]{3,2,0,1:T(8,128)S(1)}, u32[]{:S(2)}, u32[]{:S(2)}) collective-permute-start(f32[8,1,16,512]{3,2,0,1:T(8,128)} %bitcast.44), channel_id=1, source_target_pairs={{1,0},{2,1},{3,2},{5,4},{6,5},{7,6},{9,8},{10,9},{11,10},{13,12},{... | collective-permute-start | bytes 786440 | tf_op jit(solution)/shard_map/ppermute | solution.py:38
  11.2 1.1 %copy-start = (f32[3,8,1,16,512]{4,3,2,1,0:T(8,128)S(1)}, f32[3,8,1,16,512]{4,3,2,1,0:T(8,128)}, u32[]{:S(2)}) copy-start(f32[3,8,1,16,512]{4,3,2,1,0:T(8,128)} %param.13) | copy-start | bytes 2359300
  12.3 0.9 %copy-start.1 = (f32[8,1,16,512]{3,2,1,0:T(8,128)S(1)}, f32[8,1,16,512]{3,2,1,0:T(8,128)}, u32[]{:S(2)}) copy-start(f32[8,1,16,512]{3,2,1,0:T(8,128)} %param.12) | copy-start | bytes 786436
  13.5 7.8 %copy-start.4 = (f32[8,1,4096]{2,1,0:T(1,128)S(1)}, f32[8,1,4096]{2,1,0:T(1,128)}, u32[]{:S(2)}) copy-start(f32[8,1,4096]{2,1,0:T(1,128)} %param.14) | copy-start | bytes 393220
  13.5 7.8 %copy-start.5 = (f32[8,1,4096]{2,1,0:T(1,128)S(1)}, f32[8,1,4096]{2,1,0:T(1,128)}, u32[]{:S(2)}) copy-start(f32[8,1,4096]{2,1,0:T(1,128)} %param.15) | copy-start | bytes 393220
  13.5 7.7 %copy-start.7 = (s32[64]{0:T(128)S(1)}, s32[64]{0:T(128)}, u32[]{:S(2)}) copy-start(s32[64]{0:T(128)} %param.17) | copy-start | bytes 772
  14.3 10.4 %all-to-all-start = ((f32[16,24,128]{2,1,0:T(8,128)}), f32[16,24,128]{2,1,0:T(8,128)S(1)}, u32[]{:S(2)}, u32[]{:S(2)}) async-start(f32[16,24,128]{2,1,0:T(8,128)} %bitcast.53), calls=%async_computation | async-start | bytes 393216 | tf_op jit(solution)/shard_map/all_to_all | solution.py:295
  21.5 56.8 %copy-start.3 = (f32[8,32,128]{2,1,0:T(8,128)}, f32[8,32,128]{2,1,0:T(8,128)S(1)}, u32[]{:S(2)}) copy-start(f32[8,32,128]{2,1,0:T(8,128)S(1)} %get-tuple-element.28) | copy-start | bytes 393220
  25.5 28.6 %all-to-all-start.1 = ((f32[8,32,128]{2,1,0:T(8,128)}), f32[8,32,128]{2,1,0:T(8,128)S(1)}, u32[]{:S(2)}, u32[]{:S(2)}) async-start(f32[8,32,128]{2,1,0:T(8,128)} %pass_on.1), calls=%async_computation.1 | async-start | bytes 262144 | tf_op jit(solution)/shard_map/all_to_all | solution.py:314
  55.2 10.0 %all-to-all-start.2 = ((f32[16,24,128]{2,1,0:T(8,128)}), f32[16,24,128]{2,1,0:T(8,128)S(1)}, u32[]{:S(2)}, u32[]{:S(2)}) async-start(f32[16,24,128]{2,1,0:T(8,128)} %get-tuple-element.17), calls=%async_computation.2 | async-start | bytes 393216 | tf_op jit(solution)/shard_map/all_to_all | solution.py:334
  65.3 15.1 %all-to-all-start.3 = ((f32[64,2,128]{2,1,0:T(2,128)}), f32[64,2,128]{2,1,0:T(2,128)S(1)}, u32[]{:S(2)}, u32[]{:S(2)}) async-start(f32[64,2,128]{2,1,0:T(2,128)} %get-tuple-element.20), calls=%async_computation.3 | async-start | bytes 131072 | tf_op jit(solution)/shard_map/all_to_all | solution.py:335
  70.9 8.4 %copy-start.2 = (f32[8,1,16,512]{3,2,1,0:T(8,128)S(1)}, f32[8,1,16,512]{3,2,1,0:T(8,128)}, u32[]{:S(2)}) copy-start(f32[8,1,16,512]{3,2,1,0:T(8,128)} %param.11) | copy-start | bytes 786436
  71.0 9.4 %collective-permute-start.1 = (f32[8,16,512]{2,1,0:T(8,128)S(1)}, f32[8,16,512]{2,1,0:T(8,128)S(1)}, u32[]{:S(2)}, u32[]{:S(2)}) collective-permute-start(f32[8,16,512]{2,1,0:T(8,128)S(1)} %slice.1.slice_ref), channel_id=1, source_target_pairs={{0,1},{1,2},{2,3},{4,5},{5,6},{6,7},{8,9},{9,10},{10,11},{12,13},{... | collective-permute-start | bytes 786440 | tf_op jit(solution)/shard_map/ppermute | solution.py:38

commit v3 on v2

--- a/solution.py
+++ b/solution.py
@@ -22,6 +22,7 @@
 
 VMEM = pl.BlockSpec(memory_space=pltpu.VMEM)
 SMEM = pl.BlockSpec(memory_space=pltpu.SMEM)
+ANY = pl.BlockSpec(memory_space=pl.ANY)
 
 
 def near(array):
@@ -38,33 +39,59 @@
     return lax.ppermute(block, axis, route)
 
 
-def own_kernel(rate_ref, x_ref, dual_ref, cand_ref, sums_ref):
+def own_kernel(rate_ref, x_far, dual_far, x_ref, cand_ref, sums_ref, arrived):
     channels, rows, cols = x_ref.shape
     tiles = cols // LANES
+    parts = arrived.shape[1]
+    size = channels // parts
+    copies = []
+    for part in range(parts):
+        some = pl.ds(part * size, size)
+        copies.append(
+            (
+                pltpu.make_async_copy(x_far.at[some], x_ref.at[some], arrived.at[0, part]),
+                pltpu.make_async_copy(
+                    dual_far.at[:, some], cand_ref.at[:, some], arrived.at[1, part]
+                ),
+            )
+        )
+        for copy in copies[-1]:
+            copy.start()
     rate = rate_ref[0]
     inner_row = lax.broadcasted_iota(jnp.int32, (rows, LANES), 0) < rows - 1
     edge_lane = lax.broadcasted_iota(jnp.int32, (rows, LANES), 1) == LANES - 1
-    for j in range(tiles):
-        here = pl.ds(j * LANES, LANES)
-        sums = [jnp.zeros((rows, LANES), jnp.float32) for _ in own_pairs]
-        for c in range(channels):
-            x = x_ref[c, :, here]
-            below = pltpu.roll(x, rows - 1, 0)
-            right = pltpu.roll(x, LANES - 1, 1)
-            if j + 1 < tiles:
-                after = pltpu.roll(x_ref[c, :, pl.ds((j + 1) * LANES, LANES)], LANES - 1, 1)
+    for part in range(parts):
+        for copy in copies[part]:
+            copy.wait()
+        for j in range(tiles):
+            here = pl.ds(j * LANES, LANES)
+            if part:
+                sums = [sums_ref[k, :, here] for k in range(len(own_pairs))]
             else:
-                after = x
-            steps = (jnp.where(inner_row, below - x, 0.0), jnp.where(edge_lane, after, right) - x)
-            cand = [dual_ref[a, c, :, here] + rate * steps[a] for a in range(2)]
-            for a in range(2):
-                cand_ref[a, c, :, here] = cand[a]
-            sums = [s + cand[a] * cand[b] for s, (a, b) in zip(sums, own_pairs)]
-        for k, s in enumerate(sums):
-            sums_ref[k, :, here] = s
-
-
-def gram_kernel(rate_ref, keep_ref, x_ref, next_ref, dual_ref, own_ref, sums_ref, cand_ref, out_ref):
+                sums = [jnp.zeros((rows, LANES), jnp.float32) for _ in own_pairs]
+            for c in range(part * size, part * size + size):
+                x = x_ref[c, :, here]
+                below = pltpu.roll(x, rows - 1, 0)
+                right = pltpu.roll(x, LANES - 1, 1)
+                if j + 1 < tiles:
+                    after = pltpu.roll(x_ref[c, :, pl.ds((j + 1) * LANES, LANES)], LANES - 1, 1)
+                else:
+                    after = x
+                steps = (
+                    jnp.where(inner_row, below - x, 0.0),
+                    jnp.where(edge_lane, after, right) - x,
+                )
+                cand = [cand_ref[a, c, :, here] + rate * steps[a] for a in range(2)]
+                for a in range(2):
+                    cand_ref[a, c, :, here] = cand[a]
+                sums = [s + cand[a] * cand[b] for s, (a, b) in zip(sums, own_pairs)]
+            for k, s in enumerate(sums):
+                sums_ref[k, :, here] = s
+
+
+def gram_kernel(
+    rate_ref, keep_ref, next_ref, sums_ref, x_ref, dual_ref, x_same, cand_ref, out_ref
+):
     channels, rows, cols = x_ref.shape
     tiles = cols // LANES
     per_row = len(index_pairs) * tiles
@@ -78,15 +105,15 @@
         for c in range(channels):
             step = (next_ref[c, :, here] - x_ref[c, :, here]) * keep
             cand = dual_ref[2, c, :, here] + rate * step
-            cand_ref[c, :, here] = cand
             for b in range(2):
-                sums[b, 2] = sums[b, 2] + own_ref[b, c, :, here] * cand
+                sums[b, 2] = sums[b, 2] + dual_ref[b, c, :, here] * cand
             sums[2, 2] = sums[2, 2] + cand * cand
+            cand_ref[2, c, :, here] = cand
         for k, pair in enumerate(index_pairs):
             out_ref[pl.ds(k * tiles + j, rows, stride=per_row), :] = sums[pair]
 
 
-def pass_on_kernel(parts_ref, misfit_ref, out_ref):
+def pass_on_kernel(parts_ref, misfit_ref, data_ref, out_ref, data_same):
     peers, per_row, _ = parts_ref.shape
     total = parts_ref[0]
     for p in range(1, peers):
@@ -125,10 +152,10 @@
     return entry, vectors
 
 
-def factor_kernel(radius_ref, parts_ref, out_ref, sums_ref):
+def factor_kernel(radius_ref, parts_ref, back_ref, out_ref, back_same):
     peers, held, _ = parts_ref.shape
     entries = len(index_pairs)
-    tiles = out_ref.shape[1] // entries
+    tiles = out_ref.shape[1] // (entries + 2)
 
     def summed(start, size):
         total = parts_ref[0, pl.ds(start, size), :]
@@ -146,60 +173,69 @@
     roots = [jnp.sqrt(jnp.maximum(entry[d], 0.0)) for d in range(3)]
     scales = [radius / jnp.maximum(root, radius) for root in roots]
     excess = sum(jnp.maximum(root - radius, 0.0) for root in roots) / radius
+    misfit = sum(summed(k, tiles) for k in range(entries * tiles, held, tiles))
     rows = [
         sum(vectors[a][d] * scales[d] * vectors[b][d] for d in range(3)) for a, b in index_pairs
-    ]
+    ] + [misfit, excess]
     for p in range(out_ref.shape[0]):
         for k, row in enumerate(rows):
             out_ref[p, pl.ds(k * tiles, tiles), :] = row
-    misfit = jnp.sum(summed(entries * tiles, held - entries * tiles), axis=0, keepdims=True)
-    excess = jnp.sum(excess, axis=0, keepdims=True)
-    for p in range(sums_ref.shape[0]):
-        sums_ref[p, pl.ds(0, 1), :] = misfit
-        sums_ref[p, pl.ds(1, 1), :] = excess
 
 
 def factor_image(factor_ref, rows, tiles):
     per_row = factor_ref.shape[0] // rows
 
-    def image(a, b, j):
-        k = entry_of[tuple(sorted((a, b)))]
+    def image(k, j):
         return factor_ref[pl.ds(k * tiles + j, rows, stride=per_row), :]
 
     return image
 
 
-def slice_kernel(factor_ref, own_ref, cand_ref, new_ref):
-    channels, rows, cols = cand_ref.shape
+def entry_at(a, b):
+    return entry_of[tuple(sorted((a, b)))]
+
+
+def slice_kernel(factor_ref, cand_ref, new_ref):
+    _, channels, rows, cols = cand_ref.shape
     tiles = cols // LANES
     image = factor_image(factor_ref, rows, tiles)
     for j in range(tiles):
         here = pl.ds(j * LANES, LANES)
-        factor = [image(b, 2, j) for b in range(3)]
+        factor = [image(entry_at(b, 2), j) for b in range(3)]
         for c in range(channels):
-            new_ref[c, :, here] = (
-                own_ref[0, c, :, here] * factor[0]
-                + own_ref[1, c, :, here] * factor[1]
-                + cand_ref[c, :, here] * factor[2]
-            )
+            new_ref[c, :, here] = sum(cand_ref[b, c, :, here] * factor[b] for b in range(3))
 
 
 def rest_kernel(
-    rate_ref, keep_ref, factor_ref, own_ref, cand_ref, slice_ref, volume_ref, back_ref, new_ref, ready_ref
+    rate_ref,
+    keep_ref,
+    factor_ref,
+    cand_ref,
+    slice_ref,
+    volume_ref,
+    back_ref,
+    new_ref,
+    ready_ref,
+    sums_ref,
 ):
-    channels, rows, cols = cand_ref.shape
+    _, channels, rows, cols = cand_ref.shape
     tiles = cols // LANES
     rate = rate_ref[0]
     keep = keep_ref[0]
     image = factor_image(factor_ref, rows, tiles)
+    for k in range(2):
+        total = sum(image(len(index_pairs) + k, j) for j in range(tiles))
+        total = jnp.sum(total, axis=0, keepdims=True)
+        for p in range(sums_ref.shape[0]):
+            sums_ref[p, pl.ds(k, 1), :] = total
     row_id = lax.broadcasted_iota(jnp.int32, (rows, LANES), 0)
     lane_id = lax.broadcasted_iota(jnp.int32, (rows, LANES), 1)
     before = [None] * channels
     for j in range(tiles):
         here = pl.ds(j * LANES, LANES)
-        factor = [[image(b, a, j) for b in range(3)] for a in range(2)]
+        factor = [[image(entry_at(b, a), j) for b in range(3)] for a in range(2)]
         for c in range(channels):
-            cand = [own_ref[0, c, :, here], own_ref[1, c, :, here], cand_ref[c, :, here]]
+            cand = [cand_ref[b, c, :, here] for b in range(3)]
             new = [sum(cand[b] * factor[a][b] for b in range(3)) for a in range(2)]
             along = slice_ref[c, :, here]
             for a in range(2):
@@ -267,36 +303,44 @@
 
     keep = jnp.where(last_slice, 0.0, 1.0).reshape(1)
     image_form = jax.ShapeDtypeStruct(images, f32)
-    x_near, dual_near = near(extrapolated.reshape(images)), near(dual_grad.reshape(3, *images))
 
     following = from_behind(extrapolated, "slab", -1)
-    own, own_sums = pl.pallas_call(
+    x_near, duals, own_sums = pl.pallas_call(
         own_kernel,
-        out_shape=(kept_near((2, *images)), kept_near((len(own_pairs), row_count, col_count))),
-        in_specs=[SMEM, VMEM, VMEM],
-        out_specs=(VMEM, VMEM),
+        out_shape=(
+            kept_near(images),
+            kept_near((3, *images)),
+            kept_near((len(own_pairs), row_count, col_count)),
+        ),
+        in_specs=[SMEM, ANY, ANY],
+        out_specs=(VMEM, VMEM, VMEM),
+        scratch_shapes=[pltpu.SemaphoreType.DMA((2, 4))],
         name="own",
-    )(dual_step, x_near, dual_near)
-    cand, partial_gram = pl.pallas_call(
+    )(dual_step, extrapolated.reshape(images), dual_grad.reshape(3, *images))
+    x_near, candidate, partial_gram = pl.pallas_call(
         gram_kernel,
-        out_shape=(kept_near(images), jax.ShapeDtypeStruct((row_count * held, LANES), f32)),
-        in_specs=[SMEM, SMEM, VMEM, VMEM, VMEM, VMEM, VMEM],
-        out_specs=(VMEM, VMEM),
+        out_shape=(
+            kept_near(images),
+            kept_near((3, *images)),
+            jax.ShapeDtypeStruct((row_count * held, LANES), f32),
+        ),
+        in_specs=[SMEM, SMEM, VMEM, VMEM, VMEM, VMEM],
+        out_specs=(VMEM, VMEM, VMEM),
+        input_output_aliases={4: 0, 5: 1},
         name="gram",
     )(
         dual_step,
         keep,
-        x_near,
         near(following.reshape(images)),
-        dual_near,
-        near(own),
         near(own_sums),
+        near(x_near),
+        near(duals),
     )
     gram_parts = lax.all_to_all(
         partial_gram.reshape(share_count, held, LANES), SHARE, 0, 0, tiled=True
     )
 
-    rounded = extrapolated.reshape(channels, pixels // edge, edge).astype(jnp.bfloat16)
+    rounded = x_near.reshape(channels, pixels // edge, edge).astype(jnp.bfloat16)
     picked = picked_blocks(rounded, tile_cols, pixels // edge)
     products = jnp.einsum("tij,tbj->tbi", projector, picked, preferred_element_type=f32)
     projected = gathered_products(products, tile_rows, rays // edge)
@@ -304,13 +348,17 @@
     data_new = (dual_data.reshape(projected.shape) + dual_rate * residual) / (1.0 + dual_rate)
     misfit_part = jnp.sum((residual * residual).reshape(-1, 8, LANES), axis=0)
 
-    to_far = pl.pallas_call(
+    to_far, data_new = pl.pallas_call(
         pass_on_kernel,
-        out_shape=jax.ShapeDtypeStruct((far_count, held + 8, LANES), f32),
-        in_specs=[VMEM, VMEM],
-        out_specs=VMEM,
+        out_shape=(
+            jax.ShapeDtypeStruct((far_count, held + 8, LANES), f32),
+            kept_near(data_new.shape),
+        ),
+        in_specs=[VMEM, VMEM, VMEM],
+        out_specs=(VMEM, VMEM),
+        input_output_aliases={2: 1},
         name="pass_on",
-    )(near(gram_parts), near(misfit_part))
+    )(near(gram_parts), near(misfit_part), near(data_new))
     far_parts = lax.all_to_all(to_far, FAR, 0, 0, tiled=True)
 
     data_low = data_new.astype(jnp.bfloat16)
@@ -321,44 +369,48 @@
     )
 
     radius = reg_weight * math.sqrt(total_channels)
-    to_share, sums = pl.pallas_call(
+    to_share, back_proj = pl.pallas_call(
         factor_kernel,
         out_shape=(
-            jax.ShapeDtypeStruct((share_count, held, LANES), f32),
-            jax.ShapeDtypeStruct((share_count * slab_count, 2, LANES), f32),
-        ),
-        in_specs=[SMEM, VMEM],
+            jax.ShapeDtypeStruct((share_count, held + 2 * tiles, LANES), f32),
+            kept_near(images),
+        ),
+        in_specs=[SMEM, VMEM, VMEM],
         out_specs=(VMEM, VMEM),
+        input_output_aliases={2: 1},
         name="factor",
-    )(radius, near(far_parts))
+    )(radius, near(far_parts), near(back_proj.reshape(images)))
     factor_rows = lax.all_to_all(to_share, SHARE, 0, 0, tiled=True)
-    all_sums = lax.all_to_all(sums, (*SHARE, "slab"), 0, 0, tiled=True)
-    factor_near = near(factor_rows.reshape(share_count * held, LANES))
+    factor_near = near(factor_rows.reshape(-1, LANES))
 
     new_slice = pl.pallas_call(
         slice_kernel,
         out_shape=kept_near(images),
-        in_specs=[VMEM, VMEM, VMEM],
+        in_specs=[VMEM, VMEM],
         out_specs=VMEM,
         name="slice",
-    )(factor_near, near(own), near(cand))
+    )(factor_near, near(candidate))
     prior_layer = from_behind(new_slice, "slab", 1)
-    grad_new, ready = pl.pallas_call(
+    grad_new, ready, sums = pl.pallas_call(
         rest_kernel,
-        out_shape=(jax.ShapeDtypeStruct((3, *images), f32), kept_near(images)),
-        in_specs=[SMEM, SMEM] + [VMEM] * 6,
-        out_specs=(VMEM, VMEM),
+        out_shape=(
+            jax.ShapeDtypeStruct((3, *images), f32),
+            kept_near(images),
+            jax.ShapeDtypeStruct((slab_count, 2, LANES), f32),
+        ),
+        in_specs=[SMEM, SMEM] + [VMEM] * 5,
+        out_specs=(VMEM, VMEM, VMEM),
         name="rest",
     )(
         primal_step,
         keep,
         factor_near,
-        near(own),
-        near(cand),
+        near(candidate),
         near(new_slice),
         near(volume_now.reshape(images)),
-        near(back_proj.reshape(images)),
-    )
+        near(back_proj),
+    )
+    all_sums = lax.all_to_all(sums, "slab", 0, 0, tiled=True)
     counts = (total_channels * slab_count * slices * rays, slab_count * slices * pixels)
     updated, totals = pl.pallas_call(
         functools.partial(finish_kernel, counts),

time: 81.9 us -> 79.8 us (0.974)
  blocking collectives: 0 us -> 9.91 us
  waiting for transfers between devices: 23.8 us -> 16.7 us
  starting transfers between devices: 40.5 us -> 37.2 us
  local copies, waits for them, and re-layouts: 2.24 us -> 0.81 us
  Pallas kernels: 4.84 us -> 6.25 us
  other arithmetic: 1.01 us -> 0.08 us
    all_to_all x0 -> x1, blocking collectives: none -> 9.91 us  [on_device(): factor_rows = lax.all_to_all(to_share, SHARE, 0, 0, tiled=True)]
    all_to_all x2 -> x1, starting transfers between devices: 9.17 us -> 3.24 us  [on_device(): all_sums = lax.all_to_all(sums, 'slab', 0, 0, tiled=True)]
    all_to_all x2 -> x1, waiting for transfers between devices: 6.27 us -> 2.47 us  [on_device(): all_sums = lax.all_to_all(sums, 'slab', 0, 0, tiled=True)]
    all_to_all x1, waiting for transfers between devices: 14.4 us -> 12.5 us  [on_device(): far_parts = lax.all_to_all(to_far, FAR, 0, 0, tiled=True)]
    dot_general x1, matrix products: 2.23 us -> 0.65 us  [on_device(): jnp.einsum('tij,tbi->tbj', projector, picked_back, preferred_element_type...]
    all_to_all x1, waiting for transfers between devices: 3.2 us -> 1.66 us  [on_device(): lax.all_to_all(partial_gram.reshape(share_count, held, LANES), SHARE, 0,...]
    unnamed x16 -> x11, local copies, waits for them, and re-layouts: 2.11 us -> 0.68 us
    all_to_all x1, starting transfers between devices: 3.87 us -> 5.26 us  [on_device(): lax.all_to_all(partial_gram.reshape(share_count, held, LANES), SHARE, 0,...]
  transfers between devices with their start and end apart: 6 -> 5, of which waited for: 3 -> 3; matrix products, arithmetic and copies ran while one was open for 9% -> 8% of each run, Pallas kernels for 2% -> 3%
where the time goes in v3:
time: 79.8 us; the launch traced here: 79.2 us
  starting transfers between devices  37.2 us (47%)
  waiting for transfers between devices  16.7 us (21%)
  blocking collectives  9.91 us (12%)
  Pallas kernels  6.25 us (8%)
  matrix products  5.48 us (7%)
  between operations  2.74 us (3%)
  local copies, waits for them, and re-layouts  0.81 us (1%)
    ppermute x2, starting transfers between devices, from_behind(): return lax.ppermute(block, axis, route)  14.8 us
    all_to_all x1, starting transfers between devices, on_device(): far_parts = lax.all_to_all(to_far, FAR, 0, 0, tiled=True)  13.9 us
    all_to_all x1, waiting for transfers between devices, on_device(): far_parts = lax.all_to_all(to_far, FAR, 0, 0, tiled=True)  12.5 us
    all_to_all x1, blocking collectives, on_device(): factor_rows = lax.all_to_all(to_share, SHARE, 0, 0, tiled=True)  9.91 us
    all_to_all x1, starting transfers between devices, on_device(): lax.all_to_all(partial_gram.reshape(share_count, held, LANES), SHARE, 0,...  5.26 us
    all_to_all x1, starting transfers between devices, on_device(): all_sums = lax.all_to_all(sums, 'slab', 0, 0, tiled=True)  3.24 us
    dot_general x1, matrix products, on_device(): jnp.einsum('tij,tbj->tbi', projector, picked, preferred_element_type=f32)  2.9 us
    all_to_all x1, waiting for transfers between devices, on_device(): all_sums = lax.all_to_all(sums, 'slab', 0, 0, tiled=True)  2.47 us
  transfers between devices with their start and end apart: 5, of which 3 were waited for; matrix products, arithmetic and copies ran while one was open for 8% of the time, Pallas kernels for 3%

profile of v3, /device:TPU:1, one launch (start us, length us, event | category | flops | bytes accessed | tf_op | source)
XLA Modules:
  0.0 79.2 jit_solution(4928369620783363305)
XLA Ops:
  0.6 0.0 copy-start.3
  0.6 8.8 %collective-permute-start = (f32[8,1,16,512]{3,2,0,1:T(8,128)}, f32[8,1,16,512]{3,2,0,1:T(8,128)S(1)}, u32[]{:S(2)}, u32[]{:S(2)}) collective-permute-start(f32[8,1,16,512]{3,2,0,1:T(8,128)} %bitcast.47), channel_id=1, source_target_pairs={{1,0},{2,1},{3,2},{5,4},{6,5},{7,6},{9,8},{10,9},{11,10},{13,12},{... | collective-permute-start | bytes 786440 | tf_op jit(solution)/shard_map/ppermute | solution.py:39
  10.7 1.5 %own.1 = (f32[8,16,512]{2,1,0:T(8,128)S(1)}, f32[3,8,16,512]{3,2,1,0:T(8,128)S(1)}, f32[3,16,512]{2,1,0:T(8,128)S(1)}) custom-call(f32[1]{0:T(128)} %copy.42.rate_ref, f32[8,16,512]{2,1,0:T(8,128)} %bitcast.48, f32[3,8,16,512]{3,2,1,0:T(8,128)} %bitcast.45), custom_call_target="tpu_custom_call" | custom-call | tf_op jit(solution)/shard_map/own/pallas_call | solution.py:308
  12.2 0.0 collective-permute-done
  12.2 0.9 %gram.1 = (f32[8,16,512]{2,1,0:T(8,128)S(1)}, f32[3,8,16,512]{3,2,1,0:T(8,128)S(1)}, f32[384,128]{1,0:T(8,128)}) custom-call(f32[1]{0:T(128)} %copy.42.rate_ref, f32[1]{0:T(128)} %bitcast.keep_ref, f32[8,16,512]{2,1,0:T(8,128)S(1)} %bitcast.44, f32[3,16,512]{2,1,0:T(8,128)S(1)} %get-tuple-element.19.sums_ref, ...), custom_call_target="tpu_custom_call", output_to_operand_aliasing={{0}: (4, {}), {1}: (5, {})} | custom-call | tf_op jit(solution)/shard_map/gram/pallas_call | solution.py:320
  13.1 0.0 copy-start.4
  13.1 5.3 %all-to-all-start = ((f32[16,24,128]{2,1,0:T(8,128)}), f32[16,24,128]{2,1,0:T(8,128)S(1)}, u32[]{:S(2)}, u32[]{:S(2)}) async-start(f32[16,24,128]{2,1,0:T(8,128)} %bitcast.49), calls=%async_computation | async-start | bytes 393216 | tf_op jit(solution)/shard_map/all_to_all | solution.py:339
  18.4 0.0 copy-start.2
  18.5 0.1 convert_element_type.20
  18.6 0.0 copy-done.3
  18.6 0.2 fusion.9
  18.8 0.0 copy-start.1
  18.8 2.9 %fusion.3 = f32[64,8,128]{2,1,0:T(8,128)S(1)} fusion(bf16[64,128,128]{2,1,0:T(8,128)(2,1)} %param.16, bf16[64,8,128]{2,0,1:T(8,128)(2,1)S(1)} %fusion.9), kind=kOutput, calls=%fused_computation.7 | convolution fusion | flops 16777216 | bytes 2490368 | tf_op jit(solution)/shard_map/tij,tbj->tbi/dot_general | solution.py:345
  21.7 0.0 copy-done.4
  21.7 1.2 %fusion.18 = (f32[8,32,128]{2,1,0:T(8,128)S(1)}, f32[8,32,128]{2,1,0:T(8,128)S(1)}) fusion(f32[8,32,128]{2,1,0:T(8,128)} %bitcast.51, s32[64]{0:T(128)S(1)} %copy-done.4, f32[64,8,128]{2,1,0:T(8,128)S(1)} %fusion.3), kind=kOutput, calls=%fused_computation.21 | convolution fusion | flops 25233408 | bytes 655616 | tf_op jit(solution)/shard_map/tc,tbj->bcj/dot_general | solution.py:274
  22.9 0.0 copy-done.2
  23.0 1.7 %all-to-all-done.parts_ref = f32[16,24,128]{2,1,0:T(8,128)S(1)} async-done(((f32[16,24,128]{2,1,0:T(8,128)}), f32[16,24,128]{2,1,0:T(8,128)S(1)}, u32[]{:S(2)}, u32[]{:S(2)}) %all-to-all-start) | async-done | bytes 196640 | tf_op jit(solution)/shard_map/all_to_all | solution.py:339
  24.6 0.7 pass_on.1
  25.3 13.9 %all-to-all-start.1 = ((f32[8,32,128]{2,1,0:T(8,128)}), f32[8,32,128]{2,1,0:T(8,128)S(1)}, u32[]{:S(2)}, u32[]{:S(2)}) async-start(f32[8,32,128]{2,1,0:T(8,128)} %get-tuple-element.24), calls=%async_computation.1 | async-start | bytes 262144 | tf_op jit(solution)/shard_map/all_to_all | solution.py:362
  39.2 0.2 fusion.5
  39.5 0.0 copy-done.1
  39.5 0.6 fusion.4
  40.1 0.0 copy-start
  40.1 0.3 convolution_bitcast_fusion
  40.5 12.5 %all-to-all-done.1.parts_ref = f32[8,32,128]{2,1,0:T(8,128)S(1)} async-done(((f32[8,32,128]{2,1,0:T(8,128)}), f32[8,32,128]{2,1,0:T(8,128)S(1)}, u32[]{:S(2)}, u32[]{:S(2)}) %all-to-all-start.1) | async-done | bytes 131104 | tf_op jit(solution)/shard_map/all_to_all | solution.py:362
  53.0 1.2 %factor.1 = (f32[16,32,128]{2,1,0:T(8,128)}, f32[8,16,512]{2,1,0:T(8,128)S(1)}) custom-call(f32[1]{0:T(128)S(6)} %mul.12.radius_ref, f32[8,32,128]{2,1,0:T(8,128)S(1)} %all-to-all-done.1.parts_ref, f32[8,16,512]{2,1,0:T(8,128)S(1)} %reshape_reshape.3.back_ref), custom_call_target="tpu_custom_call", output_to_operand_aliasing={{1}: (2, {})} | custom-call | tf_op jit(solution)/shard_map/factor/pallas_call | solution.py:372
  54.2 9.9 %all_to_all.20 = f32[16,32,128]{2,1,0:T(8,128)S(1)} all-to-all(f32[16,32,128]{2,1,0:T(8,128)} %get-tuple-element.26), channel_id=1, replica_groups=mesh['x'=4,'y'=2,'zfar'=8,'znear'=2,'slab'=4] {'x','y','znear'}, dimensions={0} | all-to-all | bytes 524288 | tf_op jit(solution)/shard_map/all_to_all | solution.py:383
  64.1 0.1 slice.1.slice_ref
  64.3 6.0 %collective-permute-start.1 = (f32[8,16,512]{2,1,0:T(8,128)S(1)}, f32[8,16,512]{2,1,0:T(8,128)S(1)}, u32[]{:S(2)}, u32[]{:S(2)}) collective-permute-start(f32[8,16,512]{2,1,0:T(8,128)S(1)} %slice.1.slice_ref), channel_id=1, source_target_pairs={{0,1},{1,2},{2,3},{4,5},{5,6},{6,7},{8,9},{9,10},{10,11},{12,13},{... | collective-permute-start | bytes 786440 | tf_op jit(solution)/shard_map/ppermute | solution.py:39
  71.0 0.0 copy-done
  71.0 1.1 %rest.1 = (f32[3,8,16,512]{3,2,1,0:T(8,128)}, f32[8,16,512]{2,1,0:T(8,128)S(1)}, f32[4,2,128]{2,1,0:T(2,128)}) custom-call(f32[1]{0:T(128)S(6)} %copy.43.rate_ref, f32[1]{0:T(128)} %bitcast.keep_ref, f32[512,128]{1,0:T(8,128)S(1)} %bitcast.42, f32[3,8,16,512]{3,2,1,0:T(8,128)S(1)} %get-tuple-element.27.cand_ref, f32[8,16,512]{2,1,0:T(8,128)S(1)} %slice.1.slice_ref, ...), custom_call_target="tpu_custom_call" | custom-call | tf_op jit(solution)/shard_map/rest/pallas_call | solution.py:394
  72.1 3.2 %all-to-all-start.3 = ((f32[4,2,128]{2,1,0:T(2,128)}), f32[4,2,128]{2,1,0:T(2,128)S(1)}, u32[]{:S(2)}, u32[]{:S(2)}) async-start(f32[4,2,128]{2,1,0:T(2,128)} %get-tuple-element.30), calls=%async_computation.3 | async-start | bytes 8192 | tf_op jit(solution)/shard_map/all_to_all | solution.py:413
  75.3 0.7 copy.41
  76.0 2.5 %all-to-all-done.3.sums_ref = f32[4,2,128]{2,1,0:T(2,128)S(1)} async-done(((f32[4,2,128]{2,1,0:T(2,128)}), f32[4,2,128]{2,1,0:T(2,128)S(1)}, u32[]{:S(2)}, u32[]{:S(2)}) %all-to-all-start.3) | async-done | bytes 4128 | tf_op jit(solution)/shard_map/all_to_all | solution.py:413
  78.4 0.0 collective-permute-done.1.prior_ref
  78.5 0.7 finish.1
  (4 shorter events, 0.1 us)
Async XLA Ops:
  0.6 17.9 %copy-start.3 = (s32[64]{0:T(128)S(1)}, s32[64]{0:T(128)}, u32[]{:S(2)}) copy-start(s32[64]{0:T(128)} %param.18) | copy-start | bytes 772
  0.6 11.6 %collective-permute-start = (f32[8,1,16,512]{3,2,0,1:T(8,128)}, f32[8,1,16,512]{3,2,0,1:T(8,128)S(1)}, u32[]{:S(2)}, u32[]{:S(2)}) collective-permute-start(f32[8,1,16,512]{3,2,0,1:T(8,128)} %bitcast.47), channel_id=1, source_target_pairs={{1,0},{2,1},{3,2},{5,4},{6,5},{7,6},{9,8},{10,9},{11,10},{13,12},{... | collective-permute-start | bytes 786440 | tf_op jit(solution)/shard_map/ppermute | solution.py:39
  13.1 8.6 %copy-start.4 = (s32[64]{0:T(128)S(1)}, s32[64]{0:T(128)}, u32[]{:S(2)}) copy-start(s32[64]{0:T(128)} %param.17) | copy-start | bytes 772
  13.1 11.5 %all-to-all-start = ((f32[16,24,128]{2,1,0:T(8,128)}), f32[16,24,128]{2,1,0:T(8,128)S(1)}, u32[]{:S(2)}, u32[]{:S(2)}) async-start(f32[16,24,128]{2,1,0:T(8,128)} %bitcast.49), calls=%async_computation | async-start | bytes 393216 | tf_op jit(solution)/shard_map/all_to_all | solution.py:339
  18.4 4.5 %copy-start.2 = (f32[8,1,4096]{2,1,0:T(1,128)S(1)}, f32[8,1,4096]{2,1,0:T(1,128)}, u32[]{:S(2)}) copy-start(f32[8,1,4096]{2,1,0:T(1,128)} %param.14) | copy-start | bytes 393220
  18.8 20.7 %copy-start.1 = (bf16[64,128,128]{2,1,0:T(8,128)(2,1)S(1)}, bf16[64,128,128]{2,1,0:T(8,128)(2,1)}, u32[]{:S(2)}) copy-start(bf16[64,128,128]{2,1,0:T(8,128)(2,1)} %param.16) | copy-start | bytes 6291460
  25.3 27.7 %all-to-all-start.1 = ((f32[8,32,128]{2,1,0:T(8,128)}), f32[8,32,128]{2,1,0:T(8,128)S(1)}, u32[]{:S(2)}, u32[]{:S(2)}) async-start(f32[8,32,128]{2,1,0:T(8,128)} %get-tuple-element.24), calls=%async_computation.1 | async-start | bytes 262144 | tf_op jit(solution)/shard_map/all_to_all | solution.py:362
  40.1 30.8 %copy-start = (f32[8,1,16,512]{3,2,1,0:T(8,128)S(1)}, f32[8,1,16,512]{3,2,1,0:T(8,128)}, u32[]{:S(2)}) copy-start(f32[8,1,16,512]{3,2,1,0:T(8,128)} %param.11) | copy-start | bytes 786436
  64.3 14.2 %collective-permute-start.1 = (f32[8,16,512]{2,1,0:T(8,128)S(1)}, f32[8,16,512]{2,1,0:T(8,128)S(1)}, u32[]{:S(2)}, u32[]{:S(2)}) collective-permute-start(f32[8,16,512]{2,1,0:T(8,128)S(1)} %slice.1.slice_ref), channel_id=1, source_target_pairs={{0,1},{1,2},{2,3},{4,5},{5,6},{6,7},{8,9},{9,10},{10,11},{12,13},{... | collective-permute-start | bytes 786440 | tf_op jit(solution)/shard_map/ppermute | solution.py:39
  72.1 6.4 %all-to-all-start.3 = ((f32[4,2,128]{2,1,0:T(2,128)}), f32[4,2,128]{2,1,0:T(2,128)S(1)}, u32[]{:S(2)}, u32[]{:S(2)}) async-start(f32[4,2,128]{2,1,0:T(2,128)} %get-tuple-element.30), calls=%async_computation.3 | async-start | bytes 8192 | tf_op jit(solution)/shard_map/all_to_all | solution.py:413

commit v4 on v3

--- a/solution.py
+++ b/solution.py
@@ -23,10 +23,15 @@
 VMEM = pl.BlockSpec(memory_space=pltpu.VMEM)
 SMEM = pl.BlockSpec(memory_space=pltpu.SMEM)
 ANY = pl.BlockSpec(memory_space=pl.ANY)
+SCRATCH = pltpu.CompilerParams(vmem_limit_bytes=6 * 2**20)
 
 
 def near(array):
     return pltpu.with_memory_space_constraint(array, pltpu.VMEM)
+
+
+def left_far(array):
+    return pltpu.with_memory_space_constraint(array, pltpu.HBM)
 
 
 def kept_near(shape):
@@ -39,7 +44,10 @@
     return lax.ppermute(block, axis, route)
 
 
-def own_kernel(rate_ref, x_far, dual_far, x_ref, cand_ref, sums_ref, arrived):
+def own_kernel(rate_ref, x_far, dual_far, *refs):
+    count = (len(refs) - 5) // 2
+    others_far, (x_ref, cand_ref, sums_ref), others = refs[:count], refs[count : count + 3], refs[count + 3 : -2]
+    arrived, others_in = refs[-2:]
     channels, rows, cols = x_ref.shape
     tiles = cols // LANES
     parts = arrived.shape[1]
@@ -57,6 +65,12 @@
         )
         for copy in copies[-1]:
             copy.start()
+    other_copies = [
+        pltpu.make_async_copy(far, here, others_in.at[k])
+        for k, (far, here) in enumerate(zip(others_far, others))
+    ]
+    for copy in other_copies:
+        copy.start()
     rate = rate_ref[0]
     inner_row = lax.broadcasted_iota(jnp.int32, (rows, LANES), 0) < rows - 1
     edge_lane = lax.broadcasted_iota(jnp.int32, (rows, LANES), 1) == LANES - 1
@@ -87,6 +101,8 @@
                 sums = [s + cand[a] * cand[b] for s, (a, b) in zip(sums, own_pairs)]
             for k, s in enumerate(sums):
                 sums_ref[k, :, here] = s
+    for copy in other_copies:
+        copy.wait()
 
 
 def gram_kernel(
@@ -206,6 +222,18 @@
             new_ref[c, :, here] = sum(cand_ref[b, c, :, here] * factor[b] for b in range(3))
 
 
+def sums_kernel(factor_ref, slice_ref, sums_ref):
+    slabs, count, _ = sums_ref.shape
+    rows = slice_ref.shape[1]
+    tiles = slice_ref.shape[2] // LANES
+    image = factor_image(factor_ref, rows, tiles)
+    for k in range(count):
+        total = sum(image(len(index_pairs) + k, j) for j in range(tiles))
+        total = jnp.sum(total, axis=0, keepdims=True)
+        for p in range(slabs):
+            sums_ref[p, pl.ds(k, 1), :] = total
+
+
 def rest_kernel(
     rate_ref,
     keep_ref,
@@ -216,18 +244,12 @@
     back_ref,
     new_ref,
     ready_ref,
-    sums_ref,
 ):
     _, channels, rows, cols = cand_ref.shape
     tiles = cols // LANES
     rate = rate_ref[0]
     keep = keep_ref[0]
     image = factor_image(factor_ref, rows, tiles)
-    for k in range(2):
-        total = sum(image(len(index_pairs) + k, j) for j in range(tiles))
-        total = jnp.sum(total, axis=0, keepdims=True)
-        for p in range(sums_ref.shape[0]):
-            sums_ref[p, pl.ds(k, 1), :] = total
     row_id = lax.broadcasted_iota(jnp.int32, (rows, LANES), 0)
     lane_id = lax.broadcasted_iota(jnp.int32, (rows, LANES), 1)
     before = [None] * channels
@@ -305,18 +327,25 @@
     image_form = jax.ShapeDtypeStruct(images, f32)
 
     following = from_behind(extrapolated, "slab", -1)
-    x_near, duals, own_sums = pl.pallas_call(
+    sinogram = (channels, rays // edge, edge)
+    others = (measured.reshape(sinogram), dual_data.reshape(sinogram), projector)
+    x_near, duals, own_sums, measured_near, data_near, projector_near = pl.pallas_call(
         own_kernel,
         out_shape=(
             kept_near(images),
             kept_near((3, *images)),
             kept_near((len(own_pairs), row_count, col_count)),
+            *(pltpu.VMEM(other.shape, other.dtype) for other in others),
         ),
-        in_specs=[SMEM, ANY, ANY],
-        out_specs=(VMEM, VMEM, VMEM),
-        scratch_shapes=[pltpu.SemaphoreType.DMA((2, 4))],
+        in_specs=[SMEM] + [ANY] * 5,
+        out_specs=(VMEM,) * 6,
+        scratch_shapes=[pltpu.SemaphoreType.DMA((2, 4)), pltpu.SemaphoreType.DMA((len(others),))],
+        compiler_params=SCRATCH,
         name="own",
-    )(dual_step, extrapolated.reshape(images), dual_grad.reshape(3, *images))
+    )(
+        dual_step,
+        *map(left_far, (extrapolated.reshape(images), dual_grad.reshape(3, *images), *others)),
+    )
     x_near, candidate, partial_gram = pl.pallas_call(
         gram_kernel,
         out_shape=(
@@ -327,6 +356,7 @@
         in_specs=[SMEM, SMEM, VMEM, VMEM, VMEM, VMEM],
         out_specs=(VMEM, VMEM, VMEM),
         input_output_aliases={4: 0, 5: 1},
+        compiler_params=SCRATCH,
         name="gram",
     )(
         dual_step,
@@ -342,10 +372,10 @@
 
     rounded = x_near.reshape(channels, pixels // edge, edge).astype(jnp.bfloat16)
     picked = picked_blocks(rounded, tile_cols, pixels // edge)
-    products = jnp.einsum("tij,tbj->tbi", projector, picked, preferred_element_type=f32)
+    products = jnp.einsum("tij,tbj->tbi", projector_near, picked, preferred_element_type=f32)
     projected = gathered_products(products, tile_rows, rays // edge)
-    residual = projected - measured.reshape(projected.shape)
-    data_new = (dual_data.reshape(projected.shape) + dual_rate * residual) / (1.0 + dual_rate)
+    residual = projected - measured_near
+    data_new = (data_near + dual_rate * residual) / (1.0 + dual_rate)
     misfit_part = jnp.sum((residual * residual).reshape(-1, 8, LANES), axis=0)
 
     to_far, data_new = pl.pallas_call(
@@ -357,13 +387,16 @@
         in_specs=[VMEM, VMEM, VMEM],
         out_specs=(VMEM, VMEM),
         input_output_aliases={2: 1},
+        compiler_params=SCRATCH,
         name="pass_on",
     )(near(gram_parts), near(misfit_part), near(data_new))
-    far_parts = lax.all_to_all(to_far, FAR, 0, 0, tiled=True)
+    half = far_count // 2
+    late_first = [[(half + i) % far_count for i in range(far_count)]]
+    far_parts = lax.all_to_all(to_far, FAR, 0, 0, axis_index_groups=late_first, tiled=True)
 
     data_low = data_new.astype(jnp.bfloat16)
     picked_back = picked_blocks(data_low, tile_rows, rays // edge)
-    products_back = jnp.einsum("tij,tbi->tbj", projector, picked_back, preferred_element_type=f32)
+    products_back = jnp.einsum("tij,tbi->tbj", projector_near, picked_back, preferred_element_type=f32)
     back_proj = gathered_products(products_back, tile_cols, pixels // edge).reshape(
         volume_now.shape
     )
@@ -378,6 +411,7 @@
         in_specs=[SMEM, VMEM, VMEM],
         out_specs=(VMEM, VMEM),
         input_output_aliases={2: 1},
+        compiler_params=SCRATCH,
         name="factor",
     )(radius, near(far_parts), near(back_proj.reshape(images)))
     factor_rows = lax.all_to_all(to_share, SHARE, 0, 0, tiled=True)
@@ -388,18 +422,25 @@
         out_shape=kept_near(images),
         in_specs=[VMEM, VMEM],
         out_specs=VMEM,
+        compiler_params=SCRATCH,
         name="slice",
     )(factor_near, near(candidate))
     prior_layer = from_behind(new_slice, "slab", 1)
-    grad_new, ready, sums = pl.pallas_call(
+    sums = pl.pallas_call(
+        sums_kernel,
+        out_shape=jax.ShapeDtypeStruct((slab_count, 2, LANES), f32),
+        in_specs=[VMEM, VMEM],
+        out_specs=VMEM,
+        compiler_params=SCRATCH,
+        name="sums",
+    )(factor_near, near(new_slice))
+    all_sums = lax.all_to_all(sums, "slab", 0, 0, tiled=True)
+    grad_new, ready = pl.pallas_call(
         rest_kernel,
-        out_shape=(
-            jax.ShapeDtypeStruct((3, *images), f32),
-            kept_near(images),
-            jax.ShapeDtypeStruct((slab_count, 2, LANES), f32),
-        ),
+        out_shape=(jax.ShapeDtypeStruct((3, *images), f32), kept_near(images)),
         in_specs=[SMEM, SMEM] + [VMEM] * 5,
-        out_specs=(VMEM, VMEM, VMEM),
+        out_specs=(VMEM, VMEM),
+        compiler_params=SCRATCH,
         name="rest",
     )(
         primal_step,
@@ -410,13 +451,13 @@
         near(volume_now.reshape(images)),
         near(back_proj),
     )
-    all_sums = lax.all_to_all(sums, "slab", 0, 0, tiled=True)
     counts = (total_channels * slab_count * slices * rays, slab_count * slices * pixels)
     updated, totals = pl.pallas_call(
         functools.partial(finish_kernel, counts),
         out_shape=(image_form, jax.ShapeDtypeStruct((2,), f32)),
         in_specs=[SMEM, VMEM, VMEM, VMEM],
         out_specs=(VMEM, SMEM),
+        compiler_params=SCRATCH,
         name="finish",
     )(primal_step, near(ready), near(prior_layer), near(all_sums))
     return (

time: 79.8 us -> 71.4 us (0.89)
  waiting for transfers between devices: 16.7 us -> 7.33 us
  matrix products: 5.48 us -> 3.49 us
  starting transfers between devices: 37.2 us -> 38.6 us
  other arithmetic: 0.08 us -> 0.98 us
    all_to_all x1, waiting for transfers between devices: 12.5 us -> 3.72 us  [on_device(): lax.all_to_all(to_far, FAR, 0, 0, axis_index_groups=late_first, tiled=True)]
    all_to_all x1, starting transfers between devices: 13.9 us -> 16.9 us  [on_device(): lax.all_to_all(to_far, FAR, 0, 0, axis_index_groups=late_first, tiled=True)]
    all_to_all x1, waiting for transfers between devices: 2.47 us -> 0.71 us  [on_device(): all_sums = lax.all_to_all(sums, 'slab', 0, 0, tiled=True)]
    dot_general x2, matrix products: 3.55 us -> 1.83 us  [the longest x1 1.18 us: on_device(): jnp.einsum('tij,tbj->tbi', projector_near, picked, preferred_element_type...]
    all_to_all x1, waiting for transfers between devices: 1.66 us -> 2.9 us  [on_device(): lax.all_to_all(partial_gram.reshape(share_count, held, LANES), SHARE, 0,...]
    reduce_sum x1, other arithmetic: 0.04 us -> 0.94 us  [on_device(): misfit_part = jnp.sum((residual * residual).reshape(-1, 8, LANES), axis=0)]
    all_to_all x1, starting transfers between devices: 5.26 us -> 4.4 us  [on_device(): lax.all_to_all(partial_gram.reshape(share_count, held, LANES), SHARE, 0,...]
  transfers between devices with their start and end apart: 5 -> 5, of which waited for: 3 -> 3; matrix products, arithmetic and copies ran while one was open for 8% -> 7% of each run, Pallas kernels for 3% -> 6%
where the time goes in v4:
time: 71.4 us; the launch traced here: 70.9 us
  starting transfers between devices  38.6 us (54%)
  blocking collectives  10.1 us (14%)
  waiting for transfers between devices  7.33 us (10%)
  Pallas kernels  6.92 us (10%)
  matrix products  3.49 us (5%)
  between operations  2.71 us (4%)
  other arithmetic  0.98 us (1%)
  local copies, waits for them, and re-layouts  0.8 us (1%)
    all_to_all x1, starting transfers between devices, on_device(): lax.all_to_all(to_far, FAR, 0, 0, axis_index_groups=late_first, tiled=True)  16.9 us
    ppermute x2, starting transfers between devices, from_behind(): return lax.ppermute(block, axis, route)  14.1 us
    all_to_all x1, blocking collectives, on_device(): factor_rows = lax.all_to_all(to_share, SHARE, 0, 0, tiled=True)  10.1 us
    all_to_all x1, starting transfers between devices, on_device(): lax.all_to_all(partial_gram.reshape(share_count, held, LANES), SHARE, 0,...  4.4 us
    all_to_all x1, waiting for transfers between devices, on_device(): lax.all_to_all(to_far, FAR, 0, 0, axis_index_groups=late_first, tiled=True)  3.72 us
    all_to_all x1, starting transfers between devices, on_device(): all_sums = lax.all_to_all(sums, 'slab', 0, 0, tiled=True)  3.24 us
    all_to_all x1, waiting for transfers between devices, on_device(): lax.all_to_all(partial_gram.reshape(share_count, held, LANES), SHARE, 0,...  2.9 us
    pallas_call x1, Pallas kernels, on_device(): pl.pallas_call(own_kernel, out_shape=(kept_near(images), kept_near((3, *i...  2.22 us
  transfers between devices with their start and end apart: 5, of which 3 were waited for; matrix products, arithmetic and copies ran while one was open for 7% of the time, Pallas kernels for 6%

profile of v4, /device:TPU:1, one launch (start us, length us, event | category | flops | bytes accessed | tf_op | source)
XLA Modules:
  0.0 70.9 jit_solution(2998233863404769135)
XLA Ops:
  0.6 8.8 %collective-permute-start = (f32[8,1,16,512]{3,2,0,1:T(8,128)}, f32[8,1,16,512]{3,2,0,1:T(8,128)S(1)}, u32[]{:S(2)}, u32[]{:S(2)}) collective-permute-start(f32[8,1,16,512]{3,2,0,1:T(8,128)} %bitcast.48), channel_id=1, source_target_pairs={{1,0},{2,1},{3,2},{5,4},{6,5},{7,6},{9,8},{10,9},{11,10},{13,12},{... | collective-permute-start | bytes 786440 | tf_op jit(solution)/shard_map/ppermute | solution.py:44
  10.7 0.0 copy-start.1
  10.7 2.2 %own.1 = (f32[8,16,512]{2,1,0:T(8,128)S(1)}, f32[3,8,16,512]{3,2,1,0:T(8,128)S(1)}, f32[3,16,512]{2,1,0:T(8,128)S(1)}, f32[8,32,128]{2,1,0:T(8,128)S(1)}, f32[8,...) custom-call(f32[1]{0:T(128)} %copy.42.rate_ref, f32[8,16,512]{2,1,0:T(8,128)} %bitcast.49, ...), custom_call_target="tpu_custom_call" | custom-call | tf_op jit(solution)/shard_map/own/pallas_call | solution.py:332
  13.0 0.0 collective-permute-done
  13.0 0.9 %gram.1 = (f32[8,16,512]{2,1,0:T(8,128)S(1)}, f32[3,8,16,512]{3,2,1,0:T(8,128)S(1)}, f32[384,128]{1,0:T(8,128)}) custom-call(f32[1]{0:T(128)} %copy.42.rate_ref, f32[1]{0:T(128)} %bitcast.keep_ref, f32[8,16,512]{2,1,0:T(8,128)S(1)} %bitcast.45, f32[3,16,512]{2,1,0:T(8,128)S(1)} %get-tuple-element.21.sums_ref, ...), custom_call_target="tpu_custom_call", output_to_operand_aliasing={{0}: (4, {}), {1}: (5, {})} | custom-call | tf_op jit(solution)/shard_map/gram/pallas_call | solution.py:349
  13.9 0.0 copy-start.2
  13.9 0.1 convert_element_type.20
  14.0 4.4 %all-to-all-start = ((f32[16,24,128]{2,1,0:T(8,128)}), f32[16,24,128]{2,1,0:T(8,128)S(1)}, u32[]{:S(2)}, u32[]{:S(2)}) async-start(f32[16,24,128]{2,1,0:T(8,128)} %bitcast.7), calls=%async_computation | async-start | bytes 393216 | tf_op jit(solution)/shard_map/all_to_all | solution.py:369
  18.4 0.0 copy-done.1
  18.4 0.2 fusion.9
  18.6 1.2 %fusion.3 = f32[64,8,128]{2,1,0:T(8,128)S(1)} fusion(bf16[64,128,128]{2,1,0:T(8,128)(2,1)S(1)} %get-tuple-element.26, bf16[64,8,128]{2,0,1:T(8,128)(2,1)S(1)} %fusion.9), kind=kOutput, calls=%fused_computation.7 | convolution fusion | flops 16777216 | bytes 2490368 | tf_op jit(solution)/shard_map/tij,tbj->tbi/dot_general | solution.py:375
  19.8 0.0 copy-done.2
  19.8 0.9 %fusion.18 = (f32[8,32,128]{2,1,0:T(8,128)}, f32[8,32,128]{2,1,0:T(8,128)S(1)}) fusion(f32[8,32,128]{2,1,0:T(8,128)S(1)} %get-tuple-element.27, s32[64]{0:T(128)S(1)} %copy-done.2, f32[64,8,128]{2,1,0:T(8,128)S(1)} %fusion.3), kind=kOutput, calls=%fused_computation.21 | convolution fusion | flops 25233408 | bytes 655616 | tf_op jit(solution)/shard_map/tc,tbj->bcj/dot_general | solution.py:296
  20.8 0.9 %reduce_sum.9.misfit_ref = f32[8,128]{1,0:T(8,128)S(1)} reduce(f32[32,8,128]{2,1,0:T(8,128)} %bitcast.47, f32[]{:T(128)} %constant.2.clone.1), dimensions={0}, to_apply=%region_0.1 | reduce | flops 31744 | bytes 135172 | tf_op jit(solution)/shard_map/reduce_sum | solution.py:379
  21.7 2.9 %all-to-all-done.parts_ref = f32[16,24,128]{2,1,0:T(8,128)S(1)} async-done(((f32[16,24,128]{2,1,0:T(8,128)}), f32[16,24,128]{2,1,0:T(8,128)S(1)}, u32[]{:S(2)}, u32[]{:S(2)}) %all-to-all-start) | async-done | bytes 196640 | tf_op jit(solution)/shard_map/all_to_all | solution.py:369
  24.6 0.7 pass_on.1
  25.3 0.2 fusion.5
  25.5 16.9 %all-to-all-start.1 = ((f32[8,32,128]{2,1,0:T(8,128)}), f32[8,32,128]{2,1,0:T(8,128)S(1)}, u32[]{:S(2)}, u32[]{:S(2)}) async-start(f32[8,32,128]{2,1,0:T(8,128)} %get-tuple-element.29), calls=%async_computation.1 | async-start | bytes 262144 | tf_op jit(solution)/shard_map/all_to_all | solution.py:395
  42.5 0.6 fusion.4
  43.1 0.0 copy-start
  43.1 0.3 convolution_bitcast_fusion
  43.5 3.7 %all-to-all-done.1.parts_ref = f32[8,32,128]{2,1,0:T(8,128)S(1)} async-done(((f32[8,32,128]{2,1,0:T(8,128)}), f32[8,32,128]{2,1,0:T(8,128)S(1)}, u32[]{:S(2)}, u32[]{:S(2)}) %all-to-all-start.1) | async-done | bytes 131104 | tf_op jit(solution)/shard_map/all_to_all | solution.py:395
  47.2 0.5 factor.1
  47.7 10.1 %all_to_all.20 = f32[16,32,128]{2,1,0:T(8,128)S(1)} all-to-all(f32[16,32,128]{2,1,0:T(8,128)S(1)} %get-tuple-element.31), channel_id=1, replica_groups=mesh['x'=4,'y'=2,'zfar'=8,'znear'=2,'slab'=4] {'x','y','znear'}, dimensions={0} | all-to-all | bytes 524288 | tf_op jit(solution)/shard_map/all_to_all | solution.py:417
  57.7 0.1 slice.1.slice_ref
  57.9 5.3 %collective-permute-start.1 = (f32[8,16,512]{2,1,0:T(8,128)S(1)}, f32[8,16,512]{2,1,0:T(8,128)S(1)}, u32[]{:S(2)}, u32[]{:S(2)}) collective-permute-start(f32[8,16,512]{2,1,0:T(8,128)S(1)} %slice.1.slice_ref), channel_id=1, source_target_pairs={{0,1},{1,2},{2,3},{4,5},{5,6},{6,7},{8,9},{9,10},{10,11},{12,13},{... | collective-permute-start | bytes 786440 | tf_op jit(solution)/shard_map/ppermute | solution.py:44
  63.2 0.6 sums.1
  63.8 3.2 %all-to-all-start.3 = ((f32[4,2,128]{2,1,0:T(2,128)}), f32[4,2,128]{2,1,0:T(2,128)S(1)}, u32[]{:S(2)}, u32[]{:S(2)}) async-start(f32[4,2,128]{2,1,0:T(2,128)} %sums.1), calls=%async_computation.3 | async-start | bytes 8192 | tf_op jit(solution)/shard_map/all_to_all | solution.py:437
  67.7 0.7 copy.41
  68.4 0.0 copy-done
  68.4 1.1 %rest.1 = (f32[3,8,16,512]{3,2,1,0:T(8,128)}, f32[8,16,512]{2,1,0:T(8,128)S(1)}) custom-call(f32[1]{0:T(128)S(6)} %copy.43.rate_ref, f32[1]{0:T(128)} %bitcast.keep_ref, f32[512,128]{1,0:T(8,128)S(1)} %bitcast.43, f32[3,8,16,512]{3,2,1,0:T(8,128)S(1)} %get-tuple-element.32.cand_ref, f32[8,16,512]{2,1,0:T(8,128)S(1)} %slice.1.slice_ref, ...), custom_call_target="tpu_custom_call" | custom-call | tf_op jit(solution)/shard_map/rest/pallas_call | solution.py:438
  69.5 0.7 all-to-all-done.3.sums_ref
  70.2 0.0 collective-permute-done.1.prior_ref
  70.2 0.7 %finish.1 = (f32[8,16,512]{2,1,0:T(8,128)}, f32[2]{0:T(128)}) custom-call(f32[1]{0:T(128)S(6)} %copy.43.rate_ref, f32[8,16,512]{2,1,0:T(8,128)S(1)} %get-tuple-element.34.ready_ref, f32[8,16,512]{2,1,0:T(8,128)S(1)} %collective-permute-done.1.prior_ref, f32[4,2,128]{2,1,0:T(2,128)S(1)} %all-to-all-done.3.sums_ref), custom_call_target="tpu_custom_call" | custom-call | tf_op jit(solution)/shard_map/finish/pallas_call | solution.py:455
  (3 shorter events, 0.1 us)
Async XLA Ops:
  0.6 12.3 %collective-permute-start = (f32[8,1,16,512]{3,2,0,1:T(8,128)}, f32[8,1,16,512]{3,2,0,1:T(8,128)S(1)}, u32[]{:S(2)}, u32[]{:S(2)}) collective-permute-start(f32[8,1,16,512]{3,2,0,1:T(8,128)} %bitcast.48), channel_id=1, source_target_pairs={{1,0},{2,1},{3,2},{5,4},{6,5},{7,6},{9,8},{10,9},{11,10},{13,12},{... | collective-permute-start | bytes 786440 | tf_op jit(solution)/shard_map/ppermute | solution.py:44
  10.7 7.7 %copy-start.1 = (s32[64]{0:T(128)S(1)}, s32[64]{0:T(128)}, u32[]{:S(2)}) copy-start(s32[64]{0:T(128)} %param.18) | copy-start | bytes 772
  13.9 6.0 %copy-start.2 = (s32[64]{0:T(128)S(1)}, s32[64]{0:T(128)}, u32[]{:S(2)}) copy-start(s32[64]{0:T(128)} %param.17) | copy-start | bytes 772
  14.0 10.6 %all-to-all-start = ((f32[16,24,128]{2,1,0:T(8,128)}), f32[16,24,128]{2,1,0:T(8,128)S(1)}, u32[]{:S(2)}, u32[]{:S(2)}) async-start(f32[16,24,128]{2,1,0:T(8,128)} %bitcast.7), calls=%async_computation | async-start | bytes 393216 | tf_op jit(solution)/shard_map/all_to_all | solution.py:369
  25.5 21.6 %all-to-all-start.1 = ((f32[8,32,128]{2,1,0:T(8,128)}), f32[8,32,128]{2,1,0:T(8,128)S(1)}, u32[]{:S(2)}, u32[]{:S(2)}) async-start(f32[8,32,128]{2,1,0:T(8,128)} %get-tuple-element.29), calls=%async_computation.1 | async-start | bytes 262144 | tf_op jit(solution)/shard_map/all_to_all | solution.py:395
  43.1 25.3 %copy-start = (f32[8,1,16,512]{3,2,1,0:T(8,128)S(1)}, f32[8,1,16,512]{3,2,1,0:T(8,128)}, u32[]{:S(2)}) copy-start(f32[8,1,16,512]{3,2,1,0:T(8,128)} %param.11) | copy-start | bytes 786436
  57.9 12.3 %collective-permute-start.1 = (f32[8,16,512]{2,1,0:T(8,128)S(1)}, f32[8,16,512]{2,1,0:T(8,128)S(1)}, u32[]{:S(2)}, u32[]{:S(2)}) collective-permute-start(f32[8,16,512]{2,1,0:T(8,128)S(1)} %slice.1.slice_ref), channel_id=1, source_target_pairs={{0,1},{1,2},{2,3},{4,5},{5,6},{6,7},{8,9},{9,10},{10,11},{12,13},{... | collective-permute-start | bytes 786440 | tf_op jit(solution)/shard_map/ppermute | solution.py:44
  63.8 6.4 %all-to-all-start.3 = ((f32[4,2,128]{2,1,0:T(2,128)}), f32[4,2,128]{2,1,0:T(2,128)S(1)}, u32[]{:S(2)}, u32[]{:S(2)}) async-start(f32[4,2,128]{2,1,0:T(2,128)} %sums.1), calls=%async_computation.3 | async-start | bytes 8192 | tf_op jit(solution)/shard_map/all_to_all | solution.py:437

commit v5 on v3

--- a/solution.py
+++ b/solution.py
@@ -1,4 +1,5 @@
 import functools
+import itertools
 import math
 
 import jax
@@ -23,14 +24,31 @@
 VMEM = pl.BlockSpec(memory_space=pltpu.VMEM)
 SMEM = pl.BlockSpec(memory_space=pltpu.SMEM)
 ANY = pl.BlockSpec(memory_space=pl.ANY)
+SCRATCH = pltpu.CompilerParams(vmem_limit_bytes=6 * 2**20)
 
 
 def near(array):
     return pltpu.with_memory_space_constraint(array, pltpu.VMEM)
 
 
+def left_far(array):
+    return pltpu.with_memory_space_constraint(array, pltpu.HBM)
+
+
 def kept_near(shape):
     return pltpu.VMEM(shape, jnp.float32)
+
+
+def by_distance(axes, first):
+    sizes = [lax.axis_size(axis) for axis in axes]
+    places = list(itertools.product(*map(range, sizes)))
+
+    def away(place):
+        return sum(min((a - b) % n, (b - a) % n) for a, b, n in zip(place, first, sizes))
+
+    order = sorted(range(len(places)), key=lambda i: -away(places[i]))
+    order.remove(places.index(first))
+    return [places.index(first), *order]
 
 
 def from_behind(block, axis, distance):
@@ -39,7 +57,20 @@
     return lax.ppermute(block, axis, route)
 
 
-def own_kernel(rate_ref, x_far, dual_far, x_ref, cand_ref, sums_ref, arrived):
+def own_kernel(
+    rate_ref,
+    x_far,
+    dual_far,
+    measured_far,
+    data_far,
+    x_ref,
+    cand_ref,
+    sums_ref,
+    measured_ref,
+    data_ref,
+    arrived,
+    data_arrived,
+):
     channels, rows, cols = x_ref.shape
     tiles = cols // LANES
     parts = arrived.shape[1]
@@ -57,6 +88,12 @@
         )
         for copy in copies[-1]:
             copy.start()
+    data_copies = (
+        pltpu.make_async_copy(measured_far, measured_ref, data_arrived.at[0]),
+        pltpu.make_async_copy(data_far, data_ref, data_arrived.at[1]),
+    )
+    for copy in data_copies:
+        copy.start()
     rate = rate_ref[0]
     inner_row = lax.broadcasted_iota(jnp.int32, (rows, LANES), 0) < rows - 1
     edge_lane = lax.broadcasted_iota(jnp.int32, (rows, LANES), 1) == LANES - 1
@@ -87,11 +124,26 @@
                 sums = [s + cand[a] * cand[b] for s, (a, b) in zip(sums, own_pairs)]
             for k, s in enumerate(sums):
                 sums_ref[k, :, here] = s
+    for copy in data_copies:
+        copy.wait()
 
 
 def gram_kernel(
-    rate_ref, keep_ref, next_ref, sums_ref, x_ref, dual_ref, x_same, cand_ref, out_ref
+    rate_ref,
+    keep_ref,
+    projector_far,
+    next_ref,
+    sums_ref,
+    x_ref,
+    dual_ref,
+    x_same,
+    cand_ref,
+    out_ref,
+    projector_ref,
+    arrived,
 ):
+    projector_copy = pltpu.make_async_copy(projector_far, projector_ref, arrived)
+    projector_copy.start()
     channels, rows, cols = x_ref.shape
     tiles = cols // LANES
     per_row = len(index_pairs) * tiles
@@ -111,6 +163,7 @@
             cand_ref[2, c, :, here] = cand
         for k, pair in enumerate(index_pairs):
             out_ref[pl.ds(k * tiles + j, rows, stride=per_row), :] = sums[pair]
+    projector_copy.wait()
 
 
 def pass_on_kernel(parts_ref, misfit_ref, data_ref, out_ref, data_same):
@@ -152,7 +205,7 @@
     return entry, vectors
 
 
-def factor_kernel(radius_ref, parts_ref, back_ref, out_ref, back_same):
+def factor_kernel(channels, weight_ref, parts_ref, back_ref, out_ref, back_same):
     peers, held, _ = parts_ref.shape
     entries = len(index_pairs)
     tiles = out_ref.shape[1] // (entries + 2)
@@ -163,7 +216,7 @@
             total = total + parts_ref[p, pl.ds(start, size), :]
         return total
 
-    radius = radius_ref[0]
+    radius = weight_ref[0] * math.sqrt(channels)
     entry = [summed(k * tiles, tiles) for k in range(entries)]
     one, zero = jnp.ones_like(entry[0]), jnp.zeros_like(entry[0])
     vectors = [[one if r == c else zero for c in range(3)] for r in range(3)]
@@ -195,7 +248,7 @@
     return entry_of[tuple(sorted((a, b)))]
 
 
-def slice_kernel(factor_ref, cand_ref, new_ref):
+def slice_kernel(factor_ref, cand_ref, new_ref, sums_ref):
     _, channels, rows, cols = cand_ref.shape
     tiles = cols // LANES
     image = factor_image(factor_ref, rows, tiles)
@@ -204,6 +257,16 @@
         factor = [image(entry_at(b, 2), j) for b in range(3)]
         for c in range(channels):
             new_ref[c, :, here] = sum(cand_ref[b, c, :, here] * factor[b] for b in range(3))
+    per_row = factor_ref.shape[0] // rows
+    slabs, count, _ = sums_ref.shape
+    size = count * tiles
+    total = sum(
+        factor_ref[pl.ds(r * per_row + per_row - size, size), :] for r in range(rows)
+    )
+    for k in range(count):
+        row = jnp.sum(total[k * tiles : (k + 1) * tiles], axis=0, keepdims=True)
+        for p in range(slabs):
+            sums_ref[p, pl.ds(k, 1), :] = row
 
 
 def rest_kernel(
@@ -214,20 +277,17 @@
     slice_ref,
     volume_ref,
     back_ref,
+    data_ref,
     new_ref,
     ready_ref,
-    sums_ref,
+    data_out,
 ):
     _, channels, rows, cols = cand_ref.shape
     tiles = cols // LANES
     rate = rate_ref[0]
     keep = keep_ref[0]
     image = factor_image(factor_ref, rows, tiles)
-    for k in range(2):
-        total = sum(image(len(index_pairs) + k, j) for j in range(tiles))
-        total = jnp.sum(total, axis=0, keepdims=True)
-        for p in range(sums_ref.shape[0]):
-            sums_ref[p, pl.ds(k, 1), :] = total
+    data_out[...] = data_ref[...]
     row_id = lax.broadcasted_iota(jnp.int32, (rows, LANES), 0)
     lane_id = lax.broadcasted_iota(jnp.int32, (rows, LANES), 1)
     before = [None] * channels
@@ -305,47 +365,69 @@
     image_form = jax.ShapeDtypeStruct(images, f32)
 
     following = from_behind(extrapolated, "slab", -1)
-    x_near, duals, own_sums = pl.pallas_call(
+    sinogram = (channels, rays // edge, edge)
+    x_near, duals, own_sums, measured_near, data_near = pl.pallas_call(
         own_kernel,
         out_shape=(
             kept_near(images),
             kept_near((3, *images)),
             kept_near((len(own_pairs), row_count, col_count)),
+            kept_near(sinogram),
+            kept_near(sinogram),
         ),
-        in_specs=[SMEM, ANY, ANY],
-        out_specs=(VMEM, VMEM, VMEM),
-        scratch_shapes=[pltpu.SemaphoreType.DMA((2, 4))],
+        in_specs=[SMEM] + [ANY] * 4,
+        out_specs=(VMEM,) * 5,
+        scratch_shapes=[pltpu.SemaphoreType.DMA((2, 4)), pltpu.SemaphoreType.DMA((2,))],
+        compiler_params=SCRATCH,
         name="own",
-    )(dual_step, extrapolated.reshape(images), dual_grad.reshape(3, *images))
-    x_near, candidate, partial_gram = pl.pallas_call(
+    )(
+        dual_step,
+        left_far(extrapolated.reshape(images)),
+        left_far(dual_grad.reshape(3, *images)),
+        left_far(measured.reshape(sinogram)),
+        left_far(dual_data.reshape(sinogram)),
+    )
+    x_near, candidate, partial_gram, projector_near = pl.pallas_call(
         gram_kernel,
         out_shape=(
             kept_near(images),
             kept_near((3, *images)),
             jax.ShapeDtypeStruct((row_count * held, LANES), f32),
+            pltpu.VMEM(projector.shape, projector.dtype),
         ),
-        in_specs=[SMEM, SMEM, VMEM, VMEM, VMEM, VMEM],
-        out_specs=(VMEM, VMEM, VMEM),
-        input_output_aliases={4: 0, 5: 1},
+        in_specs=[SMEM, SMEM, ANY, VMEM, VMEM, VMEM, VMEM],
+        out_specs=(VMEM,) * 4,
+        scratch_shapes=[pltpu.SemaphoreType.DMA(())],
+        input_output_aliases={5: 0, 6: 1},
+        compiler_params=SCRATCH,
         name="gram",
     )(
         dual_step,
         keep,
+        left_far(projector),
         near(following.reshape(images)),
         near(own_sums),
         near(x_near),
         near(duals),
     )
+    share_order = [by_distance(SHARE, (2, 1, 1))]
+    far_order = [by_distance((FAR,), (far_count // 2,))]
+    slab_order = [by_distance(("slab",), (1,))]
     gram_parts = lax.all_to_all(
-        partial_gram.reshape(share_count, held, LANES), SHARE, 0, 0, tiled=True
+        partial_gram.reshape(share_count, held, LANES),
+        SHARE,
+        0,
+        0,
+        axis_index_groups=share_order,
+        tiled=True,
     )
 
     rounded = x_near.reshape(channels, pixels // edge, edge).astype(jnp.bfloat16)
     picked = picked_blocks(rounded, tile_cols, pixels // edge)
-    products = jnp.einsum("tij,tbj->tbi", projector, picked, preferred_element_type=f32)
+    products = jnp.einsum("tij,tbj->tbi", projector_near, picked, preferred_element_type=f32)
     projected = gathered_products(products, tile_rows, rays // edge)
-    residual = projected - measured.reshape(projected.shape)
-    data_new = (dual_data.reshape(projected.shape) + dual_rate * residual) / (1.0 + dual_rate)
+    residual = projected - measured_near
+    data_new = (data_near + dual_rate * residual) / (1.0 + dual_rate)
     misfit_part = jnp.sum((residual * residual).reshape(-1, 8, LANES), axis=0)
 
     to_far, data_new = pl.pallas_call(
@@ -357,49 +439,55 @@
         in_specs=[VMEM, VMEM, VMEM],
         out_specs=(VMEM, VMEM),
         input_output_aliases={2: 1},
+        compiler_params=SCRATCH,
         name="pass_on",
     )(near(gram_parts), near(misfit_part), near(data_new))
-    far_parts = lax.all_to_all(to_far, FAR, 0, 0, tiled=True)
+    far_parts = lax.all_to_all(to_far, FAR, 0, 0, axis_index_groups=far_order, tiled=True)
 
     data_low = data_new.astype(jnp.bfloat16)
     picked_back = picked_blocks(data_low, tile_rows, rays // edge)
-    products_back = jnp.einsum("tij,tbi->tbj", projector, picked_back, preferred_element_type=f32)
+    products_back = jnp.einsum("tij,tbi->tbj", projector_near, picked_back, preferred_element_type=f32)
     back_proj = gathered_products(products_back, tile_cols, pixels // edge).reshape(
         volume_now.shape
     )
 
-    radius = reg_weight * math.sqrt(total_channels)
     to_share, back_proj = pl.pallas_call(
-        factor_kernel,
+        functools.partial(factor_kernel, total_channels),
         out_shape=(
-            jax.ShapeDtypeStruct((share_count, held + 2 * tiles, LANES), f32),
+            kept_near((share_count, held + 2 * tiles, LANES)),
             kept_near(images),
         ),
         in_specs=[SMEM, VMEM, VMEM],
         out_specs=(VMEM, VMEM),
         input_output_aliases={2: 1},
+        compiler_params=SCRATCH,
         name="factor",
-    )(radius, near(far_parts), near(back_proj.reshape(images)))
-    factor_rows = lax.all_to_all(to_share, SHARE, 0, 0, tiled=True)
+    )(reg_weight, near(far_parts), near(back_proj.reshape(images)))
+    factor_rows = lax.all_to_all(
+        to_share, SHARE, 0, 0, axis_index_groups=share_order, tiled=True
+    )
     factor_near = near(factor_rows.reshape(-1, LANES))
 
-    new_slice = pl.pallas_call(
+    new_slice, sums = pl.pallas_call(
         slice_kernel,
-        out_shape=kept_near(images),
+        out_shape=(kept_near(images), jax.ShapeDtypeStruct((slab_count, 2, LANES), f32)),
         in_specs=[VMEM, VMEM],
-        out_specs=VMEM,
+        out_specs=(VMEM, VMEM),
+        compiler_params=SCRATCH,
         name="slice",
     )(factor_near, near(candidate))
     prior_layer = from_behind(new_slice, "slab", 1)
-    grad_new, ready, sums = pl.pallas_call(
+    all_sums = lax.all_to_all(sums, "slab", 0, 0, axis_index_groups=slab_order, tiled=True)
+    grad_new, ready, data_out = pl.pallas_call(
         rest_kernel,
         out_shape=(
             jax.ShapeDtypeStruct((3, *images), f32),
             kept_near(images),
-            jax.ShapeDtypeStruct((slab_count, 2, LANES), f32),
+            jax.ShapeDtypeStruct(sinogram, f32),
         ),
-        in_specs=[SMEM, SMEM] + [VMEM] * 5,
+        in_specs=[SMEM, SMEM] + [VMEM] * 6,
         out_specs=(VMEM, VMEM, VMEM),
+        compiler_params=SCRATCH,
         name="rest",
     )(
         primal_step,
@@ -409,20 +497,21 @@
         near(new_slice),
         near(volume_now.reshape(images)),
         near(back_proj),
-    )
-    all_sums = lax.all_to_all(sums, "slab", 0, 0, tiled=True)
+        near(data_new),
+    )
     counts = (total_channels * slab_count * slices * rays, slab_count * slices * pixels)
     updated, totals = pl.pallas_call(
         functools.partial(finish_kernel, counts),
         out_shape=(image_form, jax.ShapeDtypeStruct((2,), f32)),
         in_specs=[SMEM, VMEM, VMEM, VMEM],
         out_specs=(VMEM, SMEM),
+        compiler_params=SCRATCH,
         name="finish",
     )(primal_step, near(ready), near(prior_layer), near(all_sums))
     return (
         updated.reshape(volume_now.shape),
         grad_new.reshape(dual_grad.shape),
-        data_new.reshape(dual_data.shape),
+        data_out.reshape(dual_data.shape),
         totals,
     )
 

time: 79.8 us -> 73.2 us (0.917)
  waiting for transfers between devices: 16.7 us -> 6.16 us
  starting transfers between devices: 37.2 us -> 41.4 us
  Pallas kernels: 6.25 us -> 7.58 us
  blocking collectives: 9.91 us -> 8.7 us
  matrix products: 5.48 us -> 4.41 us
  other arithmetic: 0.08 us -> 0.96 us
    all_to_all x2, waiting for transfers between devices: 15 us -> 6.15 us  [the longest x1 3.25 us: on_device(): lax.all_to_all(to_far, FAR, 0, 0, axis_index_groups=far_order, tiled=True)]
    all_to_all x2, starting transfers between devices: 17.1 us -> 20.2 us  [the longest x1 16.9 us: on_device(): lax.all_to_all(to_far, FAR, 0, 0, axis_index_groups=far_order, tiled=True)]
    all_to_all x1, starting transfers between devices: 5.26 us -> 7.02 us  [on_device(): lax.all_to_all(partial_gram.reshape(share_count, held, LANES), SHARE, 0,...]
    dot_general x2, matrix products: 3.55 us -> 1.83 us  [the longest x1 1.18 us: on_device(): jnp.einsum('tij,tbj->tbi', projector_near, picked, preferred_element_type...]
    all_to_all x1, waiting for transfers between devices: 1.66 us -> 0.01 us  [on_device(): lax.all_to_all(partial_gram.reshape(share_count, held, LANES), SHARE, 0,...]
    pallas_call x1, Pallas kernels: 0.91 us -> 2.28 us  [on_device(): pl.pallas_call(gram_kernel, out_shape=(kept_near(images), kept_near((3, *...]
    all_to_all x1, blocking collectives: 9.91 us -> 8.7 us  [on_device(): lax.all_to_all(to_share, SHARE, 0, 0, axis_index_groups=share_order, tile...]
    dot_general x2, matrix products: 0.45 us -> 1.36 us  [picked_blocks(): jnp.einsum('tc,bcj->tbj', chosen, blocks, preferred_element_type=jnp.floa...]
  transfers between devices with their start and end apart: 5 -> 5, of which waited for: 3 -> 2; matrix products, arithmetic and copies ran while one was open for 8% -> 7% of each run, Pallas kernels for 3% -> 4%
where the time goes in v5:
time: 73.2 us; the launch traced here: 72.7 us
  starting transfers between devices  41.4 us (57%)
  blocking collectives  8.7 us (12%)
  Pallas kernels  7.58 us (10%)
  waiting for transfers between devices  6.16 us (8%)
  matrix products  4.41 us (6%)
  between operations  2.71 us (4%)
  other arithmetic  0.96 us (1%)
  local copies, waits for them, and re-layouts  0.8 us (1%)
    all_to_all x1, starting transfers between devices, on_device(): lax.all_to_all(to_far, FAR, 0, 0, axis_index_groups=far_order, tiled=True)  16.9 us
    ppermute x2, starting transfers between devices, from_behind(): return lax.ppermute(block, axis, route)  14.2 us
    all_to_all x1, blocking collectives, on_device(): lax.all_to_all(to_share, SHARE, 0, 0, axis_index_groups=share_order, tile...  8.7 us
    all_to_all x1, starting transfers between devices, on_device(): lax.all_to_all(partial_gram.reshape(share_count, held, LANES), SHARE, 0,...  7.02 us
    all_to_all x1, starting transfers between devices, on_device(): lax.all_to_all(sums, 'slab', 0, 0, axis_index_groups=slab_order, tiled=True)  3.26 us
    all_to_all x1, waiting for transfers between devices, on_device(): lax.all_to_all(to_far, FAR, 0, 0, axis_index_groups=far_order, tiled=True)  3.25 us
    all_to_all x1, waiting for transfers between devices, on_device(): lax.all_to_all(sums, 'slab', 0, 0, axis_index_groups=slab_order, tiled=True)  2.9 us
    pallas_call x1, Pallas kernels, on_device(): pl.pallas_call(gram_kernel, out_shape=(kept_near(images), kept_near((3, *...  2.28 us
  transfers between devices with their start and end apart: 5, of which 2 were waited for; matrix products, arithmetic and copies ran while one was open for 7% of the time, Pallas kernels for 4%

profile of v5, /device:TPU:1, one launch (start us, length us, event | category | flops | bytes accessed | tf_op | source)
XLA Modules:
  0.0 72.7 jit_solution(2251088270897842319)
XLA Ops:
  0.6 8.8 %collective-permute-start = (f32[8,1,16,512]{3,2,0,1:T(8,128)}, f32[8,1,16,512]{3,2,0,1:T(8,128)S(1)}, u32[]{:S(2)}, u32[]{:S(2)}) collective-permute-start(f32[8,1,16,512]{3,2,0,1:T(8,128)} %bitcast.46), channel_id=1, source_target_pairs={{1,0},{2,1},{3,2},{5,4},{6,5},{7,6},{9,8},{10,9},{11,10},{13,12},{... | collective-permute-start | bytes 786440 | tf_op jit(solution)/shard_map/ppermute | solution.py:57
  10.7 1.5 %own.1 = (f32[8,16,512]{2,1,0:T(8,128)S(1)}, f32[3,8,16,512]{3,2,1,0:T(8,128)S(1)}, f32[3,16,512]{2,1,0:T(8,128)S(1)}, f32[8,32,128]{2,1,0:T(8,128)S(1)}, f32[8,32,128]{2,1,0:T(8,128)S(1)}) custom-call(f32[1]{0:T(128)} %copy.41.rate_ref, f32[8,16,512]{2,1,0:T(8,128)} %bitcast.47, f32[3,8,16,512]{3,2,1,0:T(8,128)} %bitcast.44, f32[8,32,128]{2,1,0:T(8,128)} %bitcast.48, ...), custom_call_target="tpu_custom_call" | custom-call | tf_op jit(solution)/shard_map/own/pallas_call | solution.py:369
  12.3 0.0 collective-permute-done
  12.3 0.0 copy-start.1
  12.3 2.3 %gram.1 = (f32[8,16,512]{2,1,0:T(8,128)S(1)}, f32[3,8,16,512]{3,2,1,0:T(8,128)S(1)}, f32[384,128]{1,0:T(8,128)}, bf16[64,128,128]{2,1,0:T(8,128)(2,1)S(1)}) custom-call(f32[1]{0:T(128)} %copy.41.rate_ref, f32[1]{0:T(128)} %bitcast.keep_ref, bf16[64,128,128]{2,1,0:T(8,128)(2,1)} %projector_far.1, ...), custom_call_target="tpu_custom_call", output_to_operand_aliasing={{0}: (5, {}), {1}: (6, {})} | custom-call | tf_op jit(solution)/shard_map/gram/pallas_call | solution.py:390
  14.6 0.0 copy-start.2
  14.6 0.7 %convert_element_type.20 = bf16[8,64,128]{2,1,0:T(8,128)(2,1)} reshape(bf16[8,16,512]{2,1,0:T(8,128)(2,1)S(1)} %convert_element_type.19) | data formatting | bytes 262144 | tf_op jit(solution)/shard_map/convert_element_type | solution.py:425
  15.3 7.0 %all-to-all-start = ((f32[16,24,128]{2,1,0:T(8,128)}), f32[16,24,128]{2,1,0:T(8,128)S(1)}, u32[]{:S(2)}, u32[]{:S(2)}) async-start(f32[16,24,128]{2,1,0:T(8,128)} %bitcast.7), calls=%async_computation | async-start | bytes 393216 | tf_op jit(solution)/shard_map/all_to_all | solution.py:416
  22.4 0.0 copy-done.1
  22.4 1.1 %fusion.9 = bf16[64,8,128]{2,0,1:T(8,128)(2,1)S(1)} fusion(bf16[8,64,128]{2,1,0:T(8,128)(2,1)} %convert_element_type.20, s32[64]{0:T(128)S(1)} %copy-done.1), kind=kOutput, calls=%fused_computation.14 | convolution fusion | flops 8392704 | bytes 262400 | tf_op jit(solution)/shard_map/tc,bcj->tbj/dot_general | solution.py:327
  23.5 1.2 %fusion.3 = f32[64,8,128]{2,1,0:T(8,128)S(1)} fusion(bf16[64,128,128]{2,1,0:T(8,128)(2,1)S(1)} %get-tuple-element.29, bf16[64,8,128]{2,0,1:T(8,128)(2,1)S(1)} %fusion.9), kind=kOutput, calls=%fused_computation.7 | convolution fusion | flops 16777216 | bytes 2490368 | tf_op jit(solution)/shard_map/tij,tbj->tbi/dot_general | solution.py:427
  24.7 0.0 copy-done.2
  24.7 0.9 %add_divide_fusion = (f32[8,32,128]{2,1,0:T(8,128)S(1)}, f32[8,32,128]{2,1,0:T(8,128)}) fusion(f32[8,32,128]{2,1,0:T(8,128)S(1)} %get-tuple-element.31, f32[]{:T(128)S(6)} %add.7, f32[]{:T(128)} %bitcast.38, f32[8,32,128]{2,1,0:T(8,128)S(1)} %get-tuple-element.30, s32[64]{0:T(128)S(1)} %copy-done.2, f32[64,8,128]{2,1,0:T(8,128)S(1)} %fusion.3), kind=kOutput, calls=%fused_computation.9 | convolution fusion | flops 25331712 | bytes 786696 | tf_op jit(solution)/shard_map/tc,tbj->bcj/dot_general | solution.py:334
  25.6 0.9 %reduce_sum.9.misfit_ref = f32[8,128]{1,0:T(8,128)S(1)} reduce(f32[32,8,128]{2,1,0:T(8,128)} %bitcast.45, f32[]{:T(128)} %constant.2.clone.1), dimensions={0}, to_apply=%region_0.1 | reduce | flops 31744 | bytes 135172 | tf_op jit(solution)/shard_map/reduce_sum | solution.py:431
  26.6 0.0 all-to-all-done.parts_ref
  26.6 0.7 pass_on.1
  27.3 0.2 fusion.5
  27.5 16.9 %all-to-all-start.1 = ((f32[8,32,128]{2,1,0:T(8,128)}), f32[8,32,128]{2,1,0:T(8,128)S(1)}, u32[]{:S(2)}, u32[]{:S(2)}) async-start(f32[8,32,128]{2,1,0:T(8,128)} %get-tuple-element.32), calls=%async_computation.1 | async-start | bytes 262144 | tf_op jit(solution)/shard_map/all_to_all | solution.py:445
  44.4 0.6 fusion.4
  45.1 0.0 copy-start
  45.1 0.3 convolution_bitcast_fusion
  45.4 3.3 %all-to-all-done.1.parts_ref = f32[8,32,128]{2,1,0:T(8,128)S(1)} async-done(((f32[8,32,128]{2,1,0:T(8,128)}), f32[8,32,128]{2,1,0:T(8,128)S(1)}, u32[]{:S(2)}, u32[]{:S(2)}) %all-to-all-start.1) | async-done | bytes 131104 | tf_op jit(solution)/shard_map/all_to_all | solution.py:445
  48.7 0.5 factor.1
  49.2 8.7 %all_to_all.20 = f32[16,32,128]{2,1,0:T(8,128)S(1)} all-to-all(f32[16,32,128]{2,1,0:T(8,128)S(1)} %get-tuple-element.34), channel_id=1, replica_groups={{324,0,4,64,128,384,68,132,192,256,388,448,196,260,320,452},{325,1,5,65..., dimensions={0} | all-to-all | bytes 524288 | tf_op jit(solution)/shard_map/all_to_all | solution.py:466
  57.9 0.7 slice.1
  58.6 5.4 %collective-permute-start.1 = (f32[8,16,512]{2,1,0:T(8,128)S(1)}, f32[8,16,512]{2,1,0:T(8,128)S(1)}, u32[]{:S(2)}, u32[]{:S(2)}) collective-permute-start(f32[8,16,512]{2,1,0:T(8,128)S(1)} %get-tuple-element.36.slice_ref), channel_id=1, source_target_pairs={{0,1},{1,2},{2,3},{4,5},{5,6},{6,7},{8,9},{9,10},{10,11},{12,13},{... | collective-permute-start | bytes 786440 | tf_op jit(solution)/shard_map/ppermute | solution.py:57
  64.0 3.3 %all-to-all-start.3 = ((f32[4,2,128]{2,1,0:T(2,128)}), f32[4,2,128]{2,1,0:T(2,128)S(1)}, u32[]{:S(2)}, u32[]{:S(2)}) async-start(f32[4,2,128]{2,1,0:T(2,128)} %get-tuple-element.39), calls=%async_computation.3 | async-start | bytes 8192 | tf_op jit(solution)/shard_map/all_to_all | solution.py:480
  67.9 0.0 copy-done
  67.9 1.1 %rest.1 = (f32[3,8,16,512]{3,2,1,0:T(8,128)}, f32[8,16,512]{2,1,0:T(8,128)S(1)}, f32[8,32,128]{2,1,0:T(8,128)}) custom-call(f32[1]{0:T(128)S(6)} %copy.42.rate_ref, f32[1]{0:T(128)} %bitcast.keep_ref, f32[512,128]{1,0:T(8,128)S(1)} %bitcast.41, f32[3,8,16,512]{3,2,1,0:T(8,128)S(1)} %get-tuple-element.35.cand_ref, ...), custom_call_target="tpu_custom_call" | custom-call | tf_op jit(solution)/shard_map/rest/pallas_call | solution.py:481
  69.1 2.9 %all-to-all-done.3.sums_ref = f32[4,2,128]{2,1,0:T(2,128)S(1)} async-done(((f32[4,2,128]{2,1,0:T(2,128)}), f32[4,2,128]{2,1,0:T(2,128)S(1)}, u32[]{:S(2)}, u32[]{:S(2)}) %all-to-all-start.3) | async-done | bytes 4128 | tf_op jit(solution)/shard_map/all_to_all | solution.py:480
  72.0 0.0 collective-permute-done.1.prior_ref
  72.0 0.7 %finish.1 = (f32[8,16,512]{2,1,0:T(8,128)}, f32[2]{0:T(128)}) custom-call(f32[1]{0:T(128)S(6)} %copy.42.rate_ref, f32[8,16,512]{2,1,0:T(8,128)S(1)} %get-tuple-element.38.ready_ref, f32[8,16,512]{2,1,0:T(8,128)S(1)} %collective-permute-done.1.prior_ref, f32[4,2,128]{2,1,0:T(2,128)S(1)} %all-to-all-done.3.sums_ref), custom_call_target="tpu_custom_call" | custom-call | tf_op jit(solution)/shard_map/finish/pallas_call | solution.py:503
  (2 shorter events, 0.1 us)
Async XLA Ops:
  0.6 11.6 %collective-permute-start = (f32[8,1,16,512]{3,2,0,1:T(8,128)}, f32[8,1,16,512]{3,2,0,1:T(8,128)S(1)}, u32[]{:S(2)}, u32[]{:S(2)}) collective-permute-start(f32[8,1,16,512]{3,2,0,1:T(8,128)} %bitcast.46), channel_id=1, source_target_pairs={{1,0},{2,1},{3,2},{5,4},{6,5},{7,6},{9,8},{10,9},{11,10},{13,12},{... | collective-permute-start | bytes 786440 | tf_op jit(solution)/shard_map/ppermute | solution.py:57
  12.3 10.1 %copy-start.1 = (s32[64]{0:T(128)S(1)}, s32[64]{0:T(128)}, u32[]{:S(2)}) copy-start(s32[64]{0:T(128)} %param.18) | copy-start | bytes 772
  14.6 10.1 %copy-start.2 = (s32[64]{0:T(128)S(1)}, s32[64]{0:T(128)}, u32[]{:S(2)}) copy-start(s32[64]{0:T(128)} %param.17) | copy-start | bytes 772
  15.3 11.2 %all-to-all-start = ((f32[16,24,128]{2,1,0:T(8,128)}), f32[16,24,128]{2,1,0:T(8,128)S(1)}, u32[]{:S(2)}, u32[]{:S(2)}) async-start(f32[16,24,128]{2,1,0:T(8,128)} %bitcast.7), calls=%async_computation | async-start | bytes 393216 | tf_op jit(solution)/shard_map/all_to_all | solution.py:416
  27.5 21.2 %all-to-all-start.1 = ((f32[8,32,128]{2,1,0:T(8,128)}), f32[8,32,128]{2,1,0:T(8,128)S(1)}, u32[]{:S(2)}, u32[]{:S(2)}) async-start(f32[8,32,128]{2,1,0:T(8,128)} %get-tuple-element.32), calls=%async_computation.1 | async-start | bytes 262144 | tf_op jit(solution)/shard_map/all_to_all | solution.py:445
  45.1 22.8 %copy-start = (f32[8,1,16,512]{3,2,1,0:T(8,128)S(1)}, f32[8,1,16,512]{3,2,1,0:T(8,128)}, u32[]{:S(2)}) copy-start(f32[8,1,16,512]{3,2,1,0:T(8,128)} %param.11) | copy-start | bytes 786436
  58.6 13.4 %collective-permute-start.1 = (f32[8,16,512]{2,1,0:T(8,128)S(1)}, f32[8,16,512]{2,1,0:T(8,128)S(1)}, u32[]{:S(2)}, u32[]{:S(2)}) collective-permute-start(f32[8,16,512]{2,1,0:T(8,128)S(1)} %get-tuple-element.36.slice_ref), channel_id=1, source_target_pairs={{0,1},{1,2},{2,3},{4,5},{5,6},{6,7},{8,9},{9,10},{10,11},{12,13},{... | collective-permute-start | bytes 786440 | tf_op jit(solution)/shard_map/ppermute | solution.py:57
  64.0 8.0 %all-to-all-start.3 = ((f32[4,2,128]{2,1,0:T(2,128)}), f32[4,2,128]{2,1,0:T(2,128)S(1)}, u32[]{:S(2)}, u32[]{:S(2)}) async-start(f32[4,2,128]{2,1,0:T(2,128)} %get-tuple-element.39), calls=%async_computation.3 | async-start | bytes 8192 | tf_op jit(solution)/shard_map/all_to_all | solution.py:480

commit v6 on v5

--- a/solution.py
+++ b/solution.py
@@ -61,15 +61,13 @@
     rate_ref,
     x_far,
     dual_far,
-    measured_far,
-    data_far,
+    projector_far,
     x_ref,
     cand_ref,
     sums_ref,
-    measured_ref,
-    data_ref,
+    projector_ref,
     arrived,
-    data_arrived,
+    projector_arrived,
 ):
     channels, rows, cols = x_ref.shape
     tiles = cols // LANES
@@ -88,11 +86,17 @@
         )
         for copy in copies[-1]:
             copy.start()
-    data_copies = (
-        pltpu.make_async_copy(measured_far, measured_ref, data_arrived.at[0]),
-        pltpu.make_async_copy(data_far, data_ref, data_arrived.at[1]),
-    )
-    for copy in data_copies:
+    projector_copies = []
+    pieces = projector_arrived.shape[0]
+    size_in = projector_ref.shape[0] // pieces
+    for piece in range(pieces):
+        some = pl.ds(piece * size_in, size_in)
+        projector_copies.append(
+            pltpu.make_async_copy(
+                projector_far.at[some], projector_ref.at[some], projector_arrived.at[piece]
+            )
+        )
+    for copy in projector_copies:
         copy.start()
     rate = rate_ref[0]
     inner_row = lax.broadcasted_iota(jnp.int32, (rows, LANES), 0) < rows - 1
@@ -124,14 +128,13 @@
                 sums = [s + cand[a] * cand[b] for s, (a, b) in zip(sums, own_pairs)]
             for k, s in enumerate(sums):
                 sums_ref[k, :, here] = s
-    for copy in data_copies:
+    for copy in projector_copies:
         copy.wait()
 
 
 def gram_kernel(
     rate_ref,
     keep_ref,
-    projector_far,
     next_ref,
     sums_ref,
     x_ref,
@@ -139,11 +142,7 @@
     x_same,
     cand_ref,
     out_ref,
-    projector_ref,
-    arrived,
 ):
-    projector_copy = pltpu.make_async_copy(projector_far, projector_ref, arrived)
-    projector_copy.start()
     channels, rows, cols = x_ref.shape
     tiles = cols // LANES
     per_row = len(index_pairs) * tiles
@@ -163,15 +162,18 @@
             cand_ref[2, c, :, here] = cand
         for k, pair in enumerate(index_pairs):
             out_ref[pl.ds(k * tiles + j, rows, stride=per_row), :] = sums[pair]
-    projector_copy.wait()
-
-
-def pass_on_kernel(parts_ref, misfit_ref, data_ref, out_ref, data_same):
+
+
+def pass_on_kernel(parts_ref, residual_ref, data_ref, out_ref, data_same):
     peers, per_row, _ = parts_ref.shape
     total = parts_ref[0]
     for p in range(1, peers):
         total = total + parts_ref[p]
-    misfit = misfit_ref[...]
+    misfit = jnp.zeros((out_ref.shape[1] - per_row, LANES), jnp.float32)
+    for c in range(residual_ref.shape[0]):
+        for start in range(0, residual_ref.shape[1], misfit.shape[0]):
+            some = residual_ref[c, pl.ds(start, misfit.shape[0]), :]
+            misfit = misfit + some * some
     for p in range(out_ref.shape[0]):
         out_ref[p, :per_row, :] = total
         out_ref[p, per_row:, :] = misfit
@@ -366,45 +368,40 @@
 
     following = from_behind(extrapolated, "slab", -1)
     sinogram = (channels, rays // edge, edge)
-    x_near, duals, own_sums, measured_near, data_near = pl.pallas_call(
+    x_near, duals, own_sums, projector_near = pl.pallas_call(
         own_kernel,
         out_shape=(
             kept_near(images),
             kept_near((3, *images)),
             kept_near((len(own_pairs), row_count, col_count)),
-            kept_near(sinogram),
-            kept_near(sinogram),
+            pltpu.VMEM(projector.shape, projector.dtype),
         ),
-        in_specs=[SMEM] + [ANY] * 4,
-        out_specs=(VMEM,) * 5,
-        scratch_shapes=[pltpu.SemaphoreType.DMA((2, 4)), pltpu.SemaphoreType.DMA((2,))],
+        in_specs=[SMEM] + [ANY] * 3,
+        out_specs=(VMEM,) * 4,
+        scratch_shapes=[pltpu.SemaphoreType.DMA(n) for n in ((2, 4), (8,))],
         compiler_params=SCRATCH,
         name="own",
     )(
         dual_step,
         left_far(extrapolated.reshape(images)),
         left_far(dual_grad.reshape(3, *images)),
-        left_far(measured.reshape(sinogram)),
-        left_far(dual_data.reshape(sinogram)),
-    )
-    x_near, candidate, partial_gram, projector_near = pl.pallas_call(
+        left_far(projector),
+    )
+    x_near, candidate, partial_gram = pl.pallas_call(
         gram_kernel,
         out_shape=(
             kept_near(images),
             kept_near((3, *images)),
             jax.ShapeDtypeStruct((row_count * held, LANES), f32),
-            pltpu.VMEM(projector.shape, projector.dtype),
         ),
-        in_specs=[SMEM, SMEM, ANY, VMEM, VMEM, VMEM, VMEM],
-        out_specs=(VMEM,) * 4,
-        scratch_shapes=[pltpu.SemaphoreType.DMA(())],
-        input_output_aliases={5: 0, 6: 1},
+        in_specs=[SMEM, SMEM, VMEM, VMEM, VMEM, VMEM],
+        out_specs=(VMEM,) * 3,
+        input_output_aliases={4: 0, 5: 1},
         compiler_params=SCRATCH,
         name="gram",
     )(
         dual_step,
         keep,
-        left_far(projector),
         near(following.reshape(images)),
         near(own_sums),
         near(x_near),
@@ -412,7 +409,6 @@
     )
     share_order = [by_distance(SHARE, (2, 1, 1))]
     far_order = [by_distance((FAR,), (far_count // 2,))]
-    slab_order = [by_distance(("slab",), (1,))]
     gram_parts = lax.all_to_all(
         partial_gram.reshape(share_count, held, LANES),
         SHARE,
@@ -426,9 +422,8 @@
     picked = picked_blocks(rounded, tile_cols, pixels // edge)
     products = jnp.einsum("tij,tbj->tbi", projector_near, picked, preferred_element_type=f32)
     projected = gathered_products(products, tile_rows, rays // edge)
-    residual = projected - measured_near
-    data_new = (data_near + dual_rate * residual) / (1.0 + dual_rate)
-    misfit_part = jnp.sum((residual * residual).reshape(-1, 8, LANES), axis=0)
+    residual = projected - measured.reshape(sinogram)
+    data_new = (dual_data.reshape(sinogram) + dual_rate * residual) / (1.0 + dual_rate)
 
     to_far, data_new = pl.pallas_call(
         pass_on_kernel,
@@ -441,7 +436,7 @@
         input_output_aliases={2: 1},
         compiler_params=SCRATCH,
         name="pass_on",
-    )(near(gram_parts), near(misfit_part), near(data_new))
+    )(near(gram_parts), near(residual), near(data_new))
     far_parts = lax.all_to_all(to_far, FAR, 0, 0, axis_index_groups=far_order, tiled=True)
 
     data_low = data_new.astype(jnp.bfloat16)
@@ -477,7 +472,7 @@
         name="slice",
     )(factor_near, near(candidate))
     prior_layer = from_behind(new_slice, "slab", 1)
-    all_sums = lax.all_to_all(sums, "slab", 0, 0, axis_index_groups=slab_order, tiled=True)
+    all_sums = lax.all_to_all(sums, "slab", 0, 0, tiled=True)
     grad_new, ready, data_out = pl.pallas_call(
         rest_kernel,
         out_shape=(

time: 73.2 us -> 69.5 us (0.949)
  blocking collectives: 8.7 us -> 10.6 us
  starting transfers between devices: 41.4 us -> 39.5 us
  other arithmetic: 0.96 us -> 0.02 us
  Pallas kernels: 7.58 us -> 6.75 us
    all_to_all x1, blocking collectives: 8.7 us -> 10.6 us  [on_device(): lax.all_to_all(to_share, SHARE, 0, 0, axis_index_groups=share_order, tile...]
    all_to_all x1, waiting for transfers between devices: 2.9 us -> 1.33 us  [on_device(): all_sums = lax.all_to_all(sums, 'slab', 0, 0, tiled=True)]
    pallas_call x1, Pallas kernels: 2.28 us -> 0.91 us  [on_device(): pl.pallas_call(gram_kernel, out_shape=(kept_near(images), kept_near((3, *...]
    reduce_sum x1 -> x0, other arithmetic: 0.94 us -> none  [on_device(): misfit_part = jnp.sum((residual * residual).reshape(-1, 8, LANES), axis=0)]
    dot_general x2, matrix products: 1.36 us -> 0.45 us  [picked_blocks(): jnp.einsum('tc,bcj->tbj', chosen, blocks, preferred_element_type=jnp.floa...]
    ppermute x2, starting transfers between devices: 14.2 us -> 13.4 us  [from_behind(): return lax.ppermute(block, axis, route)]
  transfers between devices with their start and end apart: 5 -> 5, of which waited for: 2 -> 3; matrix products, arithmetic and copies ran while one was open for 7% -> 5% of each run, Pallas kernels for 4% -> 5%
where the time goes in v6:
time: 69.5 us; the launch traced here: 69 us
  starting transfers between devices  39.5 us (57%)
  blocking collectives  10.6 us (15%)
  Pallas kernels  6.75 us (10%)
  waiting for transfers between devices  5.57 us (8%)
  matrix products  3.75 us (5%)
  between operations  2.7 us (4%)
    all_to_all x1, starting transfers between devices, on_device(): lax.all_to_all(to_far, FAR, 0, 0, axis_index_groups=far_order, tiled=True)  16.3 us
    ppermute x2, starting transfers between devices, from_behind(): return lax.ppermute(block, axis, route)  13.4 us
    all_to_all x1, blocking collectives, on_device(): lax.all_to_all(to_share, SHARE, 0, 0, axis_index_groups=share_order, tile...  10.6 us
    all_to_all x1, starting transfers between devices, on_device(): lax.all_to_all(partial_gram.reshape(share_count, held, LANES), SHARE, 0,...  6.5 us
    all_to_all x1, waiting for transfers between devices, on_device(): lax.all_to_all(to_far, FAR, 0, 0, axis_index_groups=far_order, tiled=True)  3.61 us
    all_to_all x1, starting transfers between devices, on_device(): all_sums = lax.all_to_all(sums, 'slab', 0, 0, tiled=True)  3.25 us
    pallas_call x1, Pallas kernels, on_device(): pl.pallas_call(own_kernel, out_shape=(kept_near(images), kept_near((3, *i...  2.05 us
    dot_general x2, matrix products, gathered_products(): jnp.einsum('tc,tbj->bcj', chosen, products, precision=lax.Precision.HIGHEST)  1.47 us
  transfers between devices with their start and end apart: 5, of which 3 were waited for; matrix products, arithmetic and copies ran while one was open for 5% of the time, Pallas kernels for 5%

profile of v6, /device:TPU:1, one launch (start us, length us, event | category | flops | bytes accessed | tf_op | source)
XLA Modules:
  0.0 69.0 jit_solution(17028699565985732687)
XLA Ops:
  0.6 8.8 %collective-permute-start = (f32[8,1,16,512]{3,2,0,1:T(8,128)}, f32[8,1,16,512]{3,2,0,1:T(8,128)S(1)}, u32[]{:S(2)}, u32[]{:S(2)}) collective-permute-start(f32[8,1,16,512]{3,2,0,1:T(8,128)} %bitcast.44), channel_id=1, source_target_pairs={{1,0},{2,1},{3,2},{5,4},{6,5},{7,6},{9,8},{10,9},{11,10},{13,12},{... | collective-permute-start | bytes 786440 | tf_op jit(solution)/shard_map/ppermute | solution.py:57
  10.7 0.0 copy-start.2
  10.7 2.0 %own.1 = (f32[8,16,512]{2,1,0:T(8,128)S(1)}, f32[3,8,16,512]{3,2,1,0:T(8,128)S(1)}, f32[3,16,512]{2,1,0:T(8,128)S(1)}, bf16[64,128,128]{2,1,0:T(8,128)(2,1)S(1)}) custom-call(f32[1]{0:T(128)} %copy.41.rate_ref, f32[8,16,512]{2,1,0:T(8,128)} %bitcast.45, f32[3,8,16,512]{3,2,1,0:T(8,128)} %bitcast.43, bf16[64,128,128]{2,1,0:T(8,128)(2,1)} %projector_far.1), custom_call_target="tpu_custom_call" | custom-call | tf_op jit(solution)/shard_map/own/pallas_call | solution.py:371
  12.8 0.0 collective-permute-done
  12.8 0.9 %gram.1 = (f32[8,16,512]{2,1,0:T(8,128)S(1)}, f32[3,8,16,512]{3,2,1,0:T(8,128)S(1)}, f32[384,128]{1,0:T(8,128)}) custom-call(f32[1]{0:T(128)} %copy.41.rate_ref, f32[1]{0:T(128)} %bitcast.keep_ref, f32[8,16,512]{2,1,0:T(8,128)S(1)} %bitcast.42, f32[3,16,512]{2,1,0:T(8,128)S(1)} %get-tuple-element.22.sums_ref, ...), custom_call_target="tpu_custom_call", output_to_operand_aliasing={{0}: (4, {}), {1}: (5, {})} | custom-call | tf_op jit(solution)/shard_map/gram/pallas_call | solution.py:390
  13.7 0.0 copy-start.1
  13.7 0.0 copy-start.3
  13.7 0.1 convert_element_type.20
  13.8 6.5 %all-to-all-start = ((f32[16,24,128]{2,1,0:T(8,128)}), f32[16,24,128]{2,1,0:T(8,128)S(1)}, u32[]{:S(2)}, u32[]{:S(2)}) async-start(f32[16,24,128]{2,1,0:T(8,128)} %bitcast.5), calls=%async_computation | async-start | bytes 393216 | tf_op jit(solution)/shard_map/all_to_all | solution.py:412
  20.3 0.0 copy-done.2
  20.3 0.2 fusion.9
  20.6 1.2 %fusion.3 = f32[64,8,128]{2,1,0:T(8,128)S(1)} fusion(bf16[64,128,128]{2,1,0:T(8,128)(2,1)S(1)} %get-tuple-element.27, bf16[64,8,128]{2,0,1:T(8,128)(2,1)S(1)} %fusion.9), kind=kOutput, calls=%fused_computation.7 | convolution fusion | flops 16777216 | bytes 2490368 | tf_op jit(solution)/shard_map/tij,tbj->tbi/dot_general | solution.py:423
  21.7 0.0 copy-done.1
  21.7 0.0 copy-done.3
  21.8 1.2 %add_divide_fusion = (f32[8,32,128]{2,1,0:T(8,128)S(1)}, f32[8,32,128]{2,1,0:T(8,128)S(1)}) fusion(f32[8,32,128]{2,1,0:T(8,128)S(1)} %bitcast.46, f32[]{:T(128)S(6)} %add.7, f32[]{:T(128)} %bitcast.37, f32[8,32,128]{2,1,0:T(8,128)} %bitcast.47, s32[64]{0:T(128)S(1)} %copy-done.3, f32[64,8,128]{2,1,0:T(8,128)S(1)} %fusion.3), kind=kOutput, calls=%fused_computation.9 | convolution fusion | flops 25298944 | bytes 786696 | tf_op jit(solution)/shard_map/tc,tbj->bcj/dot_general | solution.py:336
  22.9 0.6 all-to-all-done.parts_ref
  23.6 0.7 %pass_on.1 = (f32[8,32,128]{2,1,0:T(8,128)}, f32[8,32,128]{2,1,0:T(8,128)S(1)}) custom-call(f32[16,24,128]{2,1,0:T(8,128)S(1)} %all-to-all-done.parts_ref, f32[8,32,128]{2,1,0:T(8,128)S(1)} %get-tuple-element.45.residual_ref, f32[8,32,128]{2,1,0:T(8,128)S(1)} %get-tuple-element.44.data_ref), custom_call_target="tpu_custom_call", output_to_operand_aliasing={{1}: (2, {})} | custom-call | tf_op jit(solution)/shard_map/pass_on/pallas_call | solution.py:428
  24.3 0.2 fusion.5
  24.5 16.3 %all-to-all-start.1 = ((f32[8,32,128]{2,1,0:T(8,128)}), f32[8,32,128]{2,1,0:T(8,128)S(1)}, u32[]{:S(2)}, u32[]{:S(2)}) async-start(f32[8,32,128]{2,1,0:T(8,128)} %get-tuple-element.28), calls=%async_computation.1 | async-start | bytes 262144 | tf_op jit(solution)/shard_map/all_to_all | solution.py:440
  40.8 0.6 fusion.4
  41.5 0.0 copy-start
  41.5 0.3 convolution_bitcast_fusion
  41.8 3.6 %all-to-all-done.1.parts_ref = f32[8,32,128]{2,1,0:T(8,128)S(1)} async-done(((f32[8,32,128]{2,1,0:T(8,128)}), f32[8,32,128]{2,1,0:T(8,128)S(1)}, u32[]{:S(2)}, u32[]{:S(2)}) %all-to-all-start.1) | async-done | bytes 131104 | tf_op jit(solution)/shard_map/all_to_all | solution.py:440
  45.4 0.5 factor.1
  45.9 10.6 %all_to_all.20 = f32[16,32,128]{2,1,0:T(8,128)S(1)} all-to-all(f32[16,32,128]{2,1,0:T(8,128)S(1)} %get-tuple-element.30), channel_id=1, replica_groups={{324,0,4,64,128,384,68,132,192,256,388,448,196,260,320,452},{325,1,5,65..., dimensions={0} | all-to-all | bytes 524288 | tf_op jit(solution)/shard_map/all_to_all | solution.py:461
  56.5 0.7 %slice.1 = (f32[8,16,512]{2,1,0:T(8,128)S(1)}, f32[4,2,128]{2,1,0:T(2,128)}) custom-call(f32[512,128]{1,0:T(8,128)S(1)} %bitcast.39, f32[3,8,16,512]{3,2,1,0:T(8,128)S(1)} %get-tuple-element.31.cand_ref), custom_call_target="tpu_custom_call" | custom-call | tf_op jit(solution)/shard_map/slice/pallas_call | solution.py:466
  57.3 4.6 %collective-permute-start.1 = (f32[8,16,512]{2,1,0:T(8,128)S(1)}, f32[8,16,512]{2,1,0:T(8,128)S(1)}, u32[]{:S(2)}, u32[]{:S(2)}) collective-permute-start(f32[8,16,512]{2,1,0:T(8,128)S(1)} %get-tuple-element.32.slice_ref), channel_id=1, source_target_pairs={{0,1},{1,2},{2,3},{4,5},{5,6},{6,7},{8,9},{9,10},{10,11},{12,13},{... | collective-permute-start | bytes 786440 | tf_op jit(solution)/shard_map/ppermute | solution.py:57
  61.9 3.2 %all-to-all-start.3 = ((f32[4,2,128]{2,1,0:T(2,128)}), f32[4,2,128]{2,1,0:T(2,128)S(1)}, u32[]{:S(2)}, u32[]{:S(2)}) async-start(f32[4,2,128]{2,1,0:T(2,128)} %get-tuple-element.35), calls=%async_computation.3 | async-start | bytes 8192 | tf_op jit(solution)/shard_map/all_to_all | solution.py:475
  65.8 0.0 copy-done
  65.8 1.1 %rest.1 = (f32[3,8,16,512]{3,2,1,0:T(8,128)}, f32[8,16,512]{2,1,0:T(8,128)S(1)}, f32[8,32,128]{2,1,0:T(8,128)}) custom-call(f32[1]{0:T(128)S(6)} %copy.42.rate_ref, f32[1]{0:T(128)} %bitcast.keep_ref, f32[512,128]{1,0:T(8,128)S(1)} %bitcast.40, f32[3,8,16,512]{3,2,1,0:T(8,128)S(1)} %get-tuple-element.31.cand_ref, ...), custom_call_target="tpu_custom_call" | custom-call | tf_op jit(solution)/shard_map/rest/pallas_call | solution.py:476
  66.9 1.3 %all-to-all-done.3.sums_ref = f32[4,2,128]{2,1,0:T(2,128)S(1)} async-done(((f32[4,2,128]{2,1,0:T(2,128)}), f32[4,2,128]{2,1,0:T(2,128)S(1)}, u32[]{:S(2)}, u32[]{:S(2)}) %all-to-all-start.3) | async-done | bytes 4128 | tf_op jit(solution)/shard_map/all_to_all | solution.py:475
  68.3 0.0 collective-permute-done.1.prior_ref
  68.3 0.7 %finish.1 = (f32[8,16,512]{2,1,0:T(8,128)}, f32[2]{0:T(128)}) custom-call(f32[1]{0:T(128)S(6)} %copy.42.rate_ref, f32[8,16,512]{2,1,0:T(8,128)S(1)} %get-tuple-element.34.ready_ref, f32[8,16,512]{2,1,0:T(8,128)S(1)} %collective-permute-done.1.prior_ref, f32[4,2,128]{2,1,0:T(2,128)S(1)} %all-to-all-done.3.sums_ref), custom_call_target="tpu_custom_call" | custom-call | tf_op jit(solution)/shard_map/finish/pallas_call | solution.py:498
  (2 shorter events, 0.1 us)
Async XLA Ops:
  0.6 12.2 %collective-permute-start = (f32[8,1,16,512]{3,2,0,1:T(8,128)}, f32[8,1,16,512]{3,2,0,1:T(8,128)S(1)}, u32[]{:S(2)}, u32[]{:S(2)}) collective-permute-start(f32[8,1,16,512]{3,2,0,1:T(8,128)} %bitcast.44), channel_id=1, source_target_pairs={{1,0},{2,1},{3,2},{5,4},{6,5},{7,6},{9,8},{10,9},{11,10},{13,12},{... | collective-permute-start | bytes 786440 | tf_op jit(solution)/shard_map/ppermute | solution.py:57
  10.7 9.6 %copy-start.2 = (s32[64]{0:T(128)S(1)}, s32[64]{0:T(128)}, u32[]{:S(2)}) copy-start(s32[64]{0:T(128)} %param.18) | copy-start | bytes 772
  13.7 8.0 %copy-start.1 = (f32[8,1,4096]{2,1,0:T(1,128)S(1)}, f32[8,1,4096]{2,1,0:T(1,128)}, u32[]{:S(2)}) copy-start(f32[8,1,4096]{2,1,0:T(1,128)} %param.14) | copy-start | bytes 393220
  13.7 8.0 %copy-start.3 = (s32[64]{0:T(128)S(1)}, s32[64]{0:T(128)}, u32[]{:S(2)}) copy-start(s32[64]{0:T(128)} %param.17) | copy-start | bytes 772
  13.8 9.7 %all-to-all-start = ((f32[16,24,128]{2,1,0:T(8,128)}), f32[16,24,128]{2,1,0:T(8,128)S(1)}, u32[]{:S(2)}, u32[]{:S(2)}) async-start(f32[16,24,128]{2,1,0:T(8,128)} %bitcast.5), calls=%async_computation | async-start | bytes 393216 | tf_op jit(solution)/shard_map/all_to_all | solution.py:412
  24.5 20.9 %all-to-all-start.1 = ((f32[8,32,128]{2,1,0:T(8,128)}), f32[8,32,128]{2,1,0:T(8,128)S(1)}, u32[]{:S(2)}, u32[]{:S(2)}) async-start(f32[8,32,128]{2,1,0:T(8,128)} %get-tuple-element.28), calls=%async_computation.1 | async-start | bytes 262144 | tf_op jit(solution)/shard_map/all_to_all | solution.py:440
  41.5 24.3 %copy-start = (f32[8,1,16,512]{3,2,1,0:T(8,128)S(1)}, f32[8,1,16,512]{3,2,1,0:T(8,128)}, u32[]{:S(2)}) copy-start(f32[8,1,16,512]{3,2,1,0:T(8,128)} %param.11) | copy-start | bytes 786436
  57.3 11.0 %collective-permute-start.1 = (f32[8,16,512]{2,1,0:T(8,128)S(1)}, f32[8,16,512]{2,1,0:T(8,128)S(1)}, u32[]{:S(2)}, u32[]{:S(2)}) collective-permute-start(f32[8,16,512]{2,1,0:T(8,128)S(1)} %get-tuple-element.32.slice_ref), channel_id=1, source_target_pairs={{0,1},{1,2},{2,3},{4,5},{5,6},{6,7},{8,9},{9,10},{10,11},{12,13},{... | collective-permute-start | bytes 786440 | tf_op jit(solution)/shard_map/ppermute | solution.py:57
  61.9 6.4 %all-to-all-start.3 = ((f32[4,2,128]{2,1,0:T(2,128)}), f32[4,2,128]{2,1,0:T(2,128)S(1)}, u32[]{:S(2)}, u32[]{:S(2)}) async-start(f32[4,2,128]{2,1,0:T(2,128)} %get-tuple-element.35), calls=%async_computation.3 | async-start | bytes 8192 | tf_op jit(solution)/shard_map/all_to_all | solution.py:475

commit v7 on v6

--- a/solution.py
+++ b/solution.py
@@ -164,7 +164,7 @@
             out_ref[pl.ds(k * tiles + j, rows, stride=per_row), :] = sums[pair]
 
 
-def pass_on_kernel(parts_ref, residual_ref, data_ref, out_ref, data_same):
+def pass_on_kernel(weight_ref, parts_ref, residual_ref, back_ref, out_ref, back_same):
     peers, per_row, _ = parts_ref.shape
     total = parts_ref[0]
     for p in range(1, peers):
@@ -207,7 +207,7 @@
     return entry, vectors
 
 
-def factor_kernel(channels, weight_ref, parts_ref, back_ref, out_ref, back_same):
+def factor_kernel(channels, weight_ref, parts_ref, out_ref):
     peers, held, _ = parts_ref.shape
     entries = len(index_pairs)
     tiles = out_ref.shape[1] // (entries + 2)
@@ -313,10 +313,13 @@
             ready_ref[c, :, here] = volume_ref[c, :, here] - rate * (back_ref[c, :, here] - spread)
 
 
-def finish_kernel(counts, rate_ref, ready_ref, prior_ref, sums_ref, updated_ref, totals_ref):
+def finish_kernel(rate_ref, ready_ref, prior_ref, updated_ref):
     rate = rate_ref[0]
     for c in range(ready_ref.shape[0]):
         updated_ref[c] = jnp.maximum(ready_ref[c] - rate * prior_ref[c], 0.0)
+
+
+def totals_kernel(counts, sums_ref, updated_far, totals_ref):
     total = sums_ref[0]
     for p in range(1, sums_ref.shape[0]):
         total = total + sums_ref[p]
@@ -408,7 +411,7 @@
         near(duals),
     )
     share_order = [by_distance(SHARE, (2, 1, 1))]
-    far_order = [by_distance((FAR,), (far_count // 2,))]
+    far_order = [by_distance((FAR,), (far_count // 2 + 1,))]
     gram_parts = lax.all_to_all(
         partial_gram.reshape(share_count, held, LANES),
         SHARE,
@@ -425,39 +428,34 @@
     residual = projected - measured.reshape(sinogram)
     data_new = (dual_data.reshape(sinogram) + dual_rate * residual) / (1.0 + dual_rate)
 
-    to_far, data_new = pl.pallas_call(
-        pass_on_kernel,
-        out_shape=(
-            jax.ShapeDtypeStruct((far_count, held + 8, LANES), f32),
-            kept_near(data_new.shape),
-        ),
-        in_specs=[VMEM, VMEM, VMEM],
-        out_specs=(VMEM, VMEM),
-        input_output_aliases={2: 1},
-        compiler_params=SCRATCH,
-        name="pass_on",
-    )(near(gram_parts), near(residual), near(data_new))
-    far_parts = lax.all_to_all(to_far, FAR, 0, 0, axis_index_groups=far_order, tiled=True)
-
     data_low = data_new.astype(jnp.bfloat16)
     picked_back = picked_blocks(data_low, tile_rows, rays // edge)
     products_back = jnp.einsum("tij,tbi->tbj", projector_near, picked_back, preferred_element_type=f32)
     back_proj = gathered_products(products_back, tile_cols, pixels // edge).reshape(
         volume_now.shape
     )
-
-    to_share, back_proj = pl.pallas_call(
-        functools.partial(factor_kernel, total_channels),
+    to_far, back_proj = pl.pallas_call(
+        pass_on_kernel,
         out_shape=(
-            kept_near((share_count, held + 2 * tiles, LANES)),
+            jax.ShapeDtypeStruct((far_count, held + 8, LANES), f32),
             kept_near(images),
         ),
-        in_specs=[SMEM, VMEM, VMEM],
+        in_specs=[SMEM, VMEM, VMEM, VMEM],
         out_specs=(VMEM, VMEM),
-        input_output_aliases={2: 1},
+        input_output_aliases={3: 1},
+        compiler_params=SCRATCH,
+        name="pass_on",
+    )(reg_weight, near(gram_parts), near(residual), near(back_proj.reshape(images)))
+    far_parts = lax.all_to_all(to_far, FAR, 0, 0, axis_index_groups=far_order, tiled=True)
+
+    to_share = pl.pallas_call(
+        functools.partial(factor_kernel, total_channels),
+        out_shape=kept_near((share_count, held + 2 * tiles, LANES)),
+        in_specs=[SMEM, VMEM],
+        out_specs=VMEM,
         compiler_params=SCRATCH,
         name="factor",
-    )(reg_weight, near(far_parts), near(back_proj.reshape(images)))
+    )(reg_weight, near(far_parts))
     factor_rows = lax.all_to_all(
         to_share, SHARE, 0, 0, axis_index_groups=share_order, tiled=True
     )
@@ -495,14 +493,22 @@
         near(data_new),
     )
     counts = (total_channels * slab_count * slices * rays, slab_count * slices * pixels)
-    updated, totals = pl.pallas_call(
-        functools.partial(finish_kernel, counts),
-        out_shape=(image_form, jax.ShapeDtypeStruct((2,), f32)),
-        in_specs=[SMEM, VMEM, VMEM, VMEM],
-        out_specs=(VMEM, SMEM),
+    updated = pl.pallas_call(
+        finish_kernel,
+        out_shape=image_form,
+        in_specs=[SMEM, VMEM, VMEM],
+        out_specs=VMEM,
         compiler_params=SCRATCH,
         name="finish",
-    )(primal_step, near(ready), near(prior_layer), near(all_sums))
+    )(primal_step, near(ready), near(prior_layer))
+    totals = pl.pallas_call(
+        functools.partial(totals_kernel, counts),
+        out_shape=jax.ShapeDtypeStruct((2,), f32),
+        in_specs=[VMEM, ANY],
+        out_specs=SMEM,
+        compiler_params=SCRATCH,
+        name="totals",
+    )(near(all_sums), left_far(updated))
     return (
         updated.reshape(volume_now.shape),
         grad_new.reshape(dual_grad.shape),

time: 69.5 us -> 67.5 us (0.971)
  blocking collectives: 10.6 us -> 29.8 us
  starting transfers between devices: 39.5 us -> 23.3 us
  waiting for transfers between devices: 5.57 us -> 0.63 us
    all_to_all x0 -> x1, blocking collectives: none -> 19.9 us  [on_device(): lax.all_to_all(to_far, FAR, 0, 0, axis_index_groups=far_order, tiled=True)]
    all_to_all x1 -> x0, starting transfers between devices: 16.3 us -> none  [on_device(): lax.all_to_all(to_far, FAR, 0, 0, axis_index_groups=far_order, tiled=True)]
    all_to_all x1 -> x0, waiting for transfers between devices: 3.61 us -> none  [on_device(): lax.all_to_all(to_far, FAR, 0, 0, axis_index_groups=far_order, tiled=True)]
    all_to_all x1, blocking collectives: 10.6 us -> 9.87 us  [on_device(): lax.all_to_all(to_share, SHARE, 0, 0, axis_index_groups=share_order, tile...]
    all_to_all x1, waiting for transfers between devices: 1.33 us -> 0.62 us  [on_device(): all_sums = lax.all_to_all(sums, 'slab', 0, 0, tiled=True)]
  transfers between devices with their start and end apart: 5 -> 4, of which waited for: 3 -> 1; matrix products, arithmetic and copies ran while one was open for 5% -> 6% of each run, Pallas kernels for 5% -> 6%
where the time goes in v7:
time: 67.5 us; the launch traced here: 67.1 us
  blocking collectives  29.8 us (44%)
  starting transfers between devices  23.3 us (35%)
  Pallas kernels  6.72 us (10%)
  matrix products  3.76 us (6%)
  between operations  2.71 us (4%)
    all_to_all x1, blocking collectives, on_device(): lax.all_to_all(to_far, FAR, 0, 0, axis_index_groups=far_order, tiled=True)  19.9 us
    ppermute x2, starting transfers between devices, from_behind(): return lax.ppermute(block, axis, route)  13.6 us
    all_to_all x1, blocking collectives, on_device(): lax.all_to_all(to_share, SHARE, 0, 0, axis_index_groups=share_order, tile...  9.87 us
    all_to_all x1, starting transfers between devices, on_device(): lax.all_to_all(partial_gram.reshape(share_count, held, LANES), SHARE, 0,...  6.5 us
    all_to_all x1, starting transfers between devices, on_device(): all_sums = lax.all_to_all(sums, 'slab', 0, 0, tiled=True)  3.2 us
    pallas_call x1, Pallas kernels, on_device(): pl.pallas_call(own_kernel, out_shape=(kept_near(images), kept_near((3, *i...  2.05 us
    dot_general x2, matrix products, gathered_products(): jnp.einsum('tc,tbj->bcj', chosen, products, precision=lax.Precision.HIGHEST)  1.47 us
  transfers between devices with their start and end apart: 4, of which 1 were waited for; matrix products, arithmetic and copies ran while one was open for 6% of the time, Pallas kernels for 6%

profile of v7, /device:TPU:1, one launch (start us, length us, event | category | flops | bytes accessed | tf_op | source)
XLA Modules:
  0.0 67.1 jit_solution(15750187889768414292)
XLA Ops:
  0.6 8.8 %collective-permute-start = (f32[8,1,16,512]{3,2,0,1:T(8,128)}, f32[8,1,16,512]{3,2,0,1:T(8,128)S(1)}, u32[]{:S(2)}, u32[]{:S(2)}) collective-permute-start(f32[8,1,16,512]{3,2,0,1:T(8,128)} %bitcast.45), channel_id=1, source_target_pairs={{1,0},{2,1},{3,2},{5,4},{6,5},{7,6},{9,8},{10,9},{11,10},{13,12},{... | collective-permute-start | bytes 786440 | tf_op jit(solution)/shard_map/ppermute | solution.py:57
  10.7 0.0 copy-start.2
  10.7 2.0 %own.1 = (f32[8,16,512]{2,1,0:T(8,128)S(1)}, f32[3,8,16,512]{3,2,1,0:T(8,128)S(1)}, f32[3,16,512]{2,1,0:T(8,128)S(1)}, bf16[64,128,128]{2,1,0:T(8,128)(2,1)S(1)}) custom-call(f32[1]{0:T(128)} %copy.39.rate_ref, f32[8,16,512]{2,1,0:T(8,128)} %bitcast.46, f32[3,8,16,512]{3,2,1,0:T(8,128)} %bitcast.44, bf16[64,128,128]{2,1,0:T(8,128)(2,1)} %projector_far.1), custom_call_target="tpu_custom_call" | custom-call | tf_op jit(solution)/shard_map/own/pallas_call | solution.py:374
  12.8 0.0 collective-permute-done
  12.8 0.9 %gram.1 = (f32[8,16,512]{2,1,0:T(8,128)S(1)}, f32[3,8,16,512]{3,2,1,0:T(8,128)S(1)}, f32[384,128]{1,0:T(8,128)}) custom-call(f32[1]{0:T(128)} %copy.39.rate_ref, f32[1]{0:T(128)} %bitcast.keep_ref, f32[8,16,512]{2,1,0:T(8,128)S(1)} %bitcast.42, f32[3,16,512]{2,1,0:T(8,128)S(1)} %get-tuple-element.18.sums_ref, ...), custom_call_target="tpu_custom_call", output_to_operand_aliasing={{0}: (4, {}), {1}: (5, {})} | custom-call | tf_op jit(solution)/shard_map/gram/pallas_call | solution.py:393
  13.7 0.0 copy-start.1
  13.7 0.0 copy-start.3
  13.7 0.1 convert_element_type.20
  13.8 6.5 %all-to-all-start = ((f32[16,24,128]{2,1,0:T(8,128)}), f32[16,24,128]{2,1,0:T(8,128)S(1)}, u32[]{:S(2)}, u32[]{:S(2)}) async-start(f32[16,24,128]{2,1,0:T(8,128)} %bitcast.5), calls=%async_computation | async-start | bytes 393216 | tf_op jit(solution)/shard_map/all_to_all | solution.py:415
  20.3 0.0 copy-done.2
  20.3 0.2 fusion.9
  20.6 1.2 %fusion.3 = f32[64,8,128]{2,1,0:T(8,128)S(1)} fusion(bf16[64,128,128]{2,1,0:T(8,128)(2,1)S(1)} %get-tuple-element.23, bf16[64,8,128]{2,0,1:T(8,128)(2,1)S(1)} %fusion.9), kind=kOutput, calls=%fused_computation.7 | convolution fusion | flops 16777216 | bytes 2490368 | tf_op jit(solution)/shard_map/tij,tbj->tbi/dot_general | solution.py:426
  21.7 0.0 copy-done.1
  21.7 0.0 copy-done.3
  21.8 1.2 %add_divide_fusion = (f32[8,32,128]{2,1,0:T(8,128)S(1)}, f32[8,32,128]{2,1,0:T(8,128)S(1)}) fusion(f32[8,32,128]{2,1,0:T(8,128)S(1)} %bitcast.47, f32[]{:T(128)S(6)} %add.7, f32[]{:T(128)} %bitcast.37, f32[8,32,128]{2,1,0:T(8,128)} %bitcast.48, s32[64]{0:T(128)S(1)} %copy-done.3, f32[64,8,128]{2,1,0:T(8,128)S(1)} %fusion.3), kind=kOutput, calls=%fused_computation.9 | convolution fusion | flops 25298944 | bytes 786696 | tf_op jit(solution)/shard_map/tc,tbj->bcj/dot_general | solution.py:339
  22.9 0.2 fusion.5
  23.2 0.6 fusion.4
  23.8 0.0 copy-start
  23.8 0.3 convolution_bitcast_fusion
  24.2 0.0 all-to-all-done.parts_ref
  24.2 19.9 %all_to_all.20.parts_ref = f32[8,32,128]{2,1,0:T(8,128)S(1)} all-to-all(f32[8,32,128]{2,1,0:T(8,128)S(1)} %get-tuple-element.24), channel_id=1, replica_groups={{40,8,0,16,24,56,32,48},{41,9,1,17,25,57,33,49},{42,10,2,18,26,58,34,50..., dimensions={0} | all-to-all | bytes 262144 | tf_op jit(solution)/shard_map/all_to_all | solution.py:449
  44.1 0.5 factor.1
  44.6 9.9 %all_to_all.21 = f32[16,32,128]{2,1,0:T(8,128)S(1)} all-to-all(f32[16,32,128]{2,1,0:T(8,128)S(1)} %factor.1), channel_id=1, replica_groups={{324,0,4,64,128,384,68,132,192,256,388,448,196,260,320,452},{325,1,5,65..., dimensions={0} | all-to-all | bytes 524288 | tf_op jit(solution)/shard_map/all_to_all | solution.py:459
  54.5 0.7 %slice.1 = (f32[8,16,512]{2,1,0:T(8,128)S(1)}, f32[4,2,128]{2,1,0:T(2,128)}) custom-call(f32[512,128]{1,0:T(8,128)S(1)} %bitcast.39, f32[3,8,16,512]{3,2,1,0:T(8,128)S(1)} %get-tuple-element.25.cand_ref), custom_call_target="tpu_custom_call" | custom-call | tf_op jit(solution)/shard_map/slice/pallas_call | solution.py:464
  55.2 4.8 %collective-permute-start.1 = (f32[8,16,512]{2,1,0:T(8,128)S(1)}, f32[8,16,512]{2,1,0:T(8,128)S(1)}, u32[]{:S(2)}, u32[]{:S(2)}) collective-permute-start(f32[8,16,512]{2,1,0:T(8,128)S(1)} %get-tuple-element.26.slice_ref), channel_id=1, source_target_pairs={{0,1},{1,2},{2,3},{4,5},{5,6},{6,7},{8,9},{9,10},{10,11},{12,13},{... | collective-permute-start | bytes 786440 | tf_op jit(solution)/shard_map/ppermute | solution.py:57
  60.0 3.2 %all-to-all-start.3 = ((f32[4,2,128]{2,1,0:T(2,128)}), f32[4,2,128]{2,1,0:T(2,128)S(1)}, u32[]{:S(2)}, u32[]{:S(2)}) async-start(f32[4,2,128]{2,1,0:T(2,128)} %get-tuple-element.31), calls=%async_computation.3 | async-start | bytes 8192 | tf_op jit(solution)/shard_map/all_to_all | solution.py:473
  63.9 0.0 copy-done
  63.9 1.1 %rest.1 = (f32[3,8,16,512]{3,2,1,0:T(8,128)}, f32[8,16,512]{2,1,0:T(8,128)S(1)}, f32[8,32,128]{2,1,0:T(8,128)}) custom-call(f32[1]{0:T(128)S(6)} %copy.40.rate_ref, f32[1]{0:T(128)} %bitcast.keep_ref, f32[512,128]{1,0:T(8,128)S(1)} %bitcast.40, f32[3,8,16,512]{3,2,1,0:T(8,128)S(1)} %get-tuple-element.25.cand_ref, ...), custom_call_target="tpu_custom_call" | custom-call | tf_op jit(solution)/shard_map/rest/pallas_call | solution.py:474
  65.0 0.0 collective-permute-done.1.prior_ref
  65.0 0.7 %finish.1.updated_far = f32[8,16,512]{2,1,0:T(8,128)} custom-call(f32[1]{0:T(128)S(6)} %copy.40.rate_ref, f32[8,16,512]{2,1,0:T(8,128)S(1)} %get-tuple-element.28.ready_ref, f32[8,16,512]{2,1,0:T(8,128)S(1)} %collective-permute-done.1.prior_ref), custom_call_target="tpu_custom_call" | custom-call | tf_op jit(solution)/shard_map/finish/pallas_call | solution.py:496
  65.8 0.6 all-to-all-done.3.sums_ref
  66.4 0.6 totals.1
  (3 shorter events, 0.1 us)
Async XLA Ops:
  0.6 12.2 %collective-permute-start = (f32[8,1,16,512]{3,2,0,1:T(8,128)}, f32[8,1,16,512]{3,2,0,1:T(8,128)S(1)}, u32[]{:S(2)}, u32[]{:S(2)}) collective-permute-start(f32[8,1,16,512]{3,2,0,1:T(8,128)} %bitcast.45), channel_id=1, source_target_pairs={{1,0},{2,1},{3,2},{5,4},{6,5},{7,6},{9,8},{10,9},{11,10},{13,12},{... | collective-permute-start | bytes 786440 | tf_op jit(solution)/shard_map/ppermute | solution.py:57
  10.7 9.6 %copy-start.2 = (s32[64]{0:T(128)S(1)}, s32[64]{0:T(128)}, u32[]{:S(2)}) copy-start(s32[64]{0:T(128)} %param.18) | copy-start | bytes 772
  13.7 8.0 %copy-start.1 = (f32[8,1,4096]{2,1,0:T(1,128)S(1)}, f32[8,1,4096]{2,1,0:T(1,128)}, u32[]{:S(2)}) copy-start(f32[8,1,4096]{2,1,0:T(1,128)} %param.14) | copy-start | bytes 393220
  13.7 8.0 %copy-start.3 = (s32[64]{0:T(128)S(1)}, s32[64]{0:T(128)}, u32[]{:S(2)}) copy-start(s32[64]{0:T(128)} %param.17) | copy-start | bytes 772
  13.8 10.4 %all-to-all-start = ((f32[16,24,128]{2,1,0:T(8,128)}), f32[16,24,128]{2,1,0:T(8,128)S(1)}, u32[]{:S(2)}, u32[]{:S(2)}) async-start(f32[16,24,128]{2,1,0:T(8,128)} %bitcast.5), calls=%async_computation | async-start | bytes 393216 | tf_op jit(solution)/shard_map/all_to_all | solution.py:415
  23.8 40.1 %copy-start = (f32[8,1,16,512]{3,2,1,0:T(8,128)S(1)}, f32[8,1,16,512]{3,2,1,0:T(8,128)}, u32[]{:S(2)}) copy-start(f32[8,1,16,512]{3,2,1,0:T(8,128)} %param.11) | copy-start | bytes 786436
  55.2 9.8 %collective-permute-start.1 = (f32[8,16,512]{2,1,0:T(8,128)S(1)}, f32[8,16,512]{2,1,0:T(8,128)S(1)}, u32[]{:S(2)}, u32[]{:S(2)}) collective-permute-start(f32[8,16,512]{2,1,0:T(8,128)S(1)} %get-tuple-element.26.slice_ref), channel_id=1, source_target_pairs={{0,1},{1,2},{2,3},{4,5},{5,6},{6,7},{8,9},{9,10},{10,11},{12,13},{... | collective-permute-start | bytes 786440 | tf_op jit(solution)/shard_map/ppermute | solution.py:57
  60.0 6.4 %all-to-all-start.3 = ((f32[4,2,128]{2,1,0:T(2,128)}), f32[4,2,128]{2,1,0:T(2,128)S(1)}, u32[]{:S(2)}, u32[]{:S(2)}) async-start(f32[4,2,128]{2,1,0:T(2,128)} %get-tuple-element.31), calls=%async_computation.3 | async-start | bytes 8192 | tf_op jit(solution)/shard_map/all_to_all | solution.py:473

commit v8 on v7

--- a/solution.py
+++ b/solution.py
@@ -133,35 +133,38 @@
 
 
 def gram_kernel(
-    rate_ref,
-    keep_ref,
-    next_ref,
-    sums_ref,
-    x_ref,
-    dual_ref,
-    x_same,
-    cand_ref,
-    out_ref,
+    rate_ref, keep_ref, next_ref, sums_ref, x_ref, dual_ref, x_same, cand_ref, out_far, out_ref, left
 ):
     channels, rows, cols = x_ref.shape
     tiles = cols // LANES
     per_row = len(index_pairs) * tiles
     rate = rate_ref[0]
     keep = keep_ref[0]
-    for j in range(tiles):
-        here = pl.ds(j * LANES, LANES)
-        sums = {pair: sums_ref[k, :, here] for k, pair in enumerate(own_pairs)}
-        for b in range(3):
-            sums[b, 2] = jnp.zeros((rows, LANES), jnp.float32)
-        for c in range(channels):
-            step = (next_ref[c, :, here] - x_ref[c, :, here]) * keep
-            cand = dual_ref[2, c, :, here] + rate * step
-            for b in range(2):
-                sums[b, 2] = sums[b, 2] + dual_ref[b, c, :, here] * cand
-            sums[2, 2] = sums[2, 2] + cand * cand
-            cand_ref[2, c, :, here] = cand
-        for k, pair in enumerate(index_pairs):
-            out_ref[pl.ds(k * tiles + j, rows, stride=per_row), :] = sums[pair]
+    parts = left.shape[0]
+    size = rows // parts
+    copies = []
+    for part in range(parts):
+        these = pl.ds(part * size, size)
+        for j in range(tiles):
+            here = pl.ds(j * LANES, LANES)
+            sums = {pair: sums_ref[k, these, here] for k, pair in enumerate(own_pairs)}
+            for b in range(3):
+                sums[b, 2] = jnp.zeros((size, LANES), jnp.float32)
+            for c in range(channels):
+                step = (next_ref[c, these, here] - x_ref[c, these, here]) * keep
+                cand = dual_ref[2, c, these, here] + rate * step
+                for b in range(2):
+                    sums[b, 2] = sums[b, 2] + dual_ref[b, c, these, here] * cand
+                sums[2, 2] = sums[2, 2] + cand * cand
+                cand_ref[2, c, these, here] = cand
+            for k, pair in enumerate(index_pairs):
+                start = part * size * per_row + k * tiles + j
+                out_ref[pl.ds(start, size, stride=per_row), :] = sums[pair]
+        done = pl.ds(part * size * per_row, size * per_row)
+        copies.append(pltpu.make_async_copy(out_ref.at[done], out_far.at[done], left.at[part]))
+        copies[-1].start()
+    for copy in copies:
+        copy.wait()
 
 
 def pass_on_kernel(weight_ref, parts_ref, residual_ref, back_ref, out_ref, back_same):
@@ -250,25 +253,28 @@
     return entry_of[tuple(sorted((a, b)))]
 
 
-def slice_kernel(factor_ref, cand_ref, new_ref, sums_ref):
+def slice_kernel(factor_ref, cand_ref, new_ref, sums_far, sums_ref, left):
     _, channels, rows, cols = cand_ref.shape
     tiles = cols // LANES
     image = factor_image(factor_ref, rows, tiles)
+    per_row = factor_ref.shape[0] // rows
+    slabs, count, _ = sums_ref.shape
+    size = count * tiles
+    total = sum(
+        factor_ref[pl.ds(r * per_row + per_row - size, size), :] for r in range(rows)
+    )
+    for k in range(count):
+        row = jnp.sum(total[k * tiles : (k + 1) * tiles], axis=0, keepdims=True)
+        for p in range(slabs):
+            sums_ref[p, pl.ds(k, 1), :] = row
+    copy = pltpu.make_async_copy(sums_ref, sums_far, left)
+    copy.start()
     for j in range(tiles):
         here = pl.ds(j * LANES, LANES)
         factor = [image(entry_at(b, 2), j) for b in range(3)]
         for c in range(channels):
             new_ref[c, :, here] = sum(cand_ref[b, c, :, here] * factor[b] for b in range(3))
-    per_row = factor_ref.shape[0] // rows
-    slabs, count, _ = sums_ref.shape
-    size = count * tiles
-    total = sum(
-        factor_ref[pl.ds(r * per_row + per_row - size, size), :] for r in range(rows)
-    )
-    for k in range(count):
-        row = jnp.sum(total[k * tiles : (k + 1) * tiles], axis=0, keepdims=True)
-        for p in range(slabs):
-            sums_ref[p, pl.ds(k, 1), :] = row
+    copy.wait()
 
 
 def rest_kernel(
@@ -323,8 +329,9 @@
     total = sums_ref[0]
     for p in range(1, sums_ref.shape[0]):
         total = total + sums_ref[p]
+    across = jnp.sum(total, axis=1, keepdims=True)
     for k, count in enumerate(counts):
-        totals_ref[k] = jnp.sum(total[k : k + 1]) / count
+        totals_ref[k] = across[k, 0] * (1.0 / count)
 
 
 def picked_blocks(blocks, where, count):
@@ -395,10 +402,14 @@
         out_shape=(
             kept_near(images),
             kept_near((3, *images)),
-            jax.ShapeDtypeStruct((row_count * held, LANES), f32),
+            pltpu.HBM((row_count * held, LANES), f32),
         ),
         in_specs=[SMEM, SMEM, VMEM, VMEM, VMEM, VMEM],
-        out_specs=(VMEM,) * 3,
+        out_specs=(VMEM, VMEM, ANY),
+        scratch_shapes=[
+            pltpu.VMEM((row_count * held, LANES), f32),
+            pltpu.SemaphoreType.DMA((2,)),
+        ],
         input_output_aliases={4: 0, 5: 1},
         compiler_params=SCRATCH,
         name="gram",
@@ -463,14 +474,19 @@
 
     new_slice, sums = pl.pallas_call(
         slice_kernel,
-        out_shape=(kept_near(images), jax.ShapeDtypeStruct((slab_count, 2, LANES), f32)),
+        out_shape=(kept_near(images), pltpu.HBM((slab_count, 2, LANES), f32)),
         in_specs=[VMEM, VMEM],
-        out_specs=(VMEM, VMEM),
+        out_specs=(VMEM, ANY),
+        scratch_shapes=[
+            pltpu.VMEM((slab_count, 2, LANES), f32),
+            pltpu.SemaphoreType.DMA(()),
+        ],
         compiler_params=SCRATCH,
         name="slice",
     )(factor_near, near(candidate))
     prior_layer = from_behind(new_slice, "slab", 1)
-    all_sums = lax.all_to_all(sums, "slab", 0, 0, tiled=True)
+    slab_order = [[0, *range(slab_count // 2, slab_count), *range(1, slab_count // 2)]]
+    all_sums = lax.all_to_all(sums, "slab", 0, 0, axis_index_groups=slab_order, tiled=True)
     grad_new, ready, data_out = pl.pallas_call(
         rest_kernel,
         out_shape=(

time: 67.5 us -> 67.7 us (level)
  no operation moved by 1% of the time
where the time goes in v8:
time: 67.7 us; the launch traced here: 67.3 us
  blocking collectives  29.8 us (44%)
  starting transfers between devices  23.4 us (35%)
  Pallas kernels  6.57 us (10%)
  matrix products  3.76 us (6%)
  between operations  2.74 us (4%)
  waiting for transfers between devices  0.89 us (1%)
    all_to_all x1, blocking collectives, on_device(): lax.all_to_all(to_far, FAR, 0, 0, axis_index_groups=far_order, tiled=True)  19.9 us
    ppermute x2, starting transfers between devices, from_behind(): return lax.ppermute(block, axis, route)  13.6 us
    all_to_all x1, blocking collectives, on_device(): lax.all_to_all(to_share, SHARE, 0, 0, axis_index_groups=share_order, tile...  9.87 us
    all_to_all x1, starting transfers between devices, on_device(): lax.all_to_all(partial_gram.reshape(share_count, held, LANES), SHARE, 0,...  6.5 us
    all_to_all x1, starting transfers between devices, on_device(): lax.all_to_all(sums, 'slab', 0, 0, axis_index_groups=slab_order, tiled=True)  3.24 us
    pallas_call x1, Pallas kernels, on_device(): pl.pallas_call(own_kernel, out_shape=(kept_near(images), kept_near((3, *i...  2.05 us
    dot_general x2, matrix products, gathered_products(): jnp.einsum('tc,tbj->bcj', chosen, products, precision=lax.Precision.HIGHEST)  1.47 us
  transfers between devices with their start and end apart: 4, of which 1 were waited for; matrix products, arithmetic and copies ran while one was open for 6% of the time, Pallas kernels for 6%

profile of v8, /device:TPU:1, one launch (start us, length us, event | category | flops | bytes accessed | tf_op | source)
XLA Modules:
  0.0 67.3 jit_solution(9074622995555247254)
XLA Ops:
  0.6 8.8 %collective-permute-start = (f32[8,1,16,512]{3,2,0,1:T(8,128)}, f32[8,1,16,512]{3,2,0,1:T(8,128)S(1)}, u32[]{:S(2)}, u32[]{:S(2)}) collective-permute-start(f32[8,1,16,512]{3,2,0,1:T(8,128)} %bitcast.45), channel_id=1, source_target_pairs={{1,0},{2,1},{3,2},{5,4},{6,5},{7,6},{9,8},{10,9},{11,10},{13,12},{... | collective-permute-start | bytes 786440 | tf_op jit(solution)/shard_map/ppermute | solution.py:57
  10.7 0.0 copy-start.2
  10.7 2.0 %own.1 = (f32[8,16,512]{2,1,0:T(8,128)S(1)}, f32[3,8,16,512]{3,2,1,0:T(8,128)S(1)}, f32[3,16,512]{2,1,0:T(8,128)S(1)}, bf16[64,128,128]{2,1,0:T(8,128)(2,1)S(1)}) custom-call(f32[1]{0:T(128)} %copy.39.rate_ref, f32[8,16,512]{2,1,0:T(8,128)} %bitcast.46, f32[3,8,16,512]{3,2,1,0:T(8,128)} %bitcast.44, bf16[64,128,128]{2,1,0:T(8,128)(2,1)} %projector_far.1), custom_call_target="tpu_custom_call" | custom-call | tf_op jit(solution)/shard_map/own/pallas_call | solution.py:381
  12.8 0.0 collective-permute-done
  12.8 0.9 %gram.1 = (f32[8,16,512]{2,1,0:T(8,128)S(1)}, f32[3,8,16,512]{3,2,1,0:T(8,128)S(1)}, f32[384,128]{1,0:T(8,128)}) custom-call(f32[1]{0:T(128)} %copy.39.rate_ref, f32[1]{0:T(128)} %bitcast.keep_ref, f32[8,16,512]{2,1,0:T(8,128)S(1)} %bitcast.42, f32[3,16,512]{2,1,0:T(8,128)S(1)} %get-tuple-element.18.sums_ref, ...), custom_call_target="tpu_custom_call", output_to_operand_aliasing={{0}: (4, {}), {1}: (5, {})} | custom-call | tf_op jit(solution)/shard_map/gram/pallas_call | solution.py:400
  13.7 0.0 copy-start.1
  13.7 0.0 copy-start.3
  13.7 0.1 convert_element_type.20
  13.8 6.5 %all-to-all-start = ((f32[16,24,128]{2,1,0:T(8,128)}), f32[16,24,128]{2,1,0:T(8,128)S(1)}, u32[]{:S(2)}, u32[]{:S(2)}) async-start(f32[16,24,128]{2,1,0:T(8,128)} %bitcast.47), calls=%async_computation | async-start | bytes 393216 | tf_op jit(solution)/shard_map/all_to_all | solution.py:426
  20.3 0.0 copy-done.2
  20.3 0.2 fusion.9
  20.6 1.2 %fusion.3 = f32[64,8,128]{2,1,0:T(8,128)S(1)} fusion(bf16[64,128,128]{2,1,0:T(8,128)(2,1)S(1)} %get-tuple-element.23, bf16[64,8,128]{2,0,1:T(8,128)(2,1)S(1)} %fusion.9), kind=kOutput, calls=%fused_computation.7 | convolution fusion | flops 16777216 | bytes 2490368 | tf_op jit(solution)/shard_map/tij,tbj->tbi/dot_general | solution.py:437
  21.7 0.0 copy-done.1
  21.7 0.0 copy-done.3
  21.7 1.2 %add_divide_fusion = (f32[8,32,128]{2,1,0:T(8,128)S(1)}, f32[8,32,128]{2,1,0:T(8,128)S(1)}) fusion(f32[8,32,128]{2,1,0:T(8,128)S(1)} %bitcast.48, f32[]{:T(128)S(6)} %add.7, f32[]{:T(128)} %bitcast.37, f32[8,32,128]{2,1,0:T(8,128)} %bitcast.49, s32[64]{0:T(128)S(1)} %copy-done.3, f32[64,8,128]{2,1,0:T(8,128)S(1)} %fusion.3), kind=kOutput, calls=%fused_computation.9 | convolution fusion | flops 25298944 | bytes 786696 | tf_op jit(solution)/shard_map/tc,tbj->bcj/dot_general | solution.py:346
  22.9 0.2 fusion.5
  23.2 0.6 fusion.4
  23.8 0.0 copy-start
  23.8 0.3 convolution_bitcast_fusion
  24.2 0.0 all-to-all-done.parts_ref
  24.2 19.9 %all_to_all.20.parts_ref = f32[8,32,128]{2,1,0:T(8,128)S(1)} all-to-all(f32[8,32,128]{2,1,0:T(8,128)S(1)} %get-tuple-element.24), channel_id=1, replica_groups={{40,8,0,16,24,56,32,48},{41,9,1,17,25,57,33,49},{42,10,2,18,26,58,34,50..., dimensions={0} | all-to-all | bytes 262144 | tf_op jit(solution)/shard_map/all_to_all | solution.py:460
  44.1 0.5 factor.1
  44.6 9.9 %all_to_all.21 = f32[16,32,128]{2,1,0:T(8,128)S(1)} all-to-all(f32[16,32,128]{2,1,0:T(8,128)S(1)} %factor.1), channel_id=1, replica_groups={{324,0,4,64,128,384,68,132,192,256,388,448,196,260,320,452},{325,1,5,65..., dimensions={0} | all-to-all | bytes 524288 | tf_op jit(solution)/shard_map/all_to_all | solution.py:470
  54.5 0.6 slice.1
  55.1 4.8 %collective-permute-start.1 = (f32[8,16,512]{2,1,0:T(8,128)S(1)}, f32[8,16,512]{2,1,0:T(8,128)S(1)}, u32[]{:S(2)}, u32[]{:S(2)}) collective-permute-start(f32[8,16,512]{2,1,0:T(8,128)S(1)} %get-tuple-element.26.slice_ref), channel_id=1, source_target_pairs={{0,1},{1,2},{2,3},{4,5},{5,6},{6,7},{8,9},{9,10},{10,11},{12,13},{... | collective-permute-start | bytes 786440 | tf_op jit(solution)/shard_map/ppermute | solution.py:57
  60.0 3.2 %all-to-all-start.3 = ((f32[4,2,128]{2,1,0:T(2,128)}), f32[4,2,128]{2,1,0:T(2,128)S(1)}, u32[]{:S(2)}, u32[]{:S(2)}) async-start(f32[4,2,128]{2,1,0:T(2,128)} %get-tuple-element.31), calls=%async_computation.3 | async-start | bytes 8192 | tf_op jit(solution)/shard_map/all_to_all | solution.py:489
  63.8 0.0 copy-done
  63.9 1.1 %rest.1 = (f32[3,8,16,512]{3,2,1,0:T(8,128)}, f32[8,16,512]{2,1,0:T(8,128)S(1)}, f32[8,32,128]{2,1,0:T(8,128)}) custom-call(f32[1]{0:T(128)S(6)} %copy.40.rate_ref, f32[1]{0:T(128)} %bitcast.keep_ref, f32[512,128]{1,0:T(8,128)S(1)} %bitcast.40, f32[3,8,16,512]{3,2,1,0:T(8,128)S(1)} %get-tuple-element.25.cand_ref, ...), custom_call_target="tpu_custom_call" | custom-call | tf_op jit(solution)/shard_map/rest/pallas_call | solution.py:490
  65.0 0.0 collective-permute-done.1.prior_ref
  65.0 0.7 %finish.1.updated_far = f32[8,16,512]{2,1,0:T(8,128)} custom-call(f32[1]{0:T(128)S(6)} %copy.40.rate_ref, f32[8,16,512]{2,1,0:T(8,128)S(1)} %get-tuple-element.28.ready_ref, f32[8,16,512]{2,1,0:T(8,128)S(1)} %collective-permute-done.1.prior_ref), custom_call_target="tpu_custom_call" | custom-call | tf_op jit(solution)/shard_map/finish/pallas_call | solution.py:512
  65.8 0.9 %all-to-all-done.3.sums_ref = f32[4,2,128]{2,1,0:T(2,128)S(1)} async-done(((f32[4,2,128]{2,1,0:T(2,128)}), f32[4,2,128]{2,1,0:T(2,128)S(1)}, u32[]{:S(2)}, u32[]{:S(2)}) %all-to-all-start.3) | async-done | bytes 4128 | tf_op jit(solution)/shard_map/all_to_all | solution.py:489
  66.6 0.6 totals.1
  (3 shorter events, 0.1 us)
Async XLA Ops:
  0.6 12.2 %collective-permute-start = (f32[8,1,16,512]{3,2,0,1:T(8,128)}, f32[8,1,16,512]{3,2,0,1:T(8,128)S(1)}, u32[]{:S(2)}, u32[]{:S(2)}) collective-permute-start(f32[8,1,16,512]{3,2,0,1:T(8,128)} %bitcast.45), channel_id=1, source_target_pairs={{1,0},{2,1},{3,2},{5,4},{6,5},{7,6},{9,8},{10,9},{11,10},{13,12},{... | collective-permute-start | bytes 786440 | tf_op jit(solution)/shard_map/ppermute | solution.py:57
  10.7 9.6 %copy-start.2 = (s32[64]{0:T(128)S(1)}, s32[64]{0:T(128)}, u32[]{:S(2)}) copy-start(s32[64]{0:T(128)} %param.18) | copy-start | bytes 772
  13.7 8.1 %copy-start.1 = (f32[8,1,4096]{2,1,0:T(1,128)S(1)}, f32[8,1,4096]{2,1,0:T(1,128)}, u32[]{:S(2)}) copy-start(f32[8,1,4096]{2,1,0:T(1,128)} %param.14) | copy-start | bytes 393220
  13.7 8.1 %copy-start.3 = (s32[64]{0:T(128)S(1)}, s32[64]{0:T(128)}, u32[]{:S(2)}) copy-start(s32[64]{0:T(128)} %param.17) | copy-start | bytes 772
  13.8 10.4 %all-to-all-start = ((f32[16,24,128]{2,1,0:T(8,128)}), f32[16,24,128]{2,1,0:T(8,128)S(1)}, u32[]{:S(2)}, u32[]{:S(2)}) async-start(f32[16,24,128]{2,1,0:T(8,128)} %bitcast.47), calls=%async_computation | async-start | bytes 393216 | tf_op jit(solution)/shard_map/all_to_all | solution.py:426
  23.8 40.0 %copy-start = (f32[8,1,16,512]{3,2,1,0:T(8,128)S(1)}, f32[8,1,16,512]{3,2,1,0:T(8,128)}, u32[]{:S(2)}) copy-start(f32[8,1,16,512]{3,2,1,0:T(8,128)} %param.11) | copy-start | bytes 786436
  55.1 9.9 %collective-permute-start.1 = (f32[8,16,512]{2,1,0:T(8,128)S(1)}, f32[8,16,512]{2,1,0:T(8,128)S(1)}, u32[]{:S(2)}, u32[]{:S(2)}) collective-permute-start(f32[8,16,512]{2,1,0:T(8,128)S(1)} %get-tuple-element.26.slice_ref), channel_id=1, source_target_pairs={{0,1},{1,2},{2,3},{4,5},{5,6},{6,7},{8,9},{9,10},{10,11},{12,13},{... | collective-permute-start | bytes 786440 | tf_op jit(solution)/shard_map/ppermute | solution.py:57
  60.0 6.7 %all-to-all-start.3 = ((f32[4,2,128]{2,1,0:T(2,128)}), f32[4,2,128]{2,1,0:T(2,128)S(1)}, u32[]{:S(2)}, u32[]{:S(2)}) async-start(f32[4,2,128]{2,1,0:T(2,128)} %get-tuple-element.31), calls=%async_computation.3 | async-start | bytes 8192 | tf_op jit(solution)/shard_map/all_to_all | solution.py:489

commit v9 on v8

--- a/solution.py
+++ b/solution.py
@@ -169,17 +169,20 @@
 
 def pass_on_kernel(weight_ref, parts_ref, residual_ref, back_ref, out_ref, back_same):
     peers, per_row, _ = parts_ref.shape
+    copies, pairs, two, _ = out_ref.shape
     total = parts_ref[0]
     for p in range(1, peers):
         total = total + parts_ref[p]
-    misfit = jnp.zeros((out_ref.shape[1] - per_row, LANES), jnp.float32)
+    squares = jnp.zeros((8, LANES), jnp.float32)
     for c in range(residual_ref.shape[0]):
-        for start in range(0, residual_ref.shape[1], misfit.shape[0]):
-            some = residual_ref[c, pl.ds(start, misfit.shape[0]), :]
-            misfit = misfit + some * some
-    for p in range(out_ref.shape[0]):
-        out_ref[p, :per_row, :] = total
-        out_ref[p, per_row:, :] = misfit
+        for start in range(0, residual_ref.shape[1], 8):
+            some = residual_ref[c, pl.ds(start, 8), :]
+            squares = squares + some * some
+    misfit = sum(squares[k : k + two] for k in range(0, 8, two))
+    for k in range(pairs):
+        pair = total[two * k : two * k + two] if k < per_row // two else misfit
+        for p in range(copies):
+            out_ref[p, k] = pair
 
 
 def rotate(entry, vectors, p, q):
@@ -210,19 +213,17 @@
     return entry, vectors
 
 
-def factor_kernel(channels, weight_ref, parts_ref, out_ref):
-    peers, held, _ = parts_ref.shape
+def factor_kernel(channels, weight_ref, parts_ref, out_ref, sums_ref):
+    peers, pairs, two, _ = parts_ref.shape
     entries = len(index_pairs)
     tiles = out_ref.shape[1] // (entries + 2)
-
-    def summed(start, size):
-        total = parts_ref[0, pl.ds(start, size), :]
+    for k in range(pairs):
+        pair = parts_ref[0, k]
         for p in range(1, peers):
-            total = total + parts_ref[p, pl.ds(start, size), :]
-        return total
-
+            pair = pair + parts_ref[p, k]
+        sums_ref[pl.ds(two * k, two), :] = pair
     radius = weight_ref[0] * math.sqrt(channels)
-    entry = [summed(k * tiles, tiles) for k in range(entries)]
+    entry = [sums_ref[pl.ds(k * tiles, tiles), :] for k in range(entries)]
     one, zero = jnp.ones_like(entry[0]), jnp.zeros_like(entry[0])
     vectors = [[one if r == c else zero for c in range(3)] for r in range(3)]
     for _ in range(SWEEPS):
@@ -231,13 +232,17 @@
     roots = [jnp.sqrt(jnp.maximum(entry[d], 0.0)) for d in range(3)]
     scales = [radius / jnp.maximum(root, radius) for root in roots]
     excess = sum(jnp.maximum(root - radius, 0.0) for root in roots) / radius
-    misfit = sum(summed(k, tiles) for k in range(entries * tiles, held, tiles))
+    misfit = sums_ref[pl.ds(entries * tiles, two), :]
     rows = [
         sum(vectors[a][d] * scales[d] * vectors[b][d] for d in range(3)) for a, b in index_pairs
-    ] + [misfit, excess]
+    ]
     for p in range(out_ref.shape[0]):
         for k, row in enumerate(rows):
             out_ref[p, pl.ds(k * tiles, tiles), :] = row
+        out_ref[p, pl.ds(entries * tiles, two), :] = misfit
+        for start in range(entries * tiles + two, (entries + 1) * tiles, two):
+            out_ref[p, pl.ds(start, two), :] = jnp.zeros_like(misfit)
+        out_ref[p, pl.ds((entries + 1) * tiles, tiles), :] = excess
 
 
 def factor_image(factor_ref, rows, tiles):
@@ -448,7 +453,7 @@
     to_far, back_proj = pl.pallas_call(
         pass_on_kernel,
         out_shape=(
-            jax.ShapeDtypeStruct((far_count, held + 8, LANES), f32),
+            jax.ShapeDtypeStruct((far_count, held // 2 + 1, 2, LANES), f32),
             kept_near(images),
         ),
         in_specs=[SMEM, VMEM, VMEM, VMEM],
@@ -464,6 +469,7 @@
         out_shape=kept_near((share_count, held + 2 * tiles, LANES)),
         in_specs=[SMEM, VMEM],
         out_specs=VMEM,
+        scratch_shapes=[pltpu.VMEM((held + 2, LANES), f32)],
         compiler_params=SCRATCH,
         name="factor",
     )(reg_weight, near(far_parts))

time: 67.7 us -> 67 us (0.990)
  blocking collectives: 29.8 us -> 28.5 us
    all_to_all x1, blocking collectives: 9.87 us -> 8.97 us  [on_device(): lax.all_to_all(to_share, SHARE, 0, 0, axis_index_groups=share_order, tile...]
where the time goes in v9:
time: 67 us; the launch traced here: 66.6 us
  blocking collectives  28.5 us (43%)
  starting transfers between devices  24 us (36%)
  Pallas kernels  6.59 us (10%)
  matrix products  3.76 us (6%)
  between operations  2.74 us (4%)
  waiting for transfers between devices  0.89 us (1%)
    all_to_all x1, blocking collectives, on_device(): lax.all_to_all(to_far, FAR, 0, 0, axis_index_groups=far_order, tiled=True)  19.5 us
    ppermute x2, starting transfers between devices, from_behind(): return lax.ppermute(block, axis, route)  14.2 us
    all_to_all x1, blocking collectives, on_device(): lax.all_to_all(to_share, SHARE, 0, 0, axis_index_groups=share_order, tile...  8.97 us
    all_to_all x1, starting transfers between devices, on_device(): lax.all_to_all(partial_gram.reshape(share_count, held, LANES), SHARE, 0,...  6.5 us
    all_to_all x1, starting transfers between devices, on_device(): lax.all_to_all(sums, 'slab', 0, 0, axis_index_groups=slab_order, tiled=True)  3.24 us
    pallas_call x1, Pallas kernels, on_device(): pl.pallas_call(own_kernel, out_shape=(kept_near(images), kept_near((3, *i...  2.05 us
    dot_general x2, matrix products, gathered_products(): jnp.einsum('tc,tbj->bcj', chosen, products, precision=lax.Precision.HIGHEST)  1.47 us
  transfers between devices with their start and end apart: 4, of which 1 were waited for; matrix products, arithmetic and copies ran while one was open for 6% of the time, Pallas kernels for 6%

profile of v9, /device:TPU:1, one launch (start us, length us, event | category | flops | bytes accessed | tf_op | source)
XLA Modules:
  0.0 66.6 jit_solution(13095771425082446285)
XLA Ops:
  0.6 8.8 %collective-permute-start = (f32[8,1,16,512]{3,2,0,1:T(8,128)}, f32[8,1,16,512]{3,2,0,1:T(8,128)S(1)}, u32[]{:S(2)}, u32[]{:S(2)}) collective-permute-start(f32[8,1,16,512]{3,2,0,1:T(8,128)} %bitcast.45), channel_id=1, source_target_pairs={{1,0},{2,1},{3,2},{5,4},{6,5},{7,6},{9,8},{10,9},{11,10},{13,12},{... | collective-permute-start | bytes 786440 | tf_op jit(solution)/shard_map/ppermute | solution.py:57
  10.7 0.0 copy-start.2
  10.7 2.0 %own.1 = (f32[8,16,512]{2,1,0:T(8,128)S(1)}, f32[3,8,16,512]{3,2,1,0:T(8,128)S(1)}, f32[3,16,512]{2,1,0:T(8,128)S(1)}, bf16[64,128,128]{2,1,0:T(8,128)(2,1)S(1)}) custom-call(f32[1]{0:T(128)} %copy.39.rate_ref, f32[8,16,512]{2,1,0:T(8,128)} %bitcast.46, f32[3,8,16,512]{3,2,1,0:T(8,128)} %bitcast.44, bf16[64,128,128]{2,1,0:T(8,128)(2,1)} %projector_far.1), custom_call_target="tpu_custom_call" | custom-call | tf_op jit(solution)/shard_map/own/pallas_call | solution.py:386
  12.8 0.0 collective-permute-done
  12.8 0.9 %gram.1 = (f32[8,16,512]{2,1,0:T(8,128)S(1)}, f32[3,8,16,512]{3,2,1,0:T(8,128)S(1)}, f32[384,128]{1,0:T(8,128)}) custom-call(f32[1]{0:T(128)} %copy.39.rate_ref, f32[1]{0:T(128)} %bitcast.keep_ref, f32[8,16,512]{2,1,0:T(8,128)S(1)} %bitcast.42, f32[3,16,512]{2,1,0:T(8,128)S(1)} %get-tuple-element.18.sums_ref, ...), custom_call_target="tpu_custom_call", output_to_operand_aliasing={{0}: (4, {}), {1}: (5, {})} | custom-call | tf_op jit(solution)/shard_map/gram/pallas_call | solution.py:405
  13.7 0.0 copy-start.1
  13.7 0.0 copy-start.3
  13.7 0.1 convert_element_type.20
  13.8 6.5 %all-to-all-start = ((f32[16,24,128]{2,1,0:T(8,128)}), f32[16,24,128]{2,1,0:T(8,128)S(1)}, u32[]{:S(2)}, u32[]{:S(2)}) async-start(f32[16,24,128]{2,1,0:T(8,128)} %bitcast.47), calls=%async_computation | async-start | bytes 393216 | tf_op jit(solution)/shard_map/all_to_all | solution.py:431
  20.3 0.0 copy-done.2
  20.3 0.2 fusion.9
  20.6 1.2 %fusion.3 = f32[64,8,128]{2,1,0:T(8,128)S(1)} fusion(bf16[64,128,128]{2,1,0:T(8,128)(2,1)S(1)} %get-tuple-element.23, bf16[64,8,128]{2,0,1:T(8,128)(2,1)S(1)} %fusion.9), kind=kOutput, calls=%fused_computation.7 | convolution fusion | flops 16777216 | bytes 2490368 | tf_op jit(solution)/shard_map/tij,tbj->tbi/dot_general | solution.py:442
  21.7 0.0 copy-done.1
  21.7 0.0 copy-done.3
  21.7 1.2 %add_divide_fusion = (f32[8,32,128]{2,1,0:T(8,128)S(1)}, f32[8,32,128]{2,1,0:T(8,128)S(1)}) fusion(f32[8,32,128]{2,1,0:T(8,128)S(1)} %bitcast.48, f32[]{:T(128)S(6)} %add.7, f32[]{:T(128)} %bitcast.37, f32[8,32,128]{2,1,0:T(8,128)} %bitcast.49, s32[64]{0:T(128)S(1)} %copy-done.3, f32[64,8,128]{2,1,0:T(8,128)S(1)} %fusion.3), kind=kOutput, calls=%fused_computation.9 | convolution fusion | flops 25298944 | bytes 786696 | tf_op jit(solution)/shard_map/tc,tbj->bcj/dot_general | solution.py:351
  22.9 0.2 fusion.5
  23.2 0.6 fusion.4
  23.8 0.0 copy-start
  23.8 0.3 convolution_bitcast_fusion
  24.2 0.0 all-to-all-done.parts_ref
  24.2 19.5 %all_to_all.20.parts_ref = f32[8,13,2,128]{3,2,1,0:T(2,128)S(1)} all-to-all(f32[8,13,2,128]{3,2,1,0:T(2,128)S(1)} %get-tuple-element.24), channel_id=1, replica_groups={{40,8,0,16,24,56,32,48},{41,9,1,17,25,57,33,49},{42,10,2,18,26,58,34,50..., dimensions={0} | all-to-all | bytes 212992 | tf_op jit(solution)/shard_map/all_to_all | solution.py:465
  43.8 0.5 factor.1
  44.3 9.0 %all_to_all.21 = f32[16,32,128]{2,1,0:T(8,128)S(1)} all-to-all(f32[16,32,128]{2,1,0:T(8,128)S(1)} %factor.1), channel_id=1, replica_groups={{324,0,4,64,128,384,68,132,192,256,388,448,196,260,320,452},{325,1,5,65..., dimensions={0} | all-to-all | bytes 524288 | tf_op jit(solution)/shard_map/all_to_all | solution.py:476
  53.2 0.6 slice.1
  53.9 5.4 %collective-permute-start.1 = (f32[8,16,512]{2,1,0:T(8,128)S(1)}, f32[8,16,512]{2,1,0:T(8,128)S(1)}, u32[]{:S(2)}, u32[]{:S(2)}) collective-permute-start(f32[8,16,512]{2,1,0:T(8,128)S(1)} %get-tuple-element.26.slice_ref), channel_id=1, source_target_pairs={{0,1},{1,2},{2,3},{4,5},{5,6},{6,7},{8,9},{9,10},{10,11},{12,13},{... | collective-permute-start | bytes 786440 | tf_op jit(solution)/shard_map/ppermute | solution.py:57
  59.3 3.2 %all-to-all-start.3 = ((f32[4,2,128]{2,1,0:T(2,128)}), f32[4,2,128]{2,1,0:T(2,128)S(1)}, u32[]{:S(2)}, u32[]{:S(2)}) async-start(f32[4,2,128]{2,1,0:T(2,128)} %get-tuple-element.31), calls=%async_computation.3 | async-start | bytes 8192 | tf_op jit(solution)/shard_map/all_to_all | solution.py:495
  63.2 0.0 copy-done
  63.2 1.1 %rest.1 = (f32[3,8,16,512]{3,2,1,0:T(8,128)}, f32[8,16,512]{2,1,0:T(8,128)S(1)}, f32[8,32,128]{2,1,0:T(8,128)}) custom-call(f32[1]{0:T(128)S(6)} %copy.40.rate_ref, f32[1]{0:T(128)} %bitcast.keep_ref, f32[512,128]{1,0:T(8,128)S(1)} %bitcast.40, f32[3,8,16,512]{3,2,1,0:T(8,128)S(1)} %get-tuple-element.25.cand_ref, ...), custom_call_target="tpu_custom_call" | custom-call | tf_op jit(solution)/shard_map/rest/pallas_call | solution.py:496
  64.4 0.0 collective-permute-done.1.prior_ref
  64.4 0.7 %finish.1.updated_far = f32[8,16,512]{2,1,0:T(8,128)} custom-call(f32[1]{0:T(128)S(6)} %copy.40.rate_ref, f32[8,16,512]{2,1,0:T(8,128)S(1)} %get-tuple-element.28.ready_ref, f32[8,16,512]{2,1,0:T(8,128)S(1)} %collective-permute-done.1.prior_ref), custom_call_target="tpu_custom_call" | custom-call | tf_op jit(solution)/shard_map/finish/pallas_call | solution.py:518
  65.1 0.9 %all-to-all-done.3.sums_ref = f32[4,2,128]{2,1,0:T(2,128)S(1)} async-done(((f32[4,2,128]{2,1,0:T(2,128)}), f32[4,2,128]{2,1,0:T(2,128)S(1)}, u32[]{:S(2)}, u32[]{:S(2)}) %all-to-all-start.3) | async-done | bytes 4128 | tf_op jit(solution)/shard_map/all_to_all | solution.py:495
  66.0 0.6 totals.1
  (3 shorter events, 0.1 us)
Async XLA Ops:
  0.6 12.2 %collective-permute-start = (f32[8,1,16,512]{3,2,0,1:T(8,128)}, f32[8,1,16,512]{3,2,0,1:T(8,128)S(1)}, u32[]{:S(2)}, u32[]{:S(2)}) collective-permute-start(f32[8,1,16,512]{3,2,0,1:T(8,128)} %bitcast.45), channel_id=1, source_target_pairs={{1,0},{2,1},{3,2},{5,4},{6,5},{7,6},{9,8},{10,9},{11,10},{13,12},{... | collective-permute-start | bytes 786440 | tf_op jit(solution)/shard_map/ppermute | solution.py:57
  10.7 9.6 %copy-start.2 = (s32[64]{0:T(128)S(1)}, s32[64]{0:T(128)}, u32[]{:S(2)}) copy-start(s32[64]{0:T(128)} %param.18) | copy-start | bytes 772
  13.7 8.1 %copy-start.1 = (f32[8,1,4096]{2,1,0:T(1,128)S(1)}, f32[8,1,4096]{2,1,0:T(1,128)}, u32[]{:S(2)}) copy-start(f32[8,1,4096]{2,1,0:T(1,128)} %param.14) | copy-start | bytes 393220
  13.7 8.1 %copy-start.3 = (s32[64]{0:T(128)S(1)}, s32[64]{0:T(128)}, u32[]{:S(2)}) copy-start(s32[64]{0:T(128)} %param.17) | copy-start | bytes 772
  13.8 10.4 %all-to-all-start = ((f32[16,24,128]{2,1,0:T(8,128)}), f32[16,24,128]{2,1,0:T(8,128)S(1)}, u32[]{:S(2)}, u32[]{:S(2)}) async-start(f32[16,24,128]{2,1,0:T(8,128)} %bitcast.47), calls=%async_computation | async-start | bytes 393216 | tf_op jit(solution)/shard_map/all_to_all | solution.py:431
  23.8 39.4 %copy-start = (f32[8,1,16,512]{3,2,1,0:T(8,128)S(1)}, f32[8,1,16,512]{3,2,1,0:T(8,128)}, u32[]{:S(2)}) copy-start(f32[8,1,16,512]{3,2,1,0:T(8,128)} %param.11) | copy-start | bytes 786436
  53.9 10.5 %collective-permute-start.1 = (f32[8,16,512]{2,1,0:T(8,128)S(1)}, f32[8,16,512]{2,1,0:T(8,128)S(1)}, u32[]{:S(2)}, u32[]{:S(2)}) collective-permute-start(f32[8,16,512]{2,1,0:T(8,128)S(1)} %get-tuple-element.26.slice_ref), channel_id=1, source_target_pairs={{0,1},{1,2},{2,3},{4,5},{5,6},{6,7},{8,9},{9,10},{10,11},{12,13},{... | collective-permute-start | bytes 786440 | tf_op jit(solution)/shard_map/ppermute | solution.py:57
  59.3 6.7 %all-to-all-start.3 = ((f32[4,2,128]{2,1,0:T(2,128)}), f32[4,2,128]{2,1,0:T(2,128)S(1)}, u32[]{:S(2)}, u32[]{:S(2)}) async-start(f32[4,2,128]{2,1,0:T(2,128)} %get-tuple-element.31), calls=%async_computation.3 | async-start | bytes 8192 | tf_op jit(solution)/shard_map/all_to_all | solution.py:495

commit v10 on v9

--- a/solution.py
+++ b/solution.py
@@ -216,7 +216,7 @@
 def factor_kernel(channels, weight_ref, parts_ref, out_ref, sums_ref):
     peers, pairs, two, _ = parts_ref.shape
     entries = len(index_pairs)
-    tiles = out_ref.shape[1] // (entries + 2)
+    tiles = two * (pairs - 1) // entries
     for k in range(pairs):
         pair = parts_ref[0, k]
         for p in range(1, peers):
@@ -236,13 +236,11 @@
     rows = [
         sum(vectors[a][d] * scales[d] * vectors[b][d] for d in range(3)) for a, b in index_pairs
     ]
-    for p in range(out_ref.shape[0]):
-        for k, row in enumerate(rows):
-            out_ref[p, pl.ds(k * tiles, tiles), :] = row
-        out_ref[p, pl.ds(entries * tiles, two), :] = misfit
-        for start in range(entries * tiles + two, (entries + 1) * tiles, two):
-            out_ref[p, pl.ds(start, two), :] = jnp.zeros_like(misfit)
-        out_ref[p, pl.ds((entries + 1) * tiles, tiles), :] = excess
+    last = jnp.concatenate([jnp.sum(part, axis=0, keepdims=True) for part in (misfit, excess)])
+    for k in range(pairs):
+        row, start = rows[two * k // tiles] if k + 1 < pairs else last, two * k % tiles
+        for p in range(out_ref.shape[0]):
+            out_ref[p, k] = row[start : start + two]
 
 
 def factor_image(factor_ref, rows, tiles):
@@ -258,22 +256,22 @@
     return entry_of[tuple(sorted((a, b)))]
 
 
-def slice_kernel(factor_ref, cand_ref, new_ref, sums_far, sums_ref, left):
+def slice_kernel(parts_ref, cand_ref, new_ref, factor_ref, sums_far, sums_ref, left):
     _, channels, rows, cols = cand_ref.shape
     tiles = cols // LANES
-    image = factor_image(factor_ref, rows, tiles)
-    per_row = factor_ref.shape[0] // rows
-    slabs, count, _ = sums_ref.shape
-    size = count * tiles
-    total = sum(
-        factor_ref[pl.ds(r * per_row + per_row - size, size), :] for r in range(rows)
-    )
-    for k in range(count):
-        row = jnp.sum(total[k * tiles : (k + 1) * tiles], axis=0, keepdims=True)
-        for p in range(slabs):
-            sums_ref[p, pl.ds(k, 1), :] = row
+    peers, pairs, two, _ = parts_ref.shape
+    total = parts_ref[0, pairs - 1]
+    for p in range(1, peers):
+        total = total + parts_ref[p, pairs - 1]
+    for slab in range(sums_ref.shape[0]):
+        sums_ref[slab] = total
     copy = pltpu.make_async_copy(sums_ref, sums_far, left)
     copy.start()
+    per_row = factor_ref.shape[0] // rows
+    for p in range(peers):
+        for k in range(pairs - 1):
+            factor_ref[pl.ds(p * per_row + two * k, two), :] = parts_ref[p, k]
+    image = factor_image(factor_ref, rows, tiles)
     for j in range(tiles):
         here = pl.ds(j * LANES, LANES)
         factor = [image(entry_at(b, 2), j) for b in range(3)]
@@ -466,7 +464,7 @@
 
     to_share = pl.pallas_call(
         functools.partial(factor_kernel, total_channels),
-        out_shape=kept_near((share_count, held + 2 * tiles, LANES)),
+        out_shape=kept_near((share_count, held // 2 + 1, 2, LANES)),
         in_specs=[SMEM, VMEM],
         out_specs=VMEM,
         scratch_shapes=[pltpu.VMEM((held + 2, LANES), f32)],
@@ -476,20 +474,23 @@
     factor_rows = lax.all_to_all(
         to_share, SHARE, 0, 0, axis_index_groups=share_order, tiled=True
     )
-    factor_near = near(factor_rows.reshape(-1, LANES))
-
-    new_slice, sums = pl.pallas_call(
+
+    new_slice, factor_image_rows, sums = pl.pallas_call(
         slice_kernel,
-        out_shape=(kept_near(images), pltpu.HBM((slab_count, 2, LANES), f32)),
+        out_shape=(
+            kept_near(images),
+            kept_near((row_count * held, LANES)),
+            pltpu.HBM((slab_count, 2, LANES), f32),
+        ),
         in_specs=[VMEM, VMEM],
-        out_specs=(VMEM, ANY),
+        out_specs=(VMEM, VMEM, ANY),
         scratch_shapes=[
             pltpu.VMEM((slab_count, 2, LANES), f32),
             pltpu.SemaphoreType.DMA(()),
         ],
         compiler_params=SCRATCH,
         name="slice",
-    )(factor_near, near(candidate))
+    )(near(factor_rows), near(candidate))
     prior_layer = from_behind(new_slice, "slab", 1)
     slab_order = [[0, *range(slab_count // 2, slab_count), *range(1, slab_count // 2)]]
     all_sums = lax.all_to_all(sums, "slab", 0, 0, axis_index_groups=slab_order, tiled=True)
@@ -507,7 +508,7 @@
     )(
         primal_step,
         keep,
-        factor_near,
+        near(factor_image_rows),
         near(candidate),
         near(new_slice),
         near(volume_now.reshape(images)),

time: 67 us -> 66.8 us (level)
  no operation moved by 1% of the time
where the time goes in v10:
time: 66.8 us; the launch traced here: 66.4 us
  blocking collectives  28 us (42%)
  starting transfers between devices  24.2 us (36%)
  Pallas kernels  6.53 us (10%)
  matrix products  3.76 us (6%)
  between operations  2.74 us (4%)
  waiting for transfers between devices  0.93 us (1%)
    all_to_all x1, blocking collectives, on_device(): lax.all_to_all(to_far, FAR, 0, 0, axis_index_groups=far_order, tiled=True)  19.5 us
    ppermute x2, starting transfers between devices, from_behind(): return lax.ppermute(block, axis, route)  14.5 us
    all_to_all x1, blocking collectives, on_device(): lax.all_to_all(to_share, SHARE, 0, 0, axis_index_groups=share_order, tile...  8.44 us
    all_to_all x1, starting transfers between devices, on_device(): lax.all_to_all(partial_gram.reshape(share_count, held, LANES), SHARE, 0,...  6.5 us
    all_to_all x1, starting transfers between devices, on_device(): lax.all_to_all(sums, 'slab', 0, 0, axis_index_groups=slab_order, tiled=True)  3.24 us
    pallas_call x1, Pallas kernels, on_device(): pl.pallas_call(own_kernel, out_shape=(kept_near(images), kept_near((3, *i...  2.05 us
    dot_general x2, matrix products, gathered_products(): jnp.einsum('tc,tbj->bcj', chosen, products, precision=lax.Precision.HIGHEST)  1.47 us
  transfers between devices with their start and end apart: 4, of which 1 were waited for; matrix products, arithmetic and copies ran while one was open for 6% of the time, Pallas kernels for 6%

profile of v10, /device:TPU:1, one launch (start us, length us, event | category | flops | bytes accessed | tf_op | source)
XLA Modules:
  0.0 66.4 jit_solution(18350837007531741967)
XLA Ops:
  0.6 8.8 %collective-permute-start = (f32[8,1,16,512]{3,2,0,1:T(8,128)}, f32[8,1,16,512]{3,2,0,1:T(8,128)S(1)}, u32[]{:S(2)}, u32[]{:S(2)}) collective-permute-start(f32[8,1,16,512]{3,2,0,1:T(8,128)} %bitcast.42), channel_id=1, source_target_pairs={{1,0},{2,1},{3,2},{5,4},{6,5},{7,6},{9,8},{10,9},{11,10},{13,12},{... | collective-permute-start | bytes 786440 | tf_op jit(solution)/shard_map/ppermute | solution.py:57
  10.7 0.0 copy-start.2
  10.7 2.0 %own.1 = (f32[8,16,512]{2,1,0:T(8,128)S(1)}, f32[3,8,16,512]{3,2,1,0:T(8,128)S(1)}, f32[3,16,512]{2,1,0:T(8,128)S(1)}, bf16[64,128,128]{2,1,0:T(8,128)(2,1)S(1)}) custom-call(f32[1]{0:T(128)} %copy.39.rate_ref, f32[8,16,512]{2,1,0:T(8,128)} %bitcast.43, f32[3,8,16,512]{3,2,1,0:T(8,128)} %bitcast.41, bf16[64,128,128]{2,1,0:T(8,128)(2,1)} %projector_far.1), custom_call_target="tpu_custom_call" | custom-call | tf_op jit(solution)/shard_map/own/pallas_call | solution.py:384
  12.8 0.0 collective-permute-done
  12.8 0.9 %gram.1 = (f32[8,16,512]{2,1,0:T(8,128)S(1)}, f32[3,8,16,512]{3,2,1,0:T(8,128)S(1)}, f32[384,128]{1,0:T(8,128)}) custom-call(f32[1]{0:T(128)} %copy.39.rate_ref, f32[1]{0:T(128)} %bitcast.keep_ref, f32[8,16,512]{2,1,0:T(8,128)S(1)} %bitcast.39, f32[3,16,512]{2,1,0:T(8,128)S(1)} %get-tuple-element.19.sums_ref, ...), custom_call_target="tpu_custom_call", output_to_operand_aliasing={{0}: (4, {}), {1}: (5, {})} | custom-call | tf_op jit(solution)/shard_map/gram/pallas_call | solution.py:403
  13.7 0.0 copy-start.1
  13.7 0.0 copy-start.3
  13.7 0.1 convert_element_type.20
  13.8 6.5 %all-to-all-start = ((f32[16,24,128]{2,1,0:T(8,128)}), f32[16,24,128]{2,1,0:T(8,128)S(1)}, u32[]{:S(2)}, u32[]{:S(2)}) async-start(f32[16,24,128]{2,1,0:T(8,128)} %bitcast.44), calls=%async_computation | async-start | bytes 393216 | tf_op jit(solution)/shard_map/all_to_all | solution.py:429
  20.3 0.0 copy-done.2
  20.3 0.2 fusion.9
  20.6 1.2 %fusion.3 = f32[64,8,128]{2,1,0:T(8,128)S(1)} fusion(bf16[64,128,128]{2,1,0:T(8,128)(2,1)S(1)} %get-tuple-element.24, bf16[64,8,128]{2,0,1:T(8,128)(2,1)S(1)} %fusion.9), kind=kOutput, calls=%fused_computation.7 | convolution fusion | flops 16777216 | bytes 2490368 | tf_op jit(solution)/shard_map/tij,tbj->tbi/dot_general | solution.py:440
  21.7 0.0 copy-done.1
  21.7 0.0 copy-done.3
  21.7 1.2 %add_divide_fusion = (f32[8,32,128]{2,1,0:T(8,128)S(1)}, f32[8,32,128]{2,1,0:T(8,128)S(1)}) fusion(f32[8,32,128]{2,1,0:T(8,128)S(1)} %bitcast.45, f32[]{:T(128)S(6)} %add.7, f32[]{:T(128)} %bitcast.36, f32[8,32,128]{2,1,0:T(8,128)} %bitcast.46, s32[64]{0:T(128)S(1)} %copy-done.3, f32[64,8,128]{2,1,0:T(8,128)S(1)} %fusion.3), kind=kOutput, calls=%fused_computation.9 | convolution fusion | flops 25298944 | bytes 786696 | tf_op jit(solution)/shard_map/tc,tbj->bcj/dot_general | solution.py:349
  22.9 0.2 fusion.5
  23.2 0.6 fusion.4
  23.8 0.0 copy-start
  23.8 0.3 convolution_bitcast_fusion
  24.2 0.0 all-to-all-done.parts_ref
  24.2 19.5 %all_to_all.20.parts_ref = f32[8,13,2,128]{3,2,1,0:T(2,128)S(1)} all-to-all(f32[8,13,2,128]{3,2,1,0:T(2,128)S(1)} %get-tuple-element.25), channel_id=1, replica_groups={{40,8,0,16,24,56,32,48},{41,9,1,17,25,57,33,49},{42,10,2,18,26,58,34,50..., dimensions={0} | all-to-all | bytes 212992 | tf_op jit(solution)/shard_map/all_to_all | solution.py:463
  43.8 0.5 factor.1
  44.3 8.4 %all_to_all.21.parts_ref = f32[16,13,2,128]{3,2,1,0:T(2,128)S(1)} all-to-all(f32[16,13,2,128]{3,2,1,0:T(2,128)S(1)} %factor.1), channel_id=1, replica_groups={{324,0,4,64,128,384,68,132,192,256,388,448,196,260,320,452},{325,1,5,65..., dimensions={0} | all-to-all | bytes 425984 | tf_op jit(solution)/shard_map/all_to_all | solution.py:474
  52.7 0.6 slice.1
  53.3 5.7 %collective-permute-start.1 = (f32[8,16,512]{2,1,0:T(8,128)S(1)}, f32[8,16,512]{2,1,0:T(8,128)S(1)}, u32[]{:S(2)}, u32[]{:S(2)}) collective-permute-start(f32[8,16,512]{2,1,0:T(8,128)S(1)} %get-tuple-element.28.slice_ref), channel_id=1, source_target_pairs={{0,1},{1,2},{2,3},{4,5},{5,6},{6,7},{8,9},{9,10},{10,11},{12,13},{... | collective-permute-start | bytes 786440 | tf_op jit(solution)/shard_map/ppermute | solution.py:57
  59.0 3.2 %all-to-all-start.3 = ((f32[4,2,128]{2,1,0:T(2,128)}), f32[4,2,128]{2,1,0:T(2,128)S(1)}, u32[]{:S(2)}, u32[]{:S(2)}) async-start(f32[4,2,128]{2,1,0:T(2,128)} %get-tuple-element.33), calls=%async_computation.3 | async-start | bytes 8192 | tf_op jit(solution)/shard_map/all_to_all | solution.py:496
  62.9 0.0 copy-done
  62.9 1.1 %rest.1 = (f32[3,8,16,512]{3,2,1,0:T(8,128)}, f32[8,16,512]{2,1,0:T(8,128)S(1)}, f32[8,32,128]{2,1,0:T(8,128)}) custom-call(f32[1]{0:T(128)S(6)} %copy.40.rate_ref, f32[1]{0:T(128)} %bitcast.keep_ref, f32[384,128]{1,0:T(8,128)S(1)} %get-tuple-element.27.factor_ref, f32[3,8,16,512]{3,2,1,0:T(8,128)S(1)} %get-tuple-element.26.cand_ref, ...), custom_call_target="tpu_custom_call" | custom-call | tf_op jit(solution)/shard_map/rest/pallas_call | solution.py:497
  64.0 0.0 collective-permute-done.1.prior_ref
  64.0 0.7 %finish.1.updated_far = f32[8,16,512]{2,1,0:T(8,128)} custom-call(f32[1]{0:T(128)S(6)} %copy.40.rate_ref, f32[8,16,512]{2,1,0:T(8,128)S(1)} %get-tuple-element.30.ready_ref, f32[8,16,512]{2,1,0:T(8,128)S(1)} %collective-permute-done.1.prior_ref), custom_call_target="tpu_custom_call" | custom-call | tf_op jit(solution)/shard_map/finish/pallas_call | solution.py:519
  64.8 0.9 %all-to-all-done.3.sums_ref = f32[4,2,128]{2,1,0:T(2,128)S(1)} async-done(((f32[4,2,128]{2,1,0:T(2,128)}), f32[4,2,128]{2,1,0:T(2,128)S(1)}, u32[]{:S(2)}, u32[]{:S(2)}) %all-to-all-start.3) | async-done | bytes 4128 | tf_op jit(solution)/shard_map/all_to_all | solution.py:496
  65.7 0.6 totals.1
  (3 shorter events, 0.1 us)
Async XLA Ops:
  0.6 12.2 %collective-permute-start = (f32[8,1,16,512]{3,2,0,1:T(8,128)}, f32[8,1,16,512]{3,2,0,1:T(8,128)S(1)}, u32[]{:S(2)}, u32[]{:S(2)}) collective-permute-start(f32[8,1,16,512]{3,2,0,1:T(8,128)} %bitcast.42), channel_id=1, source_target_pairs={{1,0},{2,1},{3,2},{5,4},{6,5},{7,6},{9,8},{10,9},{11,10},{13,12},{... | collective-permute-start | bytes 786440 | tf_op jit(solution)/shard_map/ppermute | solution.py:57
  10.7 9.6 %copy-start.2 = (s32[64]{0:T(128)S(1)}, s32[64]{0:T(128)}, u32[]{:S(2)}) copy-start(s32[64]{0:T(128)} %param.18) | copy-start | bytes 772
  13.7 8.1 %copy-start.1 = (f32[8,1,4096]{2,1,0:T(1,128)S(1)}, f32[8,1,4096]{2,1,0:T(1,128)}, u32[]{:S(2)}) copy-start(f32[8,1,4096]{2,1,0:T(1,128)} %param.14) | copy-start | bytes 393220
  13.7 8.1 %copy-start.3 = (s32[64]{0:T(128)S(1)}, s32[64]{0:T(128)}, u32[]{:S(2)}) copy-start(s32[64]{0:T(128)} %param.17) | copy-start | bytes 772
  13.8 10.4 %all-to-all-start = ((f32[16,24,128]{2,1,0:T(8,128)}), f32[16,24,128]{2,1,0:T(8,128)S(1)}, u32[]{:S(2)}, u32[]{:S(2)}) async-start(f32[16,24,128]{2,1,0:T(8,128)} %bitcast.44), calls=%async_computation | async-start | bytes 393216 | tf_op jit(solution)/shard_map/all_to_all | solution.py:429
  23.8 39.1 %copy-start = (f32[8,1,16,512]{3,2,1,0:T(8,128)S(1)}, f32[8,1,16,512]{3,2,1,0:T(8,128)}, u32[]{:S(2)}) copy-start(f32[8,1,16,512]{3,2,1,0:T(8,128)} %param.11) | copy-start | bytes 786436
  53.3 10.7 %collective-permute-start.1 = (f32[8,16,512]{2,1,0:T(8,128)S(1)}, f32[8,16,512]{2,1,0:T(8,128)S(1)}, u32[]{:S(2)}, u32[]{:S(2)}) collective-permute-start(f32[8,16,512]{2,1,0:T(8,128)S(1)} %get-tuple-element.28.slice_ref), channel_id=1, source_target_pairs={{0,1},{1,2},{2,3},{4,5},{5,6},{6,7},{8,9},{9,10},{10,11},{12,13},{... | collective-permute-start | bytes 786440 | tf_op jit(solution)/shard_map/ppermute | solution.py:57
  59.0 6.7 %all-to-all-start.3 = ((f32[4,2,128]{2,1,0:T(2,128)}), f32[4,2,128]{2,1,0:T(2,128)S(1)}, u32[]{:S(2)}, u32[]{:S(2)}) async-start(f32[4,2,128]{2,1,0:T(2,128)} %get-tuple-element.33), calls=%async_computation.3 | async-start | bytes 8192 | tf_op jit(solution)/shard_map/all_to_all | solution.py:496

commit v11 on v10

--- a/solution.py
+++ b/solution.py
@@ -425,7 +425,7 @@
         near(duals),
     )
     share_order = [by_distance(SHARE, (2, 1, 1))]
-    far_order = [by_distance((FAR,), (far_count // 2 + 1,))]
+    far_order = [by_distance((FAR,), (far_count // 2 + 2,))]
     gram_parts = lax.all_to_all(
         partial_gram.reshape(share_count, held, LANES),
         SHARE,

time: 66.8 us -> 69.6 us (1.042)
  blocking collectives: 28 us -> 30.9 us
    all_to_all x1, blocking collectives: 19.5 us -> 22.5 us  [on_device(): lax.all_to_all(to_far, FAR, 0, 0, axis_index_groups=far_order, tiled=True)]
  transfers between devices with their start and end apart: 4 -> 4, of which waited for: 1 -> 1; matrix products, arithmetic and copies ran while one was open for 6% -> 5% of each run, Pallas kernels for 6% -> 6%
where the time goes in v11:
time: 69.6 us; the launch traced here: 69.2 us
  blocking collectives  30.9 us (44%)
  starting transfers between devices  24.1 us (35%)
  Pallas kernels  6.53 us (9%)
  matrix products  3.76 us (5%)
  between operations  2.74 us (4%)
  waiting for transfers between devices  0.93 us (1%)
    all_to_all x1, blocking collectives, on_device(): lax.all_to_all(to_far, FAR, 0, 0, axis_index_groups=far_order, tiled=True)  22.5 us
    ppermute x2, starting transfers between devices, from_behind(): return lax.ppermute(block, axis, route)  14.4 us
    all_to_all x1, blocking collectives, on_device(): lax.all_to_all(to_share, SHARE, 0, 0, axis_index_groups=share_order, tile...  8.43 us
    all_to_all x1, starting transfers between devices, on_device(): lax.all_to_all(partial_gram.reshape(share_count, held, LANES), SHARE, 0,...  6.5 us
    all_to_all x1, starting transfers between devices, on_device(): lax.all_to_all(sums, 'slab', 0, 0, axis_index_groups=slab_order, tiled=True)  3.24 us
    pallas_call x1, Pallas kernels, on_device(): pl.pallas_call(own_kernel, out_shape=(kept_near(images), kept_near((3, *i...  2.05 us
    dot_general x2, matrix products, gathered_products(): jnp.einsum('tc,tbj->bcj', chosen, products, precision=lax.Precision.HIGHEST)  1.47 us
  transfers between devices with their start and end apart: 4, of which 1 were waited for; matrix products, arithmetic and copies ran while one was open for 5% of the time, Pallas kernels for 6%

profile of v11, /device:TPU:1, one launch (start us, length us, event | category | flops | bytes accessed | tf_op | source)
XLA Modules:
  0.0 69.2 jit_solution(6570229913799121241)
XLA Ops:
  0.6 8.8 %collective-permute-start = (f32[8,1,16,512]{3,2,0,1:T(8,128)}, f32[8,1,16,512]{3,2,0,1:T(8,128)S(1)}, u32[]{:S(2)}, u32[]{:S(2)}) collective-permute-start(f32[8,1,16,512]{3,2,0,1:T(8,128)} %bitcast.42), channel_id=1, source_target_pairs={{1,0},{2,1},{3,2},{5,4},{6,5},{7,6},{9,8},{10,9},{11,10},{13,12},{... | collective-permute-start | bytes 786440 | tf_op jit(solution)/shard_map/ppermute | solution.py:57
  10.7 0.0 copy-start.2
  10.7 2.0 %own.1 = (f32[8,16,512]{2,1,0:T(8,128)S(1)}, f32[3,8,16,512]{3,2,1,0:T(8,128)S(1)}, f32[3,16,512]{2,1,0:T(8,128)S(1)}, bf16[64,128,128]{2,1,0:T(8,128)(2,1)S(1)}) custom-call(f32[1]{0:T(128)} %copy.39.rate_ref, f32[8,16,512]{2,1,0:T(8,128)} %bitcast.43, f32[3,8,16,512]{3,2,1,0:T(8,128)} %bitcast.41, bf16[64,128,128]{2,1,0:T(8,128)(2,1)} %projector_far.1), custom_call_target="tpu_custom_call" | custom-call | tf_op jit(solution)/shard_map/own/pallas_call | solution.py:384
  12.8 0.0 collective-permute-done
  12.8 0.9 %gram.1 = (f32[8,16,512]{2,1,0:T(8,128)S(1)}, f32[3,8,16,512]{3,2,1,0:T(8,128)S(1)}, f32[384,128]{1,0:T(8,128)}) custom-call(f32[1]{0:T(128)} %copy.39.rate_ref, f32[1]{0:T(128)} %bitcast.keep_ref, f32[8,16,512]{2,1,0:T(8,128)S(1)} %bitcast.39, f32[3,16,512]{2,1,0:T(8,128)S(1)} %get-tuple-element.19.sums_ref, ...), custom_call_target="tpu_custom_call", output_to_operand_aliasing={{0}: (4, {}), {1}: (5, {})} | custom-call | tf_op jit(solution)/shard_map/gram/pallas_call | solution.py:403
  13.7 0.0 copy-start.1
  13.7 0.0 copy-start.3
  13.7 0.1 convert_element_type.20
  13.8 6.5 %all-to-all-start = ((f32[16,24,128]{2,1,0:T(8,128)}), f32[16,24,128]{2,1,0:T(8,128)S(1)}, u32[]{:S(2)}, u32[]{:S(2)}) async-start(f32[16,24,128]{2,1,0:T(8,128)} %bitcast.44), calls=%async_computation | async-start | bytes 393216 | tf_op jit(solution)/shard_map/all_to_all | solution.py:429
  20.3 0.0 copy-done.2
  20.3 0.2 fusion.9
  20.6 1.2 %fusion.3 = f32[64,8,128]{2,1,0:T(8,128)S(1)} fusion(bf16[64,128,128]{2,1,0:T(8,128)(2,1)S(1)} %get-tuple-element.24, bf16[64,8,128]{2,0,1:T(8,128)(2,1)S(1)} %fusion.9), kind=kOutput, calls=%fused_computation.7 | convolution fusion | flops 16777216 | bytes 2490368 | tf_op jit(solution)/shard_map/tij,tbj->tbi/dot_general | solution.py:440
  21.7 0.0 copy-done.1
  21.7 0.0 copy-done.3
  21.7 1.2 %add_divide_fusion = (f32[8,32,128]{2,1,0:T(8,128)S(1)}, f32[8,32,128]{2,1,0:T(8,128)S(1)}) fusion(f32[8,32,128]{2,1,0:T(8,128)S(1)} %bitcast.45, f32[]{:T(128)S(6)} %add.7, f32[]{:T(128)} %bitcast.36, f32[8,32,128]{2,1,0:T(8,128)} %bitcast.46, s32[64]{0:T(128)S(1)} %copy-done.3, f32[64,8,128]{2,1,0:T(8,128)S(1)} %fusion.3), kind=kOutput, calls=%fused_computation.9 | convolution fusion | flops 25298944 | bytes 786696 | tf_op jit(solution)/shard_map/tc,tbj->bcj/dot_general | solution.py:349
  22.9 0.2 fusion.5
  23.2 0.6 fusion.4
  23.8 0.0 copy-start
  23.8 0.3 convolution_bitcast_fusion
  24.2 0.0 all-to-all-done.parts_ref
  24.2 22.5 %all_to_all.20.parts_ref = f32[8,13,2,128]{3,2,1,0:T(2,128)S(1)} all-to-all(f32[8,13,2,128]{3,2,1,0:T(2,128)S(1)} %get-tuple-element.25), channel_id=1, replica_groups={{48,16,8,24,0,32,40,56},{49,17,9,25,1,33,41,57},{50,18,10,26,2,34,42,58..., dimensions={0} | all-to-all | bytes 212992 | tf_op jit(solution)/shard_map/all_to_all | solution.py:463
  46.7 0.5 factor.1
  47.2 8.4 %all_to_all.21.parts_ref = f32[16,13,2,128]{3,2,1,0:T(2,128)S(1)} all-to-all(f32[16,13,2,128]{3,2,1,0:T(2,128)S(1)} %factor.1), channel_id=1, replica_groups={{324,0,4,64,128,384,68,132,192,256,388,448,196,260,320,452},{325,1,5,65..., dimensions={0} | all-to-all | bytes 425984 | tf_op jit(solution)/shard_map/all_to_all | solution.py:474
  55.7 0.6 slice.1
  56.3 5.6 %collective-permute-start.1 = (f32[8,16,512]{2,1,0:T(8,128)S(1)}, f32[8,16,512]{2,1,0:T(8,128)S(1)}, u32[]{:S(2)}, u32[]{:S(2)}) collective-permute-start(f32[8,16,512]{2,1,0:T(8,128)S(1)} %get-tuple-element.28.slice_ref), channel_id=1, source_target_pairs={{0,1},{1,2},{2,3},{4,5},{5,6},{6,7},{8,9},{9,10},{10,11},{12,13},{... | collective-permute-start | bytes 786440 | tf_op jit(solution)/shard_map/ppermute | solution.py:57
  61.9 3.2 %all-to-all-start.3 = ((f32[4,2,128]{2,1,0:T(2,128)}), f32[4,2,128]{2,1,0:T(2,128)S(1)}, u32[]{:S(2)}, u32[]{:S(2)}) async-start(f32[4,2,128]{2,1,0:T(2,128)} %get-tuple-element.33), calls=%async_computation.3 | async-start | bytes 8192 | tf_op jit(solution)/shard_map/all_to_all | solution.py:496
  65.8 0.0 copy-done
  65.8 1.1 %rest.1 = (f32[3,8,16,512]{3,2,1,0:T(8,128)}, f32[8,16,512]{2,1,0:T(8,128)S(1)}, f32[8,32,128]{2,1,0:T(8,128)}) custom-call(f32[1]{0:T(128)S(6)} %copy.40.rate_ref, f32[1]{0:T(128)} %bitcast.keep_ref, f32[384,128]{1,0:T(8,128)S(1)} %get-tuple-element.27.factor_ref, f32[3,8,16,512]{3,2,1,0:T(8,128)S(1)} %get-tuple-element.26.cand_ref, ...), custom_call_target="tpu_custom_call" | custom-call | tf_op jit(solution)/shard_map/rest/pallas_call | solution.py:497
  66.9 0.0 collective-permute-done.1.prior_ref
  66.9 0.7 %finish.1.updated_far = f32[8,16,512]{2,1,0:T(8,128)} custom-call(f32[1]{0:T(128)S(6)} %copy.40.rate_ref, f32[8,16,512]{2,1,0:T(8,128)S(1)} %get-tuple-element.30.ready_ref, f32[8,16,512]{2,1,0:T(8,128)S(1)} %collective-permute-done.1.prior_ref), custom_call_target="tpu_custom_call" | custom-call | tf_op jit(solution)/shard_map/finish/pallas_call | solution.py:519
  67.6 0.9 %all-to-all-done.3.sums_ref = f32[4,2,128]{2,1,0:T(2,128)S(1)} async-done(((f32[4,2,128]{2,1,0:T(2,128)}), f32[4,2,128]{2,1,0:T(2,128)S(1)}, u32[]{:S(2)}, u32[]{:S(2)}) %all-to-all-start.3) | async-done | bytes 4128 | tf_op jit(solution)/shard_map/all_to_all | solution.py:496
  68.6 0.6 totals.1
  (3 shorter events, 0.1 us)
Async XLA Ops:
  0.6 12.2 %collective-permute-start = (f32[8,1,16,512]{3,2,0,1:T(8,128)}, f32[8,1,16,512]{3,2,0,1:T(8,128)S(1)}, u32[]{:S(2)}, u32[]{:S(2)}) collective-permute-start(f32[8,1,16,512]{3,2,0,1:T(8,128)} %bitcast.42), channel_id=1, source_target_pairs={{1,0},{2,1},{3,2},{5,4},{6,5},{7,6},{9,8},{10,9},{11,10},{13,12},{... | collective-permute-start | bytes 786440 | tf_op jit(solution)/shard_map/ppermute | solution.py:57
  10.7 9.6 %copy-start.2 = (s32[64]{0:T(128)S(1)}, s32[64]{0:T(128)}, u32[]{:S(2)}) copy-start(s32[64]{0:T(128)} %param.18) | copy-start | bytes 772
  13.7 8.1 %copy-start.1 = (f32[8,1,4096]{2,1,0:T(1,128)S(1)}, f32[8,1,4096]{2,1,0:T(1,128)}, u32[]{:S(2)}) copy-start(f32[8,1,4096]{2,1,0:T(1,128)} %param.14) | copy-start | bytes 393220
  13.7 8.1 %copy-start.3 = (s32[64]{0:T(128)S(1)}, s32[64]{0:T(128)}, u32[]{:S(2)}) copy-start(s32[64]{0:T(128)} %param.17) | copy-start | bytes 772
  13.8 10.4 %all-to-all-start = ((f32[16,24,128]{2,1,0:T(8,128)}), f32[16,24,128]{2,1,0:T(8,128)S(1)}, u32[]{:S(2)}, u32[]{:S(2)}) async-start(f32[16,24,128]{2,1,0:T(8,128)} %bitcast.44), calls=%async_computation | async-start | bytes 393216 | tf_op jit(solution)/shard_map/all_to_all | solution.py:429
  23.8 42.0 %copy-start = (f32[8,1,16,512]{3,2,1,0:T(8,128)S(1)}, f32[8,1,16,512]{3,2,1,0:T(8,128)}, u32[]{:S(2)}) copy-start(f32[8,1,16,512]{3,2,1,0:T(8,128)} %param.11) | copy-start | bytes 786436
  56.3 10.6 %collective-permute-start.1 = (f32[8,16,512]{2,1,0:T(8,128)S(1)}, f32[8,16,512]{2,1,0:T(8,128)S(1)}, u32[]{:S(2)}, u32[]{:S(2)}) collective-permute-start(f32[8,16,512]{2,1,0:T(8,128)S(1)} %get-tuple-element.28.slice_ref), channel_id=1, source_target_pairs={{0,1},{1,2},{2,3},{4,5},{5,6},{6,7},{8,9},{9,10},{10,11},{12,13},{... | collective-permute-start | bytes 786440 | tf_op jit(solution)/shard_map/ppermute | solution.py:57
  61.9 6.7 %all-to-all-start.3 = ((f32[4,2,128]{2,1,0:T(2,128)}), f32[4,2,128]{2,1,0:T(2,128)S(1)}, u32[]{:S(2)}, u32[]{:S(2)}) async-start(f32[4,2,128]{2,1,0:T(2,128)} %get-tuple-element.33), calls=%async_computation.3 | async-start | bytes 8192 | tf_op jit(solution)/shard_map/all_to_all | solution.py:496

commit v12 on v11

--- a/solution.py
+++ b/solution.py
@@ -425,7 +425,7 @@
         near(duals),
     )
     share_order = [by_distance(SHARE, (2, 1, 1))]
-    far_order = [by_distance((FAR,), (far_count // 2 + 2,))]
+    far_order = [by_distance((FAR,), (far_count // 2,))]
     gram_parts = lax.all_to_all(
         partial_gram.reshape(share_count, held, LANES),
         SHARE,

time: 69.6 us -> 67.6 us (0.971)
  blocking collectives: 30.9 us -> 29 us
    all_to_all x1, blocking collectives: 22.5 us -> 20.3 us  [on_device(): lax.all_to_all(to_far, FAR, 0, 0, axis_index_groups=far_order, tiled=True)]
  transfers between devices with their start and end apart: 4 -> 4, of which waited for: 1 -> 1; matrix products, arithmetic and copies ran while one was open for 5% -> 6% of each run, Pallas kernels for 6% -> 6%
where the time goes in v12:
time: 67.6 us; the launch traced here: 67.2 us
  blocking collectives  29 us (43%)
  starting transfers between devices  24.1 us (36%)
  Pallas kernels  6.53 us (10%)
  matrix products  3.76 us (6%)
  between operations  2.74 us (4%)
  waiting for transfers between devices  0.93 us (1%)
    all_to_all x1, blocking collectives, on_device(): lax.all_to_all(to_far, FAR, 0, 0, axis_index_groups=far_order, tiled=True)  20.3 us
    ppermute x2, starting transfers between devices, from_behind(): return lax.ppermute(block, axis, route)  14.3 us
    all_to_all x1, blocking collectives, on_device(): lax.all_to_all(to_share, SHARE, 0, 0, axis_index_groups=share_order, tile...  8.72 us
    all_to_all x1, starting transfers between devices, on_device(): lax.all_to_all(partial_gram.reshape(share_count, held, LANES), SHARE, 0,...  6.5 us
    all_to_all x1, starting transfers between devices, on_device(): lax.all_to_all(sums, 'slab', 0, 0, axis_index_groups=slab_order, tiled=True)  3.24 us
    pallas_call x1, Pallas kernels, on_device(): pl.pallas_call(own_kernel, out_shape=(kept_near(images), kept_near((3, *i...  2.05 us
    dot_general x2, matrix products, gathered_products(): jnp.einsum('tc,tbj->bcj', chosen, products, precision=lax.Precision.HIGHEST)  1.47 us
  transfers between devices with their start and end apart: 4, of which 1 were waited for; matrix products, arithmetic and copies ran while one was open for 6% of the time, Pallas kernels for 6%

profile of v12, /device:TPU:1, one launch (start us, length us, event | category | flops | bytes accessed | tf_op | source)
XLA Modules:
  0.0 67.2 jit_solution(9648606775406056010)
XLA Ops:
  0.6 8.8 %collective-permute-start = (f32[8,1,16,512]{3,2,0,1:T(8,128)}, f32[8,1,16,512]{3,2,0,1:T(8,128)S(1)}, u32[]{:S(2)}, u32[]{:S(2)}) collective-permute-start(f32[8,1,16,512]{3,2,0,1:T(8,128)} %bitcast.42), channel_id=1, source_target_pairs={{1,0},{2,1},{3,2},{5,4},{6,5},{7,6},{9,8},{10,9},{11,10},{13,12},{... | collective-permute-start | bytes 786440 | tf_op jit(solution)/shard_map/ppermute | solution.py:57
  10.7 0.0 copy-start.2
  10.7 2.0 %own.1 = (f32[8,16,512]{2,1,0:T(8,128)S(1)}, f32[3,8,16,512]{3,2,1,0:T(8,128)S(1)}, f32[3,16,512]{2,1,0:T(8,128)S(1)}, bf16[64,128,128]{2,1,0:T(8,128)(2,1)S(1)}) custom-call(f32[1]{0:T(128)} %copy.39.rate_ref, f32[8,16,512]{2,1,0:T(8,128)} %bitcast.43, f32[3,8,16,512]{3,2,1,0:T(8,128)} %bitcast.41, bf16[64,128,128]{2,1,0:T(8,128)(2,1)} %projector_far.1), custom_call_target="tpu_custom_call" | custom-call | tf_op jit(solution)/shard_map/own/pallas_call | solution.py:384
  12.8 0.0 collective-permute-done
  12.8 0.9 %gram.1 = (f32[8,16,512]{2,1,0:T(8,128)S(1)}, f32[3,8,16,512]{3,2,1,0:T(8,128)S(1)}, f32[384,128]{1,0:T(8,128)}) custom-call(f32[1]{0:T(128)} %copy.39.rate_ref, f32[1]{0:T(128)} %bitcast.keep_ref, f32[8,16,512]{2,1,0:T(8,128)S(1)} %bitcast.39, f32[3,16,512]{2,1,0:T(8,128)S(1)} %get-tuple-element.19.sums_ref, ...), custom_call_target="tpu_custom_call", output_to_operand_aliasing={{0}: (4, {}), {1}: (5, {})} | custom-call | tf_op jit(solution)/shard_map/gram/pallas_call | solution.py:403
  13.7 0.0 copy-start.1
  13.7 0.0 copy-start.3
  13.7 0.1 convert_element_type.20
  13.8 6.5 %all-to-all-start = ((f32[16,24,128]{2,1,0:T(8,128)}), f32[16,24,128]{2,1,0:T(8,128)S(1)}, u32[]{:S(2)}, u32[]{:S(2)}) async-start(f32[16,24,128]{2,1,0:T(8,128)} %bitcast.44), calls=%async_computation | async-start | bytes 393216 | tf_op jit(solution)/shard_map/all_to_all | solution.py:429
  20.3 0.0 copy-done.2
  20.3 0.2 fusion.9
  20.6 1.2 %fusion.3 = f32[64,8,128]{2,1,0:T(8,128)S(1)} fusion(bf16[64,128,128]{2,1,0:T(8,128)(2,1)S(1)} %get-tuple-element.24, bf16[64,8,128]{2,0,1:T(8,128)(2,1)S(1)} %fusion.9), kind=kOutput, calls=%fused_computation.7 | convolution fusion | flops 16777216 | bytes 2490368 | tf_op jit(solution)/shard_map/tij,tbj->tbi/dot_general | solution.py:440
  21.7 0.0 copy-done.1
  21.7 0.0 copy-done.3
  21.7 1.2 %add_divide_fusion = (f32[8,32,128]{2,1,0:T(8,128)S(1)}, f32[8,32,128]{2,1,0:T(8,128)S(1)}) fusion(f32[8,32,128]{2,1,0:T(8,128)S(1)} %bitcast.45, f32[]{:T(128)S(6)} %add.7, f32[]{:T(128)} %bitcast.36, f32[8,32,128]{2,1,0:T(8,128)} %bitcast.46, s32[64]{0:T(128)S(1)} %copy-done.3, f32[64,8,128]{2,1,0:T(8,128)S(1)} %fusion.3), kind=kOutput, calls=%fused_computation.9 | convolution fusion | flops 25298944 | bytes 786696 | tf_op jit(solution)/shard_map/tc,tbj->bcj/dot_general | solution.py:349
  22.9 0.2 fusion.5
  23.2 0.6 fusion.4
  23.8 0.0 copy-start
  23.8 0.3 convolution_bitcast_fusion
  24.2 0.0 all-to-all-done.parts_ref
  24.2 20.3 %all_to_all.20.parts_ref = f32[8,13,2,128]{3,2,1,0:T(2,128)S(1)} all-to-all(f32[8,13,2,128]{3,2,1,0:T(2,128)S(1)} %get-tuple-element.25), channel_id=1, replica_groups={{32,0,8,56,16,48,24,40},{33,1,9,57,17,49,25,41},{34,2,10,58,18,50,26,42..., dimensions={0} | all-to-all | bytes 212992 | tf_op jit(solution)/shard_map/all_to_all | solution.py:463
  44.5 0.5 factor.1
  45.0 8.7 %all_to_all.21.parts_ref = f32[16,13,2,128]{3,2,1,0:T(2,128)S(1)} all-to-all(f32[16,13,2,128]{3,2,1,0:T(2,128)S(1)} %factor.1), channel_id=1, replica_groups={{324,0,4,64,128,384,68,132,192,256,388,448,196,260,320,452},{325,1,5,65..., dimensions={0} | all-to-all | bytes 425984 | tf_op jit(solution)/shard_map/all_to_all | solution.py:474
  53.7 0.6 slice.1
  54.3 5.6 %collective-permute-start.1 = (f32[8,16,512]{2,1,0:T(8,128)S(1)}, f32[8,16,512]{2,1,0:T(8,128)S(1)}, u32[]{:S(2)}, u32[]{:S(2)}) collective-permute-start(f32[8,16,512]{2,1,0:T(8,128)S(1)} %get-tuple-element.28.slice_ref), channel_id=1, source_target_pairs={{0,1},{1,2},{2,3},{4,5},{5,6},{6,7},{8,9},{9,10},{10,11},{12,13},{... | collective-permute-start | bytes 786440 | tf_op jit(solution)/shard_map/ppermute | solution.py:57
  59.9 3.2 %all-to-all-start.3 = ((f32[4,2,128]{2,1,0:T(2,128)}), f32[4,2,128]{2,1,0:T(2,128)S(1)}, u32[]{:S(2)}, u32[]{:S(2)}) async-start(f32[4,2,128]{2,1,0:T(2,128)} %get-tuple-element.33), calls=%async_computation.3 | async-start | bytes 8192 | tf_op jit(solution)/shard_map/all_to_all | solution.py:496
  63.8 0.0 copy-done
  63.8 1.1 %rest.1 = (f32[3,8,16,512]{3,2,1,0:T(8,128)}, f32[8,16,512]{2,1,0:T(8,128)S(1)}, f32[8,32,128]{2,1,0:T(8,128)}) custom-call(f32[1]{0:T(128)S(6)} %copy.40.rate_ref, f32[1]{0:T(128)} %bitcast.keep_ref, f32[384,128]{1,0:T(8,128)S(1)} %get-tuple-element.27.factor_ref, f32[3,8,16,512]{3,2,1,0:T(8,128)S(1)} %get-tuple-element.26.cand_ref, ...), custom_call_target="tpu_custom_call" | custom-call | tf_op jit(solution)/shard_map/rest/pallas_call | solution.py:497
  64.9 0.0 collective-permute-done.1.prior_ref
  64.9 0.7 %finish.1.updated_far = f32[8,16,512]{2,1,0:T(8,128)} custom-call(f32[1]{0:T(128)S(6)} %copy.40.rate_ref, f32[8,16,512]{2,1,0:T(8,128)S(1)} %get-tuple-element.30.ready_ref, f32[8,16,512]{2,1,0:T(8,128)S(1)} %collective-permute-done.1.prior_ref), custom_call_target="tpu_custom_call" | custom-call | tf_op jit(solution)/shard_map/finish/pallas_call | solution.py:519
  65.6 0.9 %all-to-all-done.3.sums_ref = f32[4,2,128]{2,1,0:T(2,128)S(1)} async-done(((f32[4,2,128]{2,1,0:T(2,128)}), f32[4,2,128]{2,1,0:T(2,128)S(1)}, u32[]{:S(2)}, u32[]{:S(2)}) %all-to-all-start.3) | async-done | bytes 4128 | tf_op jit(solution)/shard_map/all_to_all | solution.py:496
  66.6 0.6 totals.1
  (3 shorter events, 0.1 us)
Async XLA Ops:
  0.6 12.2 %collective-permute-start = (f32[8,1,16,512]{3,2,0,1:T(8,128)}, f32[8,1,16,512]{3,2,0,1:T(8,128)S(1)}, u32[]{:S(2)}, u32[]{:S(2)}) collective-permute-start(f32[8,1,16,512]{3,2,0,1:T(8,128)} %bitcast.42), channel_id=1, source_target_pairs={{1,0},{2,1},{3,2},{5,4},{6,5},{7,6},{9,8},{10,9},{11,10},{13,12},{... | collective-permute-start | bytes 786440 | tf_op jit(solution)/shard_map/ppermute | solution.py:57
  10.7 9.6 %copy-start.2 = (s32[64]{0:T(128)S(1)}, s32[64]{0:T(128)}, u32[]{:S(2)}) copy-start(s32[64]{0:T(128)} %param.18) | copy-start | bytes 772
  13.7 8.1 %copy-start.1 = (f32[8,1,4096]{2,1,0:T(1,128)S(1)}, f32[8,1,4096]{2,1,0:T(1,128)}, u32[]{:S(2)}) copy-start(f32[8,1,4096]{2,1,0:T(1,128)} %param.14) | copy-start | bytes 393220
  13.7 8.1 %copy-start.3 = (s32[64]{0:T(128)S(1)}, s32[64]{0:T(128)}, u32[]{:S(2)}) copy-start(s32[64]{0:T(128)} %param.17) | copy-start | bytes 772
  13.8 10.4 %all-to-all-start = ((f32[16,24,128]{2,1,0:T(8,128)}), f32[16,24,128]{2,1,0:T(8,128)S(1)}, u32[]{:S(2)}, u32[]{:S(2)}) async-start(f32[16,24,128]{2,1,0:T(8,128)} %bitcast.44), calls=%async_computation | async-start | bytes 393216 | tf_op jit(solution)/shard_map/all_to_all | solution.py:429
  23.8 40.0 %copy-start = (f32[8,1,16,512]{3,2,1,0:T(8,128)S(1)}, f32[8,1,16,512]{3,2,1,0:T(8,128)}, u32[]{:S(2)}) copy-start(f32[8,1,16,512]{3,2,1,0:T(8,128)} %param.11) | copy-start | bytes 786436
  54.3 10.6 %collective-permute-start.1 = (f32[8,16,512]{2,1,0:T(8,128)S(1)}, f32[8,16,512]{2,1,0:T(8,128)S(1)}, u32[]{:S(2)}, u32[]{:S(2)}) collective-permute-start(f32[8,16,512]{2,1,0:T(8,128)S(1)} %get-tuple-element.28.slice_ref), channel_id=1, source_target_pairs={{0,1},{1,2},{2,3},{4,5},{5,6},{6,7},{8,9},{9,10},{10,11},{12,13},{... | collective-permute-start | bytes 786440 | tf_op jit(solution)/shard_map/ppermute | solution.py:57
  59.9 6.7 %all-to-all-start.3 = ((f32[4,2,128]{2,1,0:T(2,128)}), f32[4,2,128]{2,1,0:T(2,128)S(1)}, u32[]{:S(2)}, u32[]{:S(2)}) async-start(f32[4,2,128]{2,1,0:T(2,128)} %get-tuple-element.33), calls=%async_computation.3 | async-start | bytes 8192 | tf_op jit(solution)/shard_map/all_to_all | solution.py:496

commit v13 on v12

--- a/solution.py
+++ b/solution.py
@@ -425,7 +425,7 @@
         near(duals),
     )
     share_order = [by_distance(SHARE, (2, 1, 1))]
-    far_order = [by_distance((FAR,), (far_count // 2,))]
+    far_order = [[(far_count // 2 + 1 + i) % far_count for i in range(far_count)]]
     gram_parts = lax.all_to_all(
         partial_gram.reshape(share_count, held, LANES),
         SHARE,

time: 67.6 us -> 67.2 us (level)
  blocking collectives: 29 us -> 28.1 us
    all_to_all x1, blocking collectives: 20.3 us -> 19.6 us  [on_device(): lax.all_to_all(to_far, FAR, 0, 0, axis_index_groups=far_order, tiled=True)]
where the time goes in v13:
time: 67.2 us; the launch traced here: 66.8 us
  blocking collectives  28.1 us (42%)
  starting transfers between devices  24.6 us (37%)
  Pallas kernels  6.53 us (10%)
  matrix products  3.76 us (6%)
  between operations  2.74 us (4%)
  waiting for transfers between devices  0.93 us (1%)
    all_to_all x1, blocking collectives, on_device(): lax.all_to_all(to_far, FAR, 0, 0, axis_index_groups=far_order, tiled=True)  19.6 us
    ppermute x2, starting transfers between devices, from_behind(): return lax.ppermute(block, axis, route)  14.8 us
    all_to_all x1, blocking collectives, on_device(): lax.all_to_all(to_share, SHARE, 0, 0, axis_index_groups=share_order, tile...  8.58 us
    all_to_all x1, starting transfers between devices, on_device(): lax.all_to_all(partial_gram.reshape(share_count, held, LANES), SHARE, 0,...  6.5 us
    all_to_all x1, starting transfers between devices, on_device(): lax.all_to_all(sums, 'slab', 0, 0, axis_index_groups=slab_order, tiled=True)  3.24 us
    pallas_call x1, Pallas kernels, on_device(): pl.pallas_call(own_kernel, out_shape=(kept_near(images), kept_near((3, *i...  2.05 us
    dot_general x2, matrix products, gathered_products(): jnp.einsum('tc,tbj->bcj', chosen, products, precision=lax.Precision.HIGHEST)  1.47 us
  transfers between devices with their start and end apart: 4, of which 1 were waited for; matrix products, arithmetic and copies ran while one was open for 6% of the time, Pallas kernels for 6%

profile of v13, /device:TPU:1, one launch (start us, length us, event | category | flops | bytes accessed | tf_op | source)
XLA Modules:
  0.0 66.8 jit_solution(16607492744233301691)
XLA Ops:
  0.6 8.8 %collective-permute-start = (f32[8,1,16,512]{3,2,0,1:T(8,128)}, f32[8,1,16,512]{3,2,0,1:T(8,128)S(1)}, u32[]{:S(2)}, u32[]{:S(2)}) collective-permute-start(f32[8,1,16,512]{3,2,0,1:T(8,128)} %bitcast.42), channel_id=1, source_target_pairs={{1,0},{2,1},{3,2},{5,4},{6,5},{7,6},{9,8},{10,9},{11,10},{13,12},{... | collective-permute-start | bytes 786440 | tf_op jit(solution)/shard_map/ppermute | solution.py:57
  10.7 0.0 copy-start.2
  10.7 2.0 %own.1 = (f32[8,16,512]{2,1,0:T(8,128)S(1)}, f32[3,8,16,512]{3,2,1,0:T(8,128)S(1)}, f32[3,16,512]{2,1,0:T(8,128)S(1)}, bf16[64,128,128]{2,1,0:T(8,128)(2,1)S(1)}) custom-call(f32[1]{0:T(128)} %copy.39.rate_ref, f32[8,16,512]{2,1,0:T(8,128)} %bitcast.43, f32[3,8,16,512]{3,2,1,0:T(8,128)} %bitcast.41, bf16[64,128,128]{2,1,0:T(8,128)(2,1)} %projector_far.1), custom_call_target="tpu_custom_call" | custom-call | tf_op jit(solution)/shard_map/own/pallas_call | solution.py:384
  12.8 0.0 collective-permute-done
  12.8 0.9 %gram.1 = (f32[8,16,512]{2,1,0:T(8,128)S(1)}, f32[3,8,16,512]{3,2,1,0:T(8,128)S(1)}, f32[384,128]{1,0:T(8,128)}) custom-call(f32[1]{0:T(128)} %copy.39.rate_ref, f32[1]{0:T(128)} %bitcast.keep_ref, f32[8,16,512]{2,1,0:T(8,128)S(1)} %bitcast.39, f32[3,16,512]{2,1,0:T(8,128)S(1)} %get-tuple-element.19.sums_ref, ...), custom_call_target="tpu_custom_call", output_to_operand_aliasing={{0}: (4, {}), {1}: (5, {})} | custom-call | tf_op jit(solution)/shard_map/gram/pallas_call | solution.py:403
  13.7 0.0 copy-start.1
  13.7 0.0 copy-start.3
  13.7 0.1 convert_element_type.20
  13.8 6.5 %all-to-all-start = ((f32[16,24,128]{2,1,0:T(8,128)}), f32[16,24,128]{2,1,0:T(8,128)S(1)}, u32[]{:S(2)}, u32[]{:S(2)}) async-start(f32[16,24,128]{2,1,0:T(8,128)} %bitcast.44), calls=%async_computation | async-start | bytes 393216 | tf_op jit(solution)/shard_map/all_to_all | solution.py:429
  20.3 0.0 copy-done.2
  20.3 0.2 fusion.9
  20.6 1.2 %fusion.3 = f32[64,8,128]{2,1,0:T(8,128)S(1)} fusion(bf16[64,128,128]{2,1,0:T(8,128)(2,1)S(1)} %get-tuple-element.24, bf16[64,8,128]{2,0,1:T(8,128)(2,1)S(1)} %fusion.9), kind=kOutput, calls=%fused_computation.7 | convolution fusion | flops 16777216 | bytes 2490368 | tf_op jit(solution)/shard_map/tij,tbj->tbi/dot_general | solution.py:440
  21.7 0.0 copy-done.1
  21.7 0.0 copy-done.3
  21.7 1.2 %add_divide_fusion = (f32[8,32,128]{2,1,0:T(8,128)S(1)}, f32[8,32,128]{2,1,0:T(8,128)S(1)}) fusion(f32[8,32,128]{2,1,0:T(8,128)S(1)} %bitcast.45, f32[]{:T(128)S(6)} %add.7, f32[]{:T(128)} %bitcast.36, f32[8,32,128]{2,1,0:T(8,128)} %bitcast.46, s32[64]{0:T(128)S(1)} %copy-done.3, f32[64,8,128]{2,1,0:T(8,128)S(1)} %fusion.3), kind=kOutput, calls=%fused_computation.9 | convolution fusion | flops 25298944 | bytes 786696 | tf_op jit(solution)/shard_map/tc,tbj->bcj/dot_general | solution.py:349
  22.9 0.2 fusion.5
  23.2 0.6 fusion.4
  23.8 0.0 copy-start
  23.8 0.3 convolution_bitcast_fusion
  24.2 0.0 all-to-all-done.parts_ref
  24.2 19.6 %all_to_all.20.parts_ref = f32[8,13,2,128]{3,2,1,0:T(2,128)S(1)} all-to-all(f32[8,13,2,128]{3,2,1,0:T(2,128)S(1)} %get-tuple-element.25), channel_id=1, replica_groups={{40,48,56,0,8,16,24,32},{41,49,57,1,9,17,25,33},{42,50,58,2,10,18,26,34..., dimensions={0} | all-to-all | bytes 212992 | tf_op jit(solution)/shard_map/all_to_all | solution.py:463
  43.8 0.5 factor.1
  44.3 8.6 %all_to_all.21.parts_ref = f32[16,13,2,128]{3,2,1,0:T(2,128)S(1)} all-to-all(f32[16,13,2,128]{3,2,1,0:T(2,128)S(1)} %factor.1), channel_id=1, replica_groups={{324,0,4,64,128,384,68,132,192,256,388,448,196,260,320,452},{325,1,5,65..., dimensions={0} | all-to-all | bytes 425984 | tf_op jit(solution)/shard_map/all_to_all | solution.py:474
  52.9 0.6 slice.1
  53.5 6.0 %collective-permute-start.1 = (f32[8,16,512]{2,1,0:T(8,128)S(1)}, f32[8,16,512]{2,1,0:T(8,128)S(1)}, u32[]{:S(2)}, u32[]{:S(2)}) collective-permute-start(f32[8,16,512]{2,1,0:T(8,128)S(1)} %get-tuple-element.28.slice_ref), channel_id=1, source_target_pairs={{0,1},{1,2},{2,3},{4,5},{5,6},{6,7},{8,9},{9,10},{10,11},{12,13},{... | collective-permute-start | bytes 786440 | tf_op jit(solution)/shard_map/ppermute | solution.py:57
  59.5 3.2 %all-to-all-start.3 = ((f32[4,2,128]{2,1,0:T(2,128)}), f32[4,2,128]{2,1,0:T(2,128)S(1)}, u32[]{:S(2)}, u32[]{:S(2)}) async-start(f32[4,2,128]{2,1,0:T(2,128)} %get-tuple-element.33), calls=%async_computation.3 | async-start | bytes 8192 | tf_op jit(solution)/shard_map/all_to_all | solution.py:496
  63.4 0.0 copy-done
  63.4 1.1 %rest.1 = (f32[3,8,16,512]{3,2,1,0:T(8,128)}, f32[8,16,512]{2,1,0:T(8,128)S(1)}, f32[8,32,128]{2,1,0:T(8,128)}) custom-call(f32[1]{0:T(128)S(6)} %copy.40.rate_ref, f32[1]{0:T(128)} %bitcast.keep_ref, f32[384,128]{1,0:T(8,128)S(1)} %get-tuple-element.27.factor_ref, f32[3,8,16,512]{3,2,1,0:T(8,128)S(1)} %get-tuple-element.26.cand_ref, ...), custom_call_target="tpu_custom_call" | custom-call | tf_op jit(solution)/shard_map/rest/pallas_call | solution.py:497
  64.5 0.0 collective-permute-done.1.prior_ref
  64.5 0.7 %finish.1.updated_far = f32[8,16,512]{2,1,0:T(8,128)} custom-call(f32[1]{0:T(128)S(6)} %copy.40.rate_ref, f32[8,16,512]{2,1,0:T(8,128)S(1)} %get-tuple-element.30.ready_ref, f32[8,16,512]{2,1,0:T(8,128)S(1)} %collective-permute-done.1.prior_ref), custom_call_target="tpu_custom_call" | custom-call | tf_op jit(solution)/shard_map/finish/pallas_call | solution.py:519
  65.3 0.9 %all-to-all-done.3.sums_ref = f32[4,2,128]{2,1,0:T(2,128)S(1)} async-done(((f32[4,2,128]{2,1,0:T(2,128)}), f32[4,2,128]{2,1,0:T(2,128)S(1)}, u32[]{:S(2)}, u32[]{:S(2)}) %all-to-all-start.3) | async-done | bytes 4128 | tf_op jit(solution)/shard_map/all_to_all | solution.py:496
  66.2 0.6 totals.1
  (3 shorter events, 0.1 us)
Async XLA Ops:
  0.6 12.2 %collective-permute-start = (f32[8,1,16,512]{3,2,0,1:T(8,128)}, f32[8,1,16,512]{3,2,0,1:T(8,128)S(1)}, u32[]{:S(2)}, u32[]{:S(2)}) collective-permute-start(f32[8,1,16,512]{3,2,0,1:T(8,128)} %bitcast.42), channel_id=1, source_target_pairs={{1,0},{2,1},{3,2},{5,4},{6,5},{7,6},{9,8},{10,9},{11,10},{13,12},{... | collective-permute-start | bytes 786440 | tf_op jit(solution)/shard_map/ppermute | solution.py:57
  10.7 9.6 %copy-start.2 = (s32[64]{0:T(128)S(1)}, s32[64]{0:T(128)}, u32[]{:S(2)}) copy-start(s32[64]{0:T(128)} %param.18) | copy-start | bytes 772
  13.7 8.1 %copy-start.1 = (f32[8,1,4096]{2,1,0:T(1,128)S(1)}, f32[8,1,4096]{2,1,0:T(1,128)}, u32[]{:S(2)}) copy-start(f32[8,1,4096]{2,1,0:T(1,128)} %param.14) | copy-start | bytes 393220
  13.7 8.1 %copy-start.3 = (s32[64]{0:T(128)S(1)}, s32[64]{0:T(128)}, u32[]{:S(2)}) copy-start(s32[64]{0:T(128)} %param.17) | copy-start | bytes 772
  13.8 10.4 %all-to-all-start = ((f32[16,24,128]{2,1,0:T(8,128)}), f32[16,24,128]{2,1,0:T(8,128)S(1)}, u32[]{:S(2)}, u32[]{:S(2)}) async-start(f32[16,24,128]{2,1,0:T(8,128)} %bitcast.44), calls=%async_computation | async-start | bytes 393216 | tf_op jit(solution)/shard_map/all_to_all | solution.py:429
  23.8 39.6 %copy-start = (f32[8,1,16,512]{3,2,1,0:T(8,128)S(1)}, f32[8,1,16,512]{3,2,1,0:T(8,128)}, u32[]{:S(2)}) copy-start(f32[8,1,16,512]{3,2,1,0:T(8,128)} %param.11) | copy-start | bytes 786436
  53.5 11.0 %collective-permute-start.1 = (f32[8,16,512]{2,1,0:T(8,128)S(1)}, f32[8,16,512]{2,1,0:T(8,128)S(1)}, u32[]{:S(2)}, u32[]{:S(2)}) collective-permute-start(f32[8,16,512]{2,1,0:T(8,128)S(1)} %get-tuple-element.28.slice_ref), channel_id=1, source_target_pairs={{0,1},{1,2},{2,3},{4,5},{5,6},{6,7},{8,9},{9,10},{10,11},{12,13},{... | collective-permute-start | bytes 786440 | tf_op jit(solution)/shard_map/ppermute | solution.py:57
  59.5 6.7 %all-to-all-start.3 = ((f32[4,2,128]{2,1,0:T(2,128)}), f32[4,2,128]{2,1,0:T(2,128)S(1)}, u32[]{:S(2)}, u32[]{:S(2)}) async-start(f32[4,2,128]{2,1,0:T(2,128)} %get-tuple-element.33), calls=%async_computation.3 | async-start | bytes 8192 | tf_op jit(solution)/shard_map/all_to_all | solution.py:496
